TPU v7x, 32 devices: a whole 2x2x4 slice. The times are simulated.
32 devices in a mesh: energy: 8 (over y, x, core), slab: 4 (over z).
Axes of the slice: x: 2, y: 2, z: 4, core: 2. Of those that a mesh axis runs over, the one named last changes fastest.
Arguments:
- green: bfloat16 [8, 4, 2, 384, 384], P('energy', 'slab'), may hold values from -6 to 6
- weights: int32 [8, 2, 2], P('energy'), may hold values from 1 to 63
- coupling_m: bfloat16 [2, 384, 384], replicated, may hold values from -0.3125 to 0.3125
- coupling_n: bfloat16 [2, 384, 384], replicated, may hold values from -0.3125 to 0.3125
Outputs:
- sigma: bfloat16 [8, 4, 2, 384, 384], P('energy', 'slab')
All inputs are finite; a program needn't handle non-finite values.
Results may differ from a plain program's by a relative error of at most 0.0061.
Values may be sent and summed in bfloat16 or wider, within the bound.
No kernel may reach another device: no remote copies, remote signals or barrier semaphores. Data moves between devices by JAX's collectives and lax.ppermute only.
A program may use at most 64 MiB of HBM per device.

v0:
```python
import jax
import jax.numpy as jnp
from jax import lax
from jax.sharding import PartitionSpec as P

K1 = 3
K2 = 7


def from_behind(block, axis, distance):
    devices = range(lax.axis_size(axis))
    route = [(i - distance, i) for i in devices if i - distance in devices]
    return lax.ppermute(block, axis, route)


def combine(upper, lower, wrow):
    mixed = wrow[0] * upper.astype(jnp.float32) + wrow[1] * lower.astype(jnp.float32)
    return mixed.astype(jnp.bfloat16)


def coupled(mat, combo):
    left = jnp.einsum("ij,pjk->pik", mat, combo, preferred_element_type=jnp.float32).astype(
        jnp.bfloat16
    )
    return jnp.einsum("pik,lk->pil", left, mat, preferred_element_type=jnp.float32)


def body(green, weights, coupling_m, coupling_n):
    scaled = weights[0].astype(jnp.float32) / 32.0
    near_upper = from_behind(green, "energy", -K1)
    near_lower = from_behind(green, "energy", K1)
    far_upper = from_behind(green, "energy", -K2)
    far_lower = from_behind(green, "energy", K2)
    combos = (
        combine(near_upper[0, 0], near_lower[0, 0], scaled[0]),
        combine(far_upper[0, 0], far_lower[0, 0], scaled[1]),
    )
    own = coupled(coupling_m[0], combos[0]) + coupled(coupling_m[1], combos[1])
    term = coupled(coupling_n[0], combos[0]) + coupled(coupling_n[1], combos[1])
    term = term.astype(jnp.bfloat16)[None, None]
    arrived = from_behind(term, "slab", -1)
    total = own[None, None] + arrived.astype(jnp.float32)
    return total.astype(jnp.bfloat16)


def solution(mesh):
    placed = (P("energy", "slab", None, None, None), P("energy", None, None), P(), P())
    return jax.shard_map(
        body,
        mesh=mesh,
        in_specs=placed,
        out_specs=P("energy", "slab", None, None, None),
        check_vma=False,
    )
```

profile of v0, /device:TPU:20, one launch (start us, length us, event | category | flops | bytes accessed | tf_op | source)
XLA Modules:
  0.0 47.7 jit_solution(17502918061989467498)
XLA Ops:
  0.0 1.9 %collective-permute-start = (bf16[1,1,2,384,384]{4,3,2,1,0:T(8,128)(2,1)}, bf16[1,1,2,384,384]{4,3,2,1,0:T(8,128)(2,1)S(1)}, u32[]{:S(2)}, u32[]{:S(2)}) collective-permute-start(bf16[1,1,2,384,384]{4,3,2,1,0:T(8,128)(2,1)} %param.4), channel_id=1, source_target_pairs={{12,0},{16,4},{20,8},{24,12},{28,16},{13,1},{17,5},{21,9},{25,13},... | collective-permute-start | bytes 1769480 | tf_op jit(solution)/shard_map/ppermute | solution.py:13
  1.9 3.7 %collective-permute-start.1 = (bf16[1,1,2,384,384]{4,3,2,1,0:T(8,128)(2,1)}, bf16[1,1,2,384,384]{4,3,2,1,0:T(8,128)(2,1)S(1)}, u32[]{:S(2)}, u32[]{:S(2)}) collective-permute-start(bf16[1,1,2,384,384]{4,3,2,1,0:T(8,128)(2,1)} %param.4), channel_id=1, source_target_pairs={{0,12},{4,16},{8,20},{12,24},{16,28},{1,13},{5,17},{9,21},{13,25},... | collective-permute-start | bytes 1769480 | tf_op jit(solution)/shard_map/ppermute | solution.py:13
  5.6 0.7 %collective-permute-start.2 = (bf16[1,1,2,384,384]{4,3,2,1,0:T(8,128)(2,1)}, bf16[1,1,2,384,384]{4,3,2,1,0:T(8,128)(2,1)S(1)}, u32[]{:S(2)}, u32[]{:S(2)}) collective-permute-start(bf16[1,1,2,384,384]{4,3,2,1,0:T(8,128)(2,1)} %param.4), channel_id=1, source_target_pairs={{28,0},{29,1},{30,2},{31,3}} | collective-permute-start | bytes 1769480 | tf_op jit(solution)/shard_map/ppermute | solution.py:13
  6.3 0.7 %collective-permute-start.3 = (bf16[1,1,2,384,384]{4,3,2,1,0:T(8,128)(2,1)}, bf16[1,1,2,384,384]{4,3,2,1,0:T(8,128)(2,1)S(1)}, u32[]{:S(2)}, u32[]{:S(2)}) collective-permute-start(bf16[1,1,2,384,384]{4,3,2,1,0:T(8,128)(2,1)} %param.4), channel_id=1, source_target_pairs={{0,28},{1,29},{2,30},{3,31}} | collective-permute-start | bytes 1769480 | tf_op jit(solution)/shard_map/ppermute | solution.py:13
  7.0 0.7 %multiply_bitcast_fusion = f32[2,2]{1,0:T(2,128)S(1)} fusion(s32[1,2,2]{2,1,0:T(2,128)} %param.5), kind=kLoop, calls=%fused_computation.28 | loop fusion | flops 8 | bytes 32 | tf_op jit(solution)/shard_map/div | solution.py:29
  7.7 0.7 %fusion.35 = (f32[1,1]{1,0:T(1,128)}, f32[1,1]{1,0:T(1,128)}, f32[1,1]{1,0:T(1,128)}, f32[1,1]{1,0:T(1,128)}) fusion(f32[2,2]{1,0:T(2,128)S(1)} %multiply_bitcast_fusion), kind=kLoop, calls=%fused_computation.29 | loop fusion | bytes 32 | tf_op jit(solution)/shard_map/slice | solution.py:17
  8.4 3.0 %collective-permute-done = bf16[1,1,2,384,384]{4,3,2,1,0:T(8,128)(2,1)S(1)} collective-permute-done((bf16[1,1,2,384,384]{4,3,2,1,0:T(8,128)(2,1)}, bf16[1,1,2,384,384]{4,3,2,1,0:T(8,128)(2,1)S(1)}, u32[]{:S(2)}, u32[]{:S(2)}) %collective-permute-start) | collective-permute-done | bytes 589856 | tf_op jit(solution)/shard_map/ppermute | solution.py:13
  11.4 8.2 %collective-permute-done.1 = bf16[1,1,2,384,384]{4,3,2,1,0:T(8,128)(2,1)S(1)} collective-permute-done((bf16[1,1,2,384,384]{4,3,2,1,0:T(8,128)(2,1)}, bf16[1,1,2,384,384]{4,3,2,1,0:T(8,128)(2,1)S(1)}, u32[]{:S(2)}, u32[]{:S(2)}) %collective-permute-start.1) | collective-permute-done | bytes 589856 | tf_op jit(solution)/shard_map/ppermute | solution.py:13
  19.6 0.0 copy-start
  19.7 4.3 %fusion.7 = f32[2,384,384]{2,1,0:T(8,128)} fusion(bf16[2,384,384]{2,1,0:T(8,128)(2,1)} %param.7, bf16[1,1,2,384,384]{4,3,2,1,0:T(8,128)(2,1)S(1)} %collective-permute-done.1, bf16[1,1,2,384,384]{4,3,2,1,0:T(8,128)(2,1)S(1)} %collective-permute-done, f32[]{:T(128)} %bitcast.2, f32[]{:T(128)} %bitcast.1), kind=kOutput, calls=%fused_computation.13 | convolution fusion | flops 455049216 | bytes 2949128 | tf_op jit(solution)/shard_map/pik,lk->pil/dot_general | solution.py:25
  23.9 0.0 collective-permute-done.2
  23.9 0.0 collective-permute-done.3
  23.9 0.0 copy-done
  23.9 0.0 copy-start.1
  23.9 4.3 %fusion.2 = bf16[1,1,2,384,384]{4,3,2,1,0:T(8,128)(2,1)} fusion(f32[2,384,384]{2,1,0:T(8,128)} %fusion.7, bf16[2,384,384]{2,1,0:T(8,128)(2,1)S(1)} %copy-done, bf16[1,1,2,384,384]{4,3,2,1,0:T(8,128)(2,1)S(1)} %collective-permute-done.3, bf16[1,1,2,384,384]{4,3,2,1,0:T(8,128)(2,1)S(1)} %collective-permute-done.2, f32[]{:T(128)} %bitcast.8, f32[]{:T(128)} %bitcast.7), kind=kOutput, calls=%fused_computation.8 | convolution fusion | flops 455639040 | bytes 3538952 | tf_op jit(solution)/shard_map/pik,lk->pil/dot_general | solution.py:25
  28.2 2.3 %collective-permute-start.4 = (bf16[1,1,2,384,384]{4,3,2,1,0:T(8,128)(2,1)}, bf16[1,1,2,384,384]{4,3,2,1,0:T(8,128)(2,1)S(1)}, u32[]{:S(2)}, u32[]{:S(2)}) collective-permute-start(bf16[1,1,2,384,384]{4,3,2,1,0:T(8,128)(2,1)} %fusion.2), channel_id=1, source_target_pairs={{1,0},{2,1},{3,2},{5,4},{6,5},{7,6},{9,8},{10,9},{11,10},{13,12},{... | collective-permute-start | bytes 1769480 | tf_op jit(solution)/shard_map/ppermute | solution.py:13
  30.6 0.0 copy-done.1
  30.6 3.1 %fusion.4 = f32[2,384,384]{2,1,0:T(8,128)} fusion(bf16[2,384,384]{2,1,0:T(8,128)(2,1)S(1)} %copy-done.1, bf16[1,1,2,384,384]{4,3,2,1,0:T(8,128)(2,1)S(1)} %collective-permute-done.1, bf16[1,1,2,384,384]{4,3,2,1,0:T(8,128)(2,1)S(1)} %collective-permute-done, f32[]{:T(128)} %bitcast.2, f32[]{:T(128)} %bitcast.1), kind=kOutput, calls=%fused_computation.10 | convolution fusion | flops 455049216 | bytes 2949128 | tf_op jit(solution)/shard_map/pik,lk->pil/dot_general | solution.py:25
  33.7 9.8 %collective-permute-done.4 = bf16[1,1,2,384,384]{4,3,2,1,0:T(8,128)(2,1)S(1)} collective-permute-done((bf16[1,1,2,384,384]{4,3,2,1,0:T(8,128)(2,1)}, bf16[1,1,2,384,384]{4,3,2,1,0:T(8,128)(2,1)S(1)}, u32[]{:S(2)}, u32[]{:S(2)}) %collective-permute-start.4) | collective-permute-done | bytes 589856 | tf_op jit(solution)/shard_map/ppermute | solution.py:13
  43.5 4.2 %add_convert_fusion = bf16[1,1,2,384,384]{4,3,2,1,0:T(8,128)(2,1)} fusion(bf16[1,1,2,384,384]{4,3,2,1,0:T(8,128)(2,1)S(1)} %collective-permute-done.4, f32[2,384,384]{2,1,0:T(8,128)} %fusion.4, bf16[2,384,384]{2,1,0:T(8,128)(2,1)S(1)} %copy-done.1, bf16[1,1,2,384,384]{4,3,2,1,0:T(8,128)(2,1)S(1)} %collective-permute-done.3, ...), kind=kOutput, calls=%fused_computation.15 | convolution fusion | flops 456228864 | bytes 4128776 | tf_op jit(solution)/shard_map/pik,lk->pil/dot_general | solution.py:25
Async XLA Ops:
  0.0 11.4 %collective-permute-start = (bf16[1,1,2,384,384]{4,3,2,1,0:T(8,128)(2,1)}, bf16[1,1,2,384,384]{4,3,2,1,0:T(8,128)(2,1)S(1)}, u32[]{:S(2)}, u32[]{:S(2)}) collective-permute-start(bf16[1,1,2,384,384]{4,3,2,1,0:T(8,128)(2,1)} %param.4), channel_id=1, source_target_pairs={{12,0},{16,4},{20,8},{24,12},{28,16},{13,1},{17,5},{21,9},{25,13},... | collective-permute-start | bytes 1769480 | tf_op jit(solution)/shard_map/ppermute | solution.py:13
  1.9 17.7 %collective-permute-start.1 = (bf16[1,1,2,384,384]{4,3,2,1,0:T(8,128)(2,1)}, bf16[1,1,2,384,384]{4,3,2,1,0:T(8,128)(2,1)S(1)}, u32[]{:S(2)}, u32[]{:S(2)}) collective-permute-start(bf16[1,1,2,384,384]{4,3,2,1,0:T(8,128)(2,1)} %param.4), channel_id=1, source_target_pairs={{0,12},{4,16},{8,20},{12,24},{16,28},{1,13},{5,17},{9,21},{13,25},... | collective-permute-start | bytes 1769480 | tf_op jit(solution)/shard_map/ppermute | solution.py:13
  5.6 18.3 %collective-permute-start.2 = (bf16[1,1,2,384,384]{4,3,2,1,0:T(8,128)(2,1)}, bf16[1,1,2,384,384]{4,3,2,1,0:T(8,128)(2,1)S(1)}, u32[]{:S(2)}, u32[]{:S(2)}) collective-permute-start(bf16[1,1,2,384,384]{4,3,2,1,0:T(8,128)(2,1)} %param.4), channel_id=1, source_target_pairs={{28,0},{29,1},{30,2},{31,3}} | collective-permute-start | bytes 1769480 | tf_op jit(solution)/shard_map/ppermute | solution.py:13
  6.3 17.6 %collective-permute-start.3 = (bf16[1,1,2,384,384]{4,3,2,1,0:T(8,128)(2,1)}, bf16[1,1,2,384,384]{4,3,2,1,0:T(8,128)(2,1)S(1)}, u32[]{:S(2)}, u32[]{:S(2)}) collective-permute-start(bf16[1,1,2,384,384]{4,3,2,1,0:T(8,128)(2,1)} %param.4), channel_id=1, source_target_pairs={{0,28},{1,29},{2,30},{3,31}} | collective-permute-start | bytes 1769480 | tf_op jit(solution)/shard_map/ppermute | solution.py:13
  19.6 4.3 %copy-start = (bf16[2,384,384]{2,1,0:T(8,128)(2,1)S(1)}, bf16[2,384,384]{2,1,0:T(8,128)(2,1)}, u32[]{:S(2)}) copy-start(bf16[2,384,384]{2,1,0:T(8,128)(2,1)} %param.7) | copy-start | bytes 1769476
  23.9 6.6 %copy-start.1 = (bf16[2,384,384]{2,1,0:T(8,128)(2,1)S(1)}, bf16[2,384,384]{2,1,0:T(8,128)(2,1)}, u32[]{:S(2)}) copy-start(bf16[2,384,384]{2,1,0:T(8,128)(2,1)} %param.6) | copy-start | bytes 1769476
  28.2 15.3 %collective-permute-start.4 = (bf16[1,1,2,384,384]{4,3,2,1,0:T(8,128)(2,1)}, bf16[1,1,2,384,384]{4,3,2,1,0:T(8,128)(2,1)S(1)}, u32[]{:S(2)}, u32[]{:S(2)}) collective-permute-start(bf16[1,1,2,384,384]{4,3,2,1,0:T(8,128)(2,1)} %fusion.2), channel_id=1, source_target_pairs={{1,0},{2,1},{3,2},{5,4},{6,5},{7,6},{9,8},{10,9},{11,10},{13,12},{... | collective-permute-start | bytes 1769480 | tf_op jit(solution)/shard_map/ppermute | solution.py:13
where the time goes:
time: 48.1 us; the launch traced here: 47.7 us
  waiting for transfers between devices  21.1 us (44%)
  matrix products  15.9 us (33%)
  starting transfers between devices  9.32 us (19%)
  other arithmetic  0.68 us (1%)
  local copies, waits for them, and re-layouts  0.67 us (1%)
    ppermute x5, waiting for transfers between devices, from_behind(): return lax.ppermute(block, axis, route)  21.1 us
    dot_general x4, matrix products, coupled(): jnp.einsum('pik,lk->pil', left, mat, preferred_element_type=jnp.float32)  15.9 us
    ppermute x5, starting transfers between devices, from_behind(): return lax.ppermute(block, axis, route)  9.32 us
  transfers between devices with their start and end apart: 5, of which 3 were waited for; matrix products, arithmetic and copies ran while one was open for 18% of the time, Pallas kernels for 0%

commit v1 on v0

v1 whole, which is shorter than its diff:
```python
import functools

import jax
import jax.numpy as jnp
from jax import lax
from jax.experimental import pallas as pl
from jax.experimental.pallas import tpu as pltpu
from jax.sharding import PartitionSpec as P

SHIFTS = (3, 7)
F32, BF16 = jnp.float32, jnp.bfloat16
NT = (((1,), (1,)), ((), ()))


def matchings(count):
    left = {}
    for target in range(count):
        for mode, shift in enumerate(SHIFTS):
            for side, source in enumerate((target + shift, target - shift)):
                if 0 <= source < count:
                    left[source, target] = (mode, side)
    rounds = []
    while left:
        options = {}
        for source, target in sorted(left):
            options.setdefault(source, []).append(target)
        taken = {}

        def place(source, seen):
            for target in options[source]:
                if target not in seen:
                    seen.add(target)
                    if target not in taken or place(taken[target], seen):
                        taken[target] = source
                        return True
            return False

        for source in sorted(options):
            place(source, set())
        rounds.append({t: (s,) + left.pop((s, t)) for t, s in sorted(taken.items())})
    return rounds


def lookup(table, index):
    value = jnp.int32(table[0])
    for start in range(len(table)):
        if start and table[start] != table[start - 1]:
            value = jnp.where(index >= start, jnp.int32(table[start]), value)
    return value


def factors(plan, count, weights_ref):
    me = lax.axis_index("energy")
    rows = []
    for mode in range(len(SHIFTS)):
        row = []
        for step in plan:
            codes = [0] * count
            for target, (_, which, side) in step.items():
                if which == mode:
                    codes[target] = side + 1
            code = lookup(codes, me)
            picked = jnp.where(code == 2, weights_ref[0, mode, 1], weights_ref[0, mode, 0])
            row.append(jnp.where(code > 0, picked, 0).astype(F32) / 32.0)
        rows.append(row)
    return rows


def sent_modes(plan, count):
    me = lax.axis_index("energy")
    out = []
    for step in plan:
        modes = [0] * count
        for source, mode, _ in step.values():
            modes[source] = mode
        out.append(lookup(modes, me))
    return out


def dot(a, b):
    return jnp.dot(a, b, preferred_element_type=F32)


def dot_t(a, b):
    return lax.dot_general(a, b, NT, preferred_element_type=F32)


VM = pl.BlockSpec(memory_space=pltpu.VMEM)
SM = pl.BlockSpec(memory_space=pltpu.SMEM)
ANY = pl.BlockSpec(memory_space=pl.ANY)


def call(body, ins, outs, flops, *args):
    return pl.pallas_call(
        body,
        out_shape=outs,
        in_specs=ins,
        out_specs=[VM] * len(outs),
        cost_estimate=pl.CostEstimate(flops=flops, bytes_accessed=1 << 20, transcendentals=0),
        compiler_params=pltpu.CompilerParams(vmem_limit_bytes=24 << 20),
    )(*args)


def body(count, slabs, plan, green, weights, coupling_m, coupling_n):
    size = green.shape[-1]
    block = pltpu.VMEM((size, size), BF16)
    wide = pltpu.VMEM((size, size), F32)
    rounds = len(plan)
    product = 2 * size**3

    def split(green_ref, real_ref, imag_ref, sems):
        copies = [
            pltpu.make_async_copy(green_ref.at[0, 0, part], out, sems.at[part])
            for part, out in enumerate((real_ref, imag_ref))
        ]
        for copy in copies:
            copy.start()
        for copy in copies:
            copy.wait()

    real, imag = pl.pallas_call(
        split,
        out_shape=[block, block],
        in_specs=[ANY],
        out_specs=[VM, VM],
        scratch_shapes=[pltpu.SemaphoreType.DMA((2,))],
    )(green)

    def along(x, step):
        return lax.ppermute(x, "energy", [(s, t) for t, (s, _, _) in step.items()])

    def from_next(x):
        return lax.ppermute(x, "slab", [(s, (s - 1) % slabs) for s in range(slabs)])

    near = [along(imag, step) for step in plan]
    behind = from_next(real)

    def first(real_ref, cm_ref, *outs):
        for mode, out in zip(sent_modes(plan, count), outs):
            mat = cm_ref[mode]
            out[...] = dot_t(dot(mat, real_ref[...]).astype(BF16), mat)

    partial = call(first, [VM, VM], [wide] * rounds, 2 * rounds * product, real, coupling_m)

    def terms(weights_ref, cm_ref, cn_ref, *refs):
        got, (term_ref, left_ref) = refs[:rounds], refs[rounds:]
        total = None
        for mode, row in enumerate(factors(plan, count, weights_ref)):
            combo = sum(f * ref[...].astype(F32) for f, ref in zip(row, got)).astype(BF16)
            left_ref[mode] = dot(cm_ref[mode], combo).astype(BF16)
            piece = dot_t(dot(cn_ref[mode], combo).astype(BF16), cn_ref[mode])
            total = piece if total is None else total + piece
        term_ref[...] = total.astype(BF16)

    modes = len(SHIFTS)
    term, left = call(
        terms,
        [SM, VM, VM] + [VM] * rounds,
        [block, pltpu.VMEM((modes, size, size), BF16)],
        3 * modes * product,
        weights,
        coupling_m,
        coupling_n,
        *near,
    )
    term_next = from_next(term)

    def second(behind_ref, cn_ref, *refs):
        here = jnp.where(lax.axis_index("slab") < slabs - 1, 1.0, 0.0).astype(F32)
        for mode, part, out in zip(sent_modes(plan, count), refs[:rounds], refs[rounds:]):
            mat = cn_ref[mode]
            piece = dot_t(dot(mat, behind_ref[...]).astype(BF16), mat)
            out[...] = (part[...] + here * piece).astype(BF16)

    whole = call(
        second, [VM, VM] + [VM] * rounds, [block] * rounds, 2 * rounds * product, behind, coupling_n, *partial
    )
    arrived = [along(x, step) for x, step in zip(whole, plan)]

    def own_sum(left_ref, cm_ref, out):
        out[...] = sum(dot_t(left_ref[m], cm_ref[m]) for m in range(modes))

    (own,) = call(own_sum, [VM, VM], [wide], modes * product, left, coupling_m)

    def finish(weights_ref, own_ref, term_ref, *refs):
        got, out = refs[:rounds], refs[rounds]
        rows = factors(plan, count, weights_ref)
        scale = [sum(row[r] for row in rows) for r in range(rounds)]
        out[0, 0, 0] = sum(f * ref[...].astype(F32) for f, ref in zip(scale, got)).astype(BF16)
        here = jnp.where(lax.axis_index("slab") < slabs - 1, 1.0, 0.0).astype(F32)
        out[0, 0, 1] = (own_ref[...] + here * term_ref[...].astype(F32)).astype(BF16)

    return pl.pallas_call(
        finish,
        out_shape=jax.ShapeDtypeStruct(green.shape, BF16),
        in_specs=[SM] + [VM] * (2 + rounds),
        out_specs=VM,
        compiler_params=pltpu.CompilerParams(vmem_limit_bytes=24 << 20),
    )(weights, own, term_next, *arrived)


def solution(mesh):
    count, slabs = mesh.shape["energy"], mesh.shape["slab"]
    placed = (P("energy", "slab", None, None, None), P("energy", None, None), P(), P())
    return jax.shard_map(
        functools.partial(body, count, slabs, matchings(count)),
        mesh=mesh,
        in_specs=placed,
        out_specs=P("energy", "slab", None, None, None),
        check_vma=False,
    )
```

time: 48.1 us -> 30.5 us (0.63)
  the two profiles are of different devices: /device:TPU:20 before, /device:TPU:0 now
where the time goes in v1:
time: 30.5 us; the launch traced here: 30.3 us
  starting transfers between devices  18.7 us (61%)
  Pallas kernels  7.15 us (23%)
  waiting for transfers between devices  4.31 us (14%)
    ppermute x2, starting transfers between devices, from_next(): return lax.ppermute(x, 'slab', [(s, (s - 1) % slabs) for s in range(slabs)])  9.44 us
    ppermute x4, starting transfers between devices, along(): return lax.ppermute(x, 'energy', [(s, t) for t, (s, _, _) in step.items()])  9.31 us
    pallas_call x4, Pallas kernels, call(): pl.pallas_call(body, out_shape=outs, in_specs=ins, out_specs=[VM] * len(o...  4.46 us
    ppermute x2, waiting for transfers between devices, from_next(): return lax.ppermute(x, 'slab', [(s, (s - 1) % slabs) for s in range(slabs)])  4.3 us
    pallas_call x1, Pallas kernels, body(): pl.pallas_call(finish, out_shape=jax.ShapeDtypeStruct(green.shape, BF16),...  1.56 us
    pallas_call x1, Pallas kernels, body(): pl.pallas_call(split, out_shape=[block, block], in_specs=[ANY], out_specs...  1.13 us
  transfers between devices with their start and end apart: 6, of which 2 were waited for; matrix products, arithmetic and copies ran while one was open for 0% of the time, Pallas kernels for 15%

profile of v1, /device:TPU:0, one launch (start us, length us, event | category | flops | bytes accessed | tf_op | source)
XLA Modules:
  0.0 30.3 jit_solution(3217065486244314493)
XLA Ops:
  0.0 0.0 copy-start
  0.0 1.1 %shard_map.46 = (bf16[384,384]{1,0:T(8,128)(2,1)S(1)}, bf16[384,384]{1,0:T(8,128)(2,1)S(1)}) custom-call(bf16[1,1,2,384,384]{4,3,2,1,0:T(8,128)(2,1)} %green_ref.1), custom_call_target="tpu_custom_call" | custom-call | tf_op jit(solution)/shard_map/pallas_call | solution.py:121
  1.1 5.1 %collective-permute-start.3 = (bf16[384,384]{1,0:T(8,128)(2,1)S(1)}, bf16[384,384]{1,0:T(8,128)(2,1)S(1)}, u32[]{:S(2)}, u32[]{:S(2)}) collective-permute-start(bf16[384,384]{1,0:T(8,128)(2,1)S(1)} %get-tuple-element.16.real_ref), channel_id=1, source_target_pairs={{0,3},{1,0},{2,1},{3,2},{4,7},{5,4},{6,5},{7,6},{8,11},{9,8},{10,9... | collective-permute-start | bytes 884744 | tf_op jit(solution)/shard_map/ppermute | solution.py:133
  6.2 0.0 copy-start.1
  6.2 1.6 %collective-permute-start = (bf16[384,384]{1,0:T(8,128)(2,1)S(1)}, bf16[384,384]{1,0:T(8,128)(2,1)S(1)}, u32[]{:S(2)}, u32[]{:S(2)}) collective-permute-start(bf16[384,384]{1,0:T(8,128)(2,1)S(1)} %get-tuple-element.13), channel_id=1, source_target_pairs={{28,0},{16,4},{20,8},{24,12},{4,16},{8,20},{12,24},{0,28},{29,1},{... | collective-permute-start | bytes 884744 | tf_op jit(solution)/shard_map/ppermute | solution.py:130
  7.9 3.0 %collective-permute-start.1 = (bf16[384,384]{1,0:T(8,128)(2,1)S(1)}, bf16[384,384]{1,0:T(8,128)(2,1)S(1)}, u32[]{:S(2)}, u32[]{:S(2)}) collective-permute-start(bf16[384,384]{1,0:T(8,128)(2,1)S(1)} %get-tuple-element.13), channel_id=1, source_target_pairs={{12,0},{0,12},{28,16},{16,28},{13,1},{1,13},{29,17},{17,29},{14,2}... | collective-permute-start | bytes 884744 | tf_op jit(solution)/shard_map/ppermute | solution.py:130
  10.9 0.0 copy-done
  10.9 1.0 %shard_map.49 = (f32[384,384]{1,0:T(8,128)S(1)}, f32[384,384]{1,0:T(8,128)S(1)}) custom-call(bf16[384,384]{1,0:T(8,128)(2,1)S(1)} %get-tuple-element.16.real_ref, bf16[2,384,384]{2,1,0:T(8,128)(2,1)S(1)} %copy-done), custom_call_target="tpu_custom_call" | custom-call | flops 452984832 | bytes 1048576 | tf_op jit(solution)/shard_map/pallas_call | solution.py:94
  11.9 0.6 %collective-permute-done.3.behind_ref = bf16[384,384]{1,0:T(8,128)(2,1)S(1)} collective-permute-done((bf16[384,384]{1,0:T(8,128)(2,1)S(1)}, bf16[384,384]{1,0:T(8,128)(2,1)S(1)}, u32[]{:S(2)}, u32[]{:S(2)}) %collective-permute-start.3) | collective-permute-done | bytes 294944 | tf_op jit(solution)/shard_map/ppermute | solution.py:133
  12.5 0.0 copy-done.1
  12.5 1.0 %shard_map.50 = (bf16[384,384]{1,0:T(8,128)(2,1)S(1)}, bf16[384,384]{1,0:T(8,128)(2,1)S(1)}) custom-call(bf16[384,384]{1,0:T(8,128)(2,1)S(1)} %collective-permute-done.3.behind_ref, bf16[2,384,384]{2,1,0:T(8,128)(2,1)S(1)} %copy-done.1, f32[384,384]{1,0:T(8,128)S(1)} %get-tuple-element.17.refs_0_, f32[384,384]{1,0:T(8,128)S(1)} %get-tuple-element.18.refs_1_), custom_call_target="tpu_custom_call" | custom-call | flops 452984832 | bytes 1048576 | tf_op jit(solution)/shard_map/pallas_call | solution.py:94
  13.5 0.0 copy-start.2
  13.5 1.1 %collective-permute-start.4 = (bf16[384,384]{1,0:T(8,128)(2,1)S(1)}, bf16[384,384]{1,0:T(8,128)(2,1)S(1)}, u32[]{:S(2)}, u32[]{:S(2)}) collective-permute-start(bf16[384,384]{1,0:T(8,128)(2,1)S(1)} %get-tuple-element.19), channel_id=1, source_target_pairs={{28,0},{16,4},{20,8},{24,12},{4,16},{8,20},{12,24},{0,28},{29,1},{... | collective-permute-start | bytes 884744 | tf_op jit(solution)/shard_map/ppermute | solution.py:130
  14.6 3.6 %collective-permute-start.5 = (bf16[384,384]{1,0:T(8,128)(2,1)S(1)}, bf16[384,384]{1,0:T(8,128)(2,1)S(1)}, u32[]{:S(2)}, u32[]{:S(2)}) collective-permute-start(bf16[384,384]{1,0:T(8,128)(2,1)S(1)} %get-tuple-element.20), channel_id=1, source_target_pairs={{12,0},{0,12},{28,16},{16,28},{13,1},{1,13},{29,17},{17,29},{14,2}... | collective-permute-start | bytes 884744 | tf_op jit(solution)/shard_map/ppermute | solution.py:130
  18.2 0.0 collective-permute-done.refs_0_
  18.2 0.0 collective-permute-done.1.refs_1_
  18.3 0.0 copy-done.2
  18.3 1.9 %shard_map.47 = (bf16[384,384]{1,0:T(8,128)(2,1)S(1)}, bf16[2,384,384]{2,1,0:T(8,128)(2,1)S(1)}) custom-call(s32[1,2,2]{2,1,0:T(2,128)S(1)} %copy-done.2, bf16[2,384,384]{2,1,0:T(8,128)(2,1)S(1)} %copy-done, bf16[2,384,384]{2,1,0:T(8,128)(2,1)S(1)} %copy-done.1, bf16[384,384]{1,0:T(8,128)(2,1)S(1)} %collective-permute-done.refs_0_, ...), custom_call_target="tpu_custom_call" | custom-call | flops 679477248 | bytes 1048576 | tf_op jit(solution)/shard_map/pallas_call | solution.py:94
  20.2 4.3 %collective-permute-start.2 = (bf16[384,384]{1,0:T(8,128)(2,1)S(1)}, bf16[384,384]{1,0:T(8,128)(2,1)S(1)}, u32[]{:S(2)}, u32[]{:S(2)}) collective-permute-start(bf16[384,384]{1,0:T(8,128)(2,1)S(1)} %get-tuple-element.15), channel_id=1, source_target_pairs={{0,3},{1,0},{2,1},{3,2},{4,7},{5,4},{6,5},{7,6},{8,11},{9,8},{10,9... | collective-permute-start | bytes 884744 | tf_op jit(solution)/shard_map/ppermute | solution.py:133
  24.5 0.5 %shard_map.48.own_ref = f32[384,384]{1,0:T(8,128)S(1)} custom-call(bf16[2,384,384]{2,1,0:T(8,128)(2,1)S(1)} %get-tuple-element.14.left_ref, bf16[2,384,384]{2,1,0:T(8,128)(2,1)S(1)} %copy-done), custom_call_target="tpu_custom_call" | custom-call | flops 226492416 | bytes 1048576 | tf_op jit(solution)/shard_map/pallas_call | solution.py:94
  25.1 0.0 collective-permute-done.4.refs_0_
  25.1 0.0 collective-permute-done.5.refs_1_
  25.1 3.7 %collective-permute-done.2.term_ref = bf16[384,384]{1,0:T(8,128)(2,1)S(1)} collective-permute-done((bf16[384,384]{1,0:T(8,128)(2,1)S(1)}, bf16[384,384]{1,0:T(8,128)(2,1)S(1)}, u32[]{:S(2)}, u32[]{:S(2)}) %collective-permute-start.2) | collective-permute-done | bytes 294944 | tf_op jit(solution)/shard_map/ppermute | solution.py:133
  28.8 1.6 %shard_map.51 = bf16[1,1,2,384,384]{4,3,2,1,0:T(8,128)(2,1)} custom-call(s32[1,2,2]{2,1,0:T(2,128)S(1)} %copy-done.2, f32[384,384]{1,0:T(8,128)S(1)} %shard_map.48.own_ref, bf16[384,384]{1,0:T(8,128)(2,1)S(1)} %collective-permute-done.2.term_ref, bf16[384,384]{1,0:T(8,128)(2,1)S(1)} %collective-permute-done.4.refs_0_, ...), custom_call_target="tpu_custom_call" | custom-call | tf_op jit(solution)/shard_map/pallas_call | solution.py:193
Async XLA Ops:
  0.0 10.9 %copy-start = (bf16[2,384,384]{2,1,0:T(8,128)(2,1)S(1)}, bf16[2,384,384]{2,1,0:T(8,128)(2,1)}, u32[]{:S(2)}) copy-start(bf16[2,384,384]{2,1,0:T(8,128)(2,1)} %cm_ref.5) | copy-start | bytes 1769476
  1.1 11.4 %collective-permute-start.3 = (bf16[384,384]{1,0:T(8,128)(2,1)S(1)}, bf16[384,384]{1,0:T(8,128)(2,1)S(1)}, u32[]{:S(2)}, u32[]{:S(2)}) collective-permute-start(bf16[384,384]{1,0:T(8,128)(2,1)S(1)} %get-tuple-element.16.real_ref), channel_id=1, source_target_pairs={{0,3},{1,0},{2,1},{3,2},{4,7},{5,4},{6,5},{7,6},{8,11},{9,8},{10,9... | collective-permute-start | bytes 884744 | tf_op jit(solution)/shard_map/ppermute | solution.py:133
  6.2 6.3 %copy-start.1 = (bf16[2,384,384]{2,1,0:T(8,128)(2,1)S(1)}, bf16[2,384,384]{2,1,0:T(8,128)(2,1)}, u32[]{:S(2)}) copy-start(bf16[2,384,384]{2,1,0:T(8,128)(2,1)} %cn_ref.3) | copy-start | bytes 1769476
  6.2 12.0 %collective-permute-start = (bf16[384,384]{1,0:T(8,128)(2,1)S(1)}, bf16[384,384]{1,0:T(8,128)(2,1)S(1)}, u32[]{:S(2)}, u32[]{:S(2)}) collective-permute-start(bf16[384,384]{1,0:T(8,128)(2,1)S(1)} %get-tuple-element.13), channel_id=1, source_target_pairs={{28,0},{16,4},{20,8},{24,12},{4,16},{8,20},{12,24},{0,28},{29,1},{... | collective-permute-start | bytes 884744 | tf_op jit(solution)/shard_map/ppermute | solution.py:130
  7.9 10.4 %collective-permute-start.1 = (bf16[384,384]{1,0:T(8,128)(2,1)S(1)}, bf16[384,384]{1,0:T(8,128)(2,1)S(1)}, u32[]{:S(2)}, u32[]{:S(2)}) collective-permute-start(bf16[384,384]{1,0:T(8,128)(2,1)S(1)} %get-tuple-element.13), channel_id=1, source_target_pairs={{12,0},{0,12},{28,16},{16,28},{13,1},{1,13},{29,17},{17,29},{14,2}... | collective-permute-start | bytes 884744 | tf_op jit(solution)/shard_map/ppermute | solution.py:130
  13.5 4.7 %copy-start.2 = (s32[1,2,2]{2,1,0:T(2,128)S(1)}, s32[1,2,2]{2,1,0:T(2,128)}, u32[]{:S(2)}) copy-start(s32[1,2,2]{2,1,0:T(2,128)} %weights_ref.3) | copy-start | bytes 52
  13.5 11.5 %collective-permute-start.4 = (bf16[384,384]{1,0:T(8,128)(2,1)S(1)}, bf16[384,384]{1,0:T(8,128)(2,1)S(1)}, u32[]{:S(2)}, u32[]{:S(2)}) collective-permute-start(bf16[384,384]{1,0:T(8,128)(2,1)S(1)} %get-tuple-element.19), channel_id=1, source_target_pairs={{28,0},{16,4},{20,8},{24,12},{4,16},{8,20},{12,24},{0,28},{29,1},{... | collective-permute-start | bytes 884744 | tf_op jit(solution)/shard_map/ppermute | solution.py:130
  14.6 10.5 %collective-permute-start.5 = (bf16[384,384]{1,0:T(8,128)(2,1)S(1)}, bf16[384,384]{1,0:T(8,128)(2,1)S(1)}, u32[]{:S(2)}, u32[]{:S(2)}) collective-permute-start(bf16[384,384]{1,0:T(8,128)(2,1)S(1)} %get-tuple-element.20), channel_id=1, source_target_pairs={{12,0},{0,12},{28,16},{16,28},{13,1},{1,13},{29,17},{17,29},{14,2}... | collective-permute-start | bytes 884744 | tf_op jit(solution)/shard_map/ppermute | solution.py:130
  20.2 8.6 %collective-permute-start.2 = (bf16[384,384]{1,0:T(8,128)(2,1)S(1)}, bf16[384,384]{1,0:T(8,128)(2,1)S(1)}, u32[]{:S(2)}, u32[]{:S(2)}) collective-permute-start(bf16[384,384]{1,0:T(8,128)(2,1)S(1)} %get-tuple-element.15), channel_id=1, source_target_pairs={{0,3},{1,0},{2,1},{3,2},{4,7},{5,4},{6,5},{7,6},{8,11},{9,8},{10,9... | collective-permute-start | bytes 884744 | tf_op jit(solution)/shard_map/ppermute | solution.py:133

commit v2 on v1

v2 whole, which is shorter than its diff:
```python
import functools

import jax
import jax.numpy as jnp
from jax import lax
from jax.experimental import pallas as pl
from jax.experimental.pallas import tpu as pltpu
from jax.sharding import PartitionSpec as P

SHIFTS = (3, 7)
LONG = 400
F32, BF16 = jnp.float32, jnp.bfloat16
NT = (((1,), (1,)), ((), ()))


def matchings(count):
    left = {}
    for target in range(count):
        for mode, shift in enumerate(SHIFTS):
            for side, source in enumerate((target + shift, target - shift)):
                if 0 <= source < count:
                    left[source, target] = (mode, side)
    rounds = []
    while left:
        options = {}
        for source, target in sorted(left):
            options.setdefault(source, []).append(target)
        taken = {}

        def place(source, seen):
            for target in options[source]:
                if target not in seen:
                    seen.add(target)
                    if target not in taken or place(taken[target], seen):
                        taken[target] = source
                        return True
            return False

        for source in sorted(options):
            place(source, set())
        rounds.append({t: (s,) + left.pop((s, t)) for t, s in sorted(taken.items())})
    return rounds


def lookup(table, index):
    value = jnp.int32(table[0])
    for start in range(len(table)):
        if start and table[start] != table[start - 1]:
            value = jnp.where(index >= start, jnp.int32(table[start]), value)
    return value


def routes(plan, count):
    out = []
    for step in plan:
        took, gave = [0] * count, [0] * count
        for target, (source, mode, side) in step.items():
            took[target] = 1 + mode * 2 + side
            gave[source] = mode
        out.append((took, gave))
    return out


def arriving(route):
    code = lookup(route[0], lax.axis_index("energy"))
    slot = jnp.maximum(code - 1, 0)
    return slot // 2, slot % 2, code > 0


def exchange(count, slabs, odd):
    pairs = []
    for e in range(count):
        for s in range(slabs):
            other = s + 1 if s % 2 == odd else s - 1
            if 0 <= other < slabs:
                pairs.append((e * slabs + s, e * slabs + other))
            elif e ^ 1 < count:
                pairs.append((e * slabs + s, (e ^ 1) * slabs + s))
    return pairs


def dot(a, b):
    return jnp.dot(a, b, preferred_element_type=F32)


def dot_t(a, b):
    return lax.dot_general(a, b, NT, preferred_element_type=F32)


def couple(mat, x):
    return dot_t(dot(mat, x).astype(BF16), mat)


VM = pl.BlockSpec(memory_space=pltpu.VMEM)
SM = pl.BlockSpec(memory_space=pltpu.SMEM)
ANY = pl.BlockSpec(memory_space=pl.ANY)


def call(kernel, ins, outs, products, size, *args, scratch=()):
    return pl.pallas_call(
        kernel,
        out_shape=outs,
        in_specs=ins,
        out_specs=[VM] * len(outs),
        scratch_shapes=scratch,
        cost_estimate=pl.CostEstimate(flops=2 * products * size**3, bytes_accessed=1 << 20, transcendentals=0),
        compiler_params=pltpu.CompilerParams(vmem_limit_bytes=24 << 20),
    )(*args)


def body(count, slabs, plan, green, weights, coupling_m, coupling_n):
    size = green.shape[-1]
    block = pltpu.VMEM((size, size), BF16)
    wide = pltpu.VMEM((size, size), F32)
    rounds = len(plan)
    route = routes(plan, count)

    def split(green_ref, real_ref, imag_ref, sems):
        copies = [
            pltpu.make_async_copy(green_ref.at[0, 0, part], out, sems.at[part])
            for part, out in enumerate((real_ref, imag_ref))
        ]
        for copy in copies:
            copy.start()
        for copy in copies:
            copy.wait()

    real, imag = pl.pallas_call(
        split,
        out_shape=[block, block],
        in_specs=[ANY],
        out_specs=[VM, VM],
        scratch_shapes=[pltpu.SemaphoreType.DMA((2,))],
    )(green)

    def along(x, step):
        return lax.ppermute(x, "energy", [(s, t) for t, (s, _, _) in step.items()])

    def from_next(x):
        return [lax.ppermute(x, ("energy", "slab"), exchange(count, slabs, odd)) for odd in range(2)]

    def sent_mode(r):
        return lookup(route[r][1], lax.axis_index("energy"))

    near = [along(imag, step) for step in plan]
    behind = from_next(real)

    def first(weights_ref, real_ref, cm_ref, factor_ref, *outs):
        for r, out in enumerate(outs):
            mode, side, present = arriving(route[r])
            factor = jnp.where(present, weights_ref[0, mode, side], 0).astype(F32) / 32.0
            factor_ref[r] = jnp.full((8, size), factor, F32)
            out[...] = couple(cm_ref[sent_mode(r)], real_ref[...])

    factors, *partial = call(
        first,
        [SM, VM, VM],
        [pltpu.VMEM((rounds, 8, size), F32)] + [wide] * rounds,
        2 * rounds,
        size,
        weights,
        real,
        coupling_m,
    )

    def scaled(ref, factor_ref, r):
        return factor_ref[r, 0:1, :] * ref[...].astype(F32)

    def term_first(factor_ref, cn_ref, got_ref, out_ref):
        mode, _, present = arriving(route[0])
        ahead = lax.axis_index("slab") > 0

        @pl.when(present & ahead)
        def _():
            out_ref[...] = couple(cn_ref[mode], scaled(got_ref, factor_ref, 0).astype(BF16))

        @pl.when(jnp.logical_not(present & ahead))
        def _():
            out_ref[...] = jnp.zeros_like(out_ref)

    (begun,) = call(term_first, [VM, VM, VM], [wide], 2, size, factors, coupling_n, near[0])

    def even_only(even_ref, after_ref, out_ref):
        @pl.when(lax.axis_index("slab") % 2 == 0)
        def _():
            out_ref[...] = even_ref[...]

    (held,) = call(even_only, [VM, ANY], [block], 2, size, behind[0], begun)

    def whole(rs, after):
        def kernel(held_ref, odd_ref, cn_ref, after_ref, *refs):
            parts, outs, next_ref = refs[: len(rs)], refs[len(rs) : -1], refs[-1]
            slab = lax.axis_index("slab")
            here = slab < slabs - 1
            for odd, ref in enumerate((held_ref, odd_ref)):

                @pl.when(here & (slab % 2 == odd))
                def _():
                    next_ref[...] = ref[...]

            for r, part, out in zip(rs, parts, outs):

                @pl.when(here)
                def _():
                    out[...] = (part[...] + couple(cn_ref[sent_mode(r)], next_ref[...])).astype(BF16)

                @pl.when(jnp.logical_not(here))
                def _():
                    out[...] = part[...].astype(BF16)

        return call(
            kernel,
            [VM, VM, VM, ANY] + [VM] * len(rs),
            [block] * len(rs),
            2 * len(rs),
            size,
            held,
            behind[1],
            coupling_n,
            after,
            *[partial[r] for r in rs],
            scratch=[block],
        )

    results = whole([0], begun)
    arrived = [along(results[0], plan[0])]

    def term_rest(factor_ref, cn_ref, after_ref, begun_ref, *refs):
        got, out_ref, total_ref = refs[:-2], refs[-2], refs[-1]
        total_ref[...] = begun_ref[...]
        for r, ref in enumerate(got, 1):
            mode, _, present = arriving(route[r])

            @pl.when(present & (lax.axis_index("slab") > 0))
            def _():
                total_ref[...] += couple(cn_ref[mode], scaled(ref, factor_ref, r).astype(BF16))

        out_ref[...] = total_ref[...].astype(BF16)

    (term,) = call(
        term_rest,
        [VM, VM, ANY, VM] + [VM] * (rounds - 1),
        [block],
        2 * rounds - 2,
        size,
        factors,
        coupling_n,
        results[0],
        begun,
        *near[1:],
        scratch=[wide],
    )
    term_next = from_next(term)
    if rounds > 1:
        results = results + whole(list(range(1, rounds)), term)
        arrived += [along(results[r], plan[r]) for r in range(1, rounds)]

    def own_sum(factor_ref, cm_ref, after_ref, *refs):
        got, out_ref = refs[:-1], refs[-1]
        out_ref[...] = jnp.zeros_like(out_ref)
        for r, ref in enumerate(got):
            mode, _, present = arriving(route[r])

            @pl.when(present)
            def _():
                out_ref[...] += couple(cm_ref[mode], scaled(ref, factor_ref, r).astype(BF16))

    (own,) = call(
        own_sum, [VM, VM, ANY] + [VM] * rounds, [wide], 2 * rounds, size, factors, coupling_m, results[-1], *near
    )

    def real_first(factor_ref, got_ref, out_ref):
        out_ref[...] = scaled(got_ref, factor_ref, 0)

    (real_sum,) = call(real_first, [VM, VM], [wide], LONG, size, factors, arrived[0])

    def imag_part(odd, source):
        def kernel(own_ref, term_ref, source_ref, out_ref):
            slab = lax.axis_index("slab")
            mine = slab % 2 == odd
            last = slab == slabs - 1

            @pl.when(mine & jnp.logical_not(last))
            def _():
                out_ref[...] = (own_ref[...] + term_ref[...].astype(F32)).astype(BF16)

            if odd:

                @pl.when(last)
                def _():
                    out_ref[...] = own_ref[...].astype(BF16)

                @pl.when(jnp.logical_not(mine | last))
                def _():
                    out_ref[...] = source_ref[...]

        return call(kernel, [VM, VM, VM if odd else ANY], [block], LONG, size, own, term_next[odd], source)[0]

    imag_sum = imag_part(1, imag_part(0, real_sum))

    def finish(factor_ref, imag_ref, real_ref, *refs):
        got, out_ref, held_ref, sems = refs[: rounds - 1], refs[-3], refs[-2], refs[-1]
        imag_copy = pltpu.make_async_copy(imag_ref, out_ref.at[0, 0, 1], sems.at[1])
        imag_copy.start()
        total = real_ref[...]
        for r, ref in enumerate(got, 1):
            total += scaled(ref, factor_ref, r)
        held_ref[...] = total.astype(BF16)
        real_copy = pltpu.make_async_copy(held_ref, out_ref.at[0, 0, 0], sems.at[0])
        real_copy.start()
        imag_copy.wait()
        real_copy.wait()

    return pl.pallas_call(
        finish,
        out_shape=jax.ShapeDtypeStruct(green.shape, BF16),
        in_specs=[VM] * (2 + rounds),
        out_specs=ANY,
        scratch_shapes=[block, pltpu.SemaphoreType.DMA((2,))],
        compiler_params=pltpu.CompilerParams(vmem_limit_bytes=24 << 20),
    )(factors, imag_sum, real_sum, *arrived[1:])


def solution(mesh):
    count, slabs = mesh.shape["energy"], mesh.shape["slab"]
    placed = (P("energy", "slab", None, None, None), P("energy", None, None), P(), P())
    return jax.shard_map(
        functools.partial(body, count, slabs, matchings(count)),
        mesh=mesh,
        in_specs=placed,
        out_specs=P("energy", "slab", None, None, None),
        check_vma=False,
    )
```

time: 30.5 us -> 27.8 us (0.911)
  starting transfers between devices: 18.7 us -> 14.4 us
  waiting for transfers between devices: 4.31 us -> 6.65 us
  Pallas kernels: 7.15 us -> 6.39 us
    ppermute x2 -> x4, starting transfers between devices: 9.44 us -> 5.28 us  [from_next(): lax.ppermute(x, ('energy', 'slab'), exchange(count, slabs, odd))]
    ppermute x4, waiting for transfers between devices: 0.01 us -> 2.12 us  [along(): return lax.ppermute(x, 'energy', [(s, t) for t, (s, _, _) in step.items()])]
    pallas_call x1, Pallas kernels: 1.56 us -> 0.83 us  [body(): pl.pallas_call(finish, out_shape=jax.ShapeDtypeStruct(green.shape, BF16),...]
    ppermute x2 -> x4, waiting for transfers between devices: 4.3 us -> 4.53 us  [from_next(): lax.ppermute(x, ('energy', 'slab'), exchange(count, slabs, odd))]
    pallas_call x4 -> x10, Pallas kernels: 4.46 us -> 4.44 us  [call(): pl.pallas_call(kernel, out_shape=outs, in_specs=ins, out_specs=[VM] * len...]
  transfers between devices with their start and end apart: 6 -> 8, of which waited for: 2 -> 3; matrix products, arithmetic and copies ran while one was open for 0% -> 0% of each run, Pallas kernels for 15% -> 16%
where the time goes in v2:
time: 27.8 us; the launch traced here: 27.7 us
  starting transfers between devices  14.4 us (52%)
  waiting for transfers between devices  6.65 us (24%)
  Pallas kernels  6.39 us (23%)
    ppermute x4, starting transfers between devices, along(): return lax.ppermute(x, 'energy', [(s, t) for t, (s, _, _) in step.items()])  9.17 us
    ppermute x4, starting transfers between devices, from_next(): lax.ppermute(x, ('energy', 'slab'), exchange(count, slabs, odd))  5.28 us
    ppermute x4, waiting for transfers between devices, from_next(): lax.ppermute(x, ('energy', 'slab'), exchange(count, slabs, odd))  4.53 us
    pallas_call x10, Pallas kernels, call(): pl.pallas_call(kernel, out_shape=outs, in_specs=ins, out_specs=[VM] * len...  4.44 us
    ppermute x4, waiting for transfers between devices, along(): return lax.ppermute(x, 'energy', [(s, t) for t, (s, _, _) in step.items()])  2.12 us
    pallas_call x1, Pallas kernels, body(): pl.pallas_call(split, out_shape=[block, block], in_specs=[ANY], out_specs...  1.13 us
    pallas_call x1, Pallas kernels, body(): pl.pallas_call(finish, out_shape=jax.ShapeDtypeStruct(green.shape, BF16),...  0.83 us
  transfers between devices with their start and end apart: 8, of which 3 were waited for; matrix products, arithmetic and copies ran while one was open for 0% of the time, Pallas kernels for 16%

profile of v2, /device:TPU:0, one launch (start us, length us, event | category | flops | bytes accessed | tf_op | source)
XLA Modules:
  0.0 27.7 jit_solution(2215974834755385072)
XLA Ops:
  0.0 0.0 copy-start.1
  0.0 1.1 %shard_map.46 = (bf16[384,384]{1,0:T(8,128)(2,1)S(1)}, bf16[384,384]{1,0:T(8,128)(2,1)S(1)}) custom-call(bf16[1,1,2,384,384]{4,3,2,1,0:T(8,128)(2,1)} %green_ref.1), custom_call_target="tpu_custom_call" | custom-call | tf_op jit(solution)/shard_map/pallas_call | solution.py:128
  1.1 0.0 copy-start.2
  1.2 3.4 %collective-permute-start.1 = (bf16[384,384]{1,0:T(8,128)(2,1)S(1)}, bf16[384,384]{1,0:T(8,128)(2,1)S(1)}, u32[]{:S(2)}, u32[]{:S(2)}) collective-permute-start(bf16[384,384]{1,0:T(8,128)(2,1)S(1)} %get-tuple-element.12), channel_id=1, source_target_pairs={{28,0},{16,4},{20,8},{24,12},{4,16},{8,20},{12,24},{0,28},{29,1},{... | collective-permute-start | bytes 884744 | tf_op jit(solution)/shard_map/ppermute | solution.py:137
  4.6 0.0 copy-start
  4.6 1.6 %collective-permute-start = (bf16[384,384]{1,0:T(8,128)(2,1)S(1)}, bf16[384,384]{1,0:T(8,128)(2,1)S(1)}, u32[]{:S(2)}, u32[]{:S(2)}) collective-permute-start(bf16[384,384]{1,0:T(8,128)(2,1)S(1)} %get-tuple-element.10.real_ref), channel_id=1, source_target_pairs={{0,1},{1,0},{2,3},{3,2},{4,5},{5,4},{6,7},{7,6},{8,9},{9,8},{10,11... | collective-permute-start | bytes 884744 | tf_op jit(solution)/shard_map/ppermute | solution.py:140
  6.1 0.0 collective-permute-start.2
  6.1 2.5 %collective-permute-start.3 = (bf16[384,384]{1,0:T(8,128)(2,1)S(1)}, bf16[384,384]{1,0:T(8,128)(2,1)S(1)}, u32[]{:S(2)}, u32[]{:S(2)}) collective-permute-start(bf16[384,384]{1,0:T(8,128)(2,1)S(1)} %get-tuple-element.12), channel_id=1, source_target_pairs={{12,0},{0,12},{28,16},{16,28},{13,1},{1,13},{29,17},{17,29},{14,2}... | collective-permute-start | bytes 884744 | tf_op jit(solution)/shard_map/ppermute | solution.py:137
  8.7 0.0 copy-done.1
  8.7 0.0 copy-done.2
  8.7 1.6 %shard_map.47 = (f32[2,8,384]{2,1,0:T(8,128)S(1)}, f32[384,384]{1,0:T(8,128)S(1)}, f32[384,384]{1,0:T(8,128)S(1)}) custom-call(s32[1,2,2]{2,1,0:T(2,128)S(1)} %copy-done.2, bf16[384,384]{1,0:T(8,128)(2,1)S(1)} %get-tuple-element.10.real_ref, bf16[2,384,384]{2,1,0:T(8,128)(2,1)S(1)} %copy-done.1), custom_call_target="tpu_custom_call" | custom-call | flops 452984832 | bytes 1048576 | tf_op jit(solution)/shard_map/pallas_call | solution.py:100
  10.3 0.0 collective-permute-done.1.got_ref.refs_0_
  10.3 0.0 copy-done
  10.3 0.1 shard_map.48.after_ref.begun_ref
  10.4 2.9 %collective-permute-done.even_ref = bf16[384,384]{1,0:T(8,128)(2,1)S(1)} collective-permute-done((bf16[384,384]{1,0:T(8,128)(2,1)S(1)}, bf16[384,384]{1,0:T(8,128)(2,1)S(1)}, u32[]{:S(2)}, u32[]{:S(2)}) %collective-permute-start) | collective-permute-done | bytes 294944 | tf_op jit(solution)/shard_map/ppermute | solution.py:140
  13.2 0.0 collective-permute-done.2.odd_ref
  13.3 0.7 %shard_map.50.after_ref = bf16[384,384]{1,0:T(8,128)(2,1)S(1)} custom-call(bf16[384,384]{1,0:T(8,128)(2,1)S(1)} %shard_map.49.held_ref, bf16[384,384]{1,0:T(8,128)(2,1)S(1)} %collective-permute-done.2.odd_ref, bf16[2,384,384]{2,1,0:T(8,128)(2,1)S(1)} %copy-done, f32[384,384]{1,0:T(8,128)S(1)} %shard_map.48.after_ref.begun_ref, ...), custom_call_target="tpu_custom_call" | custom-call | flops 226492416 | bytes 1048576 | tf_op jit(solution)/shard_map/pallas_call | solution.py:100
  13.9 0.4 %collective-permute-start.6 = (bf16[384,384]{1,0:T(8,128)(2,1)S(1)}, bf16[384,384]{1,0:T(8,128)(2,1)S(1)}, u32[]{:S(2)}, u32[]{:S(2)}) collective-permute-start(bf16[384,384]{1,0:T(8,128)(2,1)S(1)} %shard_map.50.after_ref), channel_id=1, source_target_pairs={{28,0},{16,4},{20,8},{24,12},{4,16},{8,20},{12,24},{0,28},{29,1},{... | collective-permute-start | bytes 884744 | tf_op jit(solution)/shard_map/ppermute | solution.py:137
  14.4 0.0 collective-permute-done.3.refs_0_.refs_1_
  14.4 0.1 shard_map.51.after_ref
  14.4 3.7 %collective-permute-start.5 = (bf16[384,384]{1,0:T(8,128)(2,1)S(1)}, bf16[384,384]{1,0:T(8,128)(2,1)S(1)}, u32[]{:S(2)}, u32[]{:S(2)}) collective-permute-start(bf16[384,384]{1,0:T(8,128)(2,1)S(1)} %shard_map.51.after_ref), channel_id=1, source_target_pairs={{0,1},{1,0},{2,3},{3,2},{4,5},{5,4},{6,7},{7,6},{8,9},{9,8},{10,11... | collective-permute-start | bytes 884744 | tf_op jit(solution)/shard_map/ppermute | solution.py:140
  18.1 0.0 collective-permute-start.4
  18.1 0.6 %shard_map.52.after_ref = bf16[384,384]{1,0:T(8,128)(2,1)S(1)} custom-call(bf16[384,384]{1,0:T(8,128)(2,1)S(1)} %shard_map.49.held_ref, bf16[384,384]{1,0:T(8,128)(2,1)S(1)} %collective-permute-done.2.odd_ref, bf16[2,384,384]{2,1,0:T(8,128)(2,1)S(1)} %copy-done, bf16[384,384]{1,0:T(8,128)(2,1)S(1)} %shard_map.51.after_ref, ...), custom_call_target="tpu_custom_call" | custom-call | flops 226492416 | bytes 1048576 | tf_op jit(solution)/shard_map/pallas_call | solution.py:100
  18.8 2.8 %collective-permute-start.7 = (bf16[384,384]{1,0:T(8,128)(2,1)S(1)}, bf16[384,384]{1,0:T(8,128)(2,1)S(1)}, u32[]{:S(2)}, u32[]{:S(2)}) collective-permute-start(bf16[384,384]{1,0:T(8,128)(2,1)S(1)} %shard_map.52.after_ref), channel_id=1, source_target_pairs={{12,0},{0,12},{28,16},{16,28},{13,1},{1,13},{29,17},{17,29},{14,2}... | collective-permute-start | bytes 884744 | tf_op jit(solution)/shard_map/ppermute | solution.py:137
  21.6 1.3 %shard_map.53.own_ref = f32[384,384]{1,0:T(8,128)S(1)} custom-call(f32[2,8,384]{2,1,0:T(8,128)S(1)} %get-tuple-element.11.factor_ref, bf16[2,384,384]{2,1,0:T(8,128)(2,1)S(1)} %copy-done.1, bf16[384,384]{1,0:T(8,128)(2,1)S(1)} %shard_map.52.after_ref, bf16[384,384]{1,0:T(8,128)(2,1)S(1)} %collective-permute-done.1.got_ref.refs_0_, ...), custom_call_target="tpu_custom_call" | custom-call | flops 452984832 | bytes 1048576 | tf_op jit(solution)/shard_map/pallas_call | solution.py:100
  22.9 0.0 collective-permute-done.6.got_ref
  22.9 1.7 %collective-permute-done.5.term_ref = bf16[384,384]{1,0:T(8,128)(2,1)S(1)} collective-permute-done((bf16[384,384]{1,0:T(8,128)(2,1)S(1)}, bf16[384,384]{1,0:T(8,128)(2,1)S(1)}, u32[]{:S(2)}, u32[]{:S(2)}) %collective-permute-start.5) | collective-permute-done | bytes 294944 | tf_op jit(solution)/shard_map/ppermute | solution.py:140
  24.6 0.1 shard_map.55.source_ref
  24.6 0.0 collective-permute-done.4.term_ref
  24.7 2.1 %collective-permute-done.7.refs_0_ = bf16[384,384]{1,0:T(8,128)(2,1)S(1)} collective-permute-done((bf16[384,384]{1,0:T(8,128)(2,1)S(1)}, bf16[384,384]{1,0:T(8,128)(2,1)S(1)}, u32[]{:S(2)}, u32[]{:S(2)}) %collective-permute-start.7) | collective-permute-done | bytes 294944 | tf_op jit(solution)/shard_map/ppermute | solution.py:137
  26.8 0.8 %shard_map.57 = bf16[1,1,2,384,384]{4,3,2,1,0:T(8,128)(2,1)} custom-call(f32[2,8,384]{2,1,0:T(8,128)S(1)} %get-tuple-element.11.factor_ref, bf16[384,384]{1,0:T(8,128)(2,1)S(1)} %shard_map.56.imag_ref, f32[384,384]{1,0:T(8,128)S(1)} %shard_map.54.source_ref.real_ref, bf16[384,384]{1,0:T(8,128)(2,1)S(1)} %collective-permute-done.7.refs_0_), custom_call_target="tpu_custom_call" | custom-call | tf_op jit(solution)/shard_map/pallas_call | solution.py:314
  (3 shorter events, 0.1 us)
Async XLA Ops:
  0.0 8.7 %copy-start.1 = (bf16[2,384,384]{2,1,0:T(8,128)(2,1)S(1)}, bf16[2,384,384]{2,1,0:T(8,128)(2,1)}, u32[]{:S(2)}) copy-start(bf16[2,384,384]{2,1,0:T(8,128)(2,1)} %cm_ref.3) | copy-start | bytes 1769476
  1.1 7.6 %copy-start.2 = (s32[1,2,2]{2,1,0:T(2,128)S(1)}, s32[1,2,2]{2,1,0:T(2,128)}, u32[]{:S(2)}) copy-start(s32[1,2,2]{2,1,0:T(2,128)} %weights_ref.1) | copy-start | bytes 52
  1.2 9.1 %collective-permute-start.1 = (bf16[384,384]{1,0:T(8,128)(2,1)S(1)}, bf16[384,384]{1,0:T(8,128)(2,1)S(1)}, u32[]{:S(2)}, u32[]{:S(2)}) collective-permute-start(bf16[384,384]{1,0:T(8,128)(2,1)S(1)} %get-tuple-element.12), channel_id=1, source_target_pairs={{28,0},{16,4},{20,8},{24,12},{4,16},{8,20},{12,24},{0,28},{29,1},{... | collective-permute-start | bytes 884744 | tf_op jit(solution)/shard_map/ppermute | solution.py:137
  4.6 5.7 %copy-start = (bf16[2,384,384]{2,1,0:T(8,128)(2,1)S(1)}, bf16[2,384,384]{2,1,0:T(8,128)(2,1)}, u32[]{:S(2)}) copy-start(bf16[2,384,384]{2,1,0:T(8,128)(2,1)} %cn_ref.7) | copy-start | bytes 1769476
  4.6 8.7 %collective-permute-start = (bf16[384,384]{1,0:T(8,128)(2,1)S(1)}, bf16[384,384]{1,0:T(8,128)(2,1)S(1)}, u32[]{:S(2)}, u32[]{:S(2)}) collective-permute-start(bf16[384,384]{1,0:T(8,128)(2,1)S(1)} %get-tuple-element.10.real_ref), channel_id=1, source_target_pairs={{0,1},{1,0},{2,3},{3,2},{4,5},{5,4},{6,7},{7,6},{8,9},{9,8},{10,11... | collective-permute-start | bytes 884744 | tf_op jit(solution)/shard_map/ppermute | solution.py:140
  6.1 7.1 %collective-permute-start.2 = (bf16[384,384]{1,0:T(8,128)(2,1)S(1)}, bf16[384,384]{1,0:T(8,128)(2,1)S(1)}, u32[]{:S(2)}, u32[]{:S(2)}) collective-permute-start(bf16[384,384]{1,0:T(8,128)(2,1)S(1)} %get-tuple-element.10.real_ref), channel_id=1, source_target_pairs={{0,4},{1,2},{2,1},{3,7},{4,0},{5,6},{6,5},{7,3},{8,12},{9,10},{10,... | collective-permute-start | bytes 884744 | tf_op jit(solution)/shard_map/ppermute | solution.py:140
  6.1 8.2 %collective-permute-start.3 = (bf16[384,384]{1,0:T(8,128)(2,1)S(1)}, bf16[384,384]{1,0:T(8,128)(2,1)S(1)}, u32[]{:S(2)}, u32[]{:S(2)}) collective-permute-start(bf16[384,384]{1,0:T(8,128)(2,1)S(1)} %get-tuple-element.12), channel_id=1, source_target_pairs={{12,0},{0,12},{28,16},{16,28},{13,1},{1,13},{29,17},{17,29},{14,2}... | collective-permute-start | bytes 884744 | tf_op jit(solution)/shard_map/ppermute | solution.py:137
  13.9 9.0 %collective-permute-start.6 = (bf16[384,384]{1,0:T(8,128)(2,1)S(1)}, bf16[384,384]{1,0:T(8,128)(2,1)S(1)}, u32[]{:S(2)}, u32[]{:S(2)}) collective-permute-start(bf16[384,384]{1,0:T(8,128)(2,1)S(1)} %shard_map.50.after_ref), channel_id=1, source_target_pairs={{28,0},{16,4},{20,8},{24,12},{4,16},{8,20},{12,24},{0,28},{29,1},{... | collective-permute-start | bytes 884744 | tf_op jit(solution)/shard_map/ppermute | solution.py:137
  14.4 10.1 %collective-permute-start.5 = (bf16[384,384]{1,0:T(8,128)(2,1)S(1)}, bf16[384,384]{1,0:T(8,128)(2,1)S(1)}, u32[]{:S(2)}, u32[]{:S(2)}) collective-permute-start(bf16[384,384]{1,0:T(8,128)(2,1)S(1)} %shard_map.51.after_ref), channel_id=1, source_target_pairs={{0,1},{1,0},{2,3},{3,2},{4,5},{5,4},{6,7},{7,6},{8,9},{9,8},{10,11... | collective-permute-start | bytes 884744 | tf_op jit(solution)/shard_map/ppermute | solution.py:140
  18.1 6.5 %collective-permute-start.4 = (bf16[384,384]{1,0:T(8,128)(2,1)S(1)}, bf16[384,384]{1,0:T(8,128)(2,1)S(1)}, u32[]{:S(2)}, u32[]{:S(2)}) collective-permute-start(bf16[384,384]{1,0:T(8,128)(2,1)S(1)} %shard_map.51.after_ref), channel_id=1, source_target_pairs={{0,4},{1,2},{2,1},{3,7},{4,0},{5,6},{6,5},{7,3},{8,12},{9,10},{10,... | collective-permute-start | bytes 884744 | tf_op jit(solution)/shard_map/ppermute | solution.py:140
  18.8 8.0 %collective-permute-start.7 = (bf16[384,384]{1,0:T(8,128)(2,1)S(1)}, bf16[384,384]{1,0:T(8,128)(2,1)S(1)}, u32[]{:S(2)}, u32[]{:S(2)}) collective-permute-start(bf16[384,384]{1,0:T(8,128)(2,1)S(1)} %shard_map.52.after_ref), channel_id=1, source_target_pairs={{12,0},{0,12},{28,16},{16,28},{13,1},{1,13},{29,17},{17,29},{14,2}... | collective-permute-start | bytes 884744 | tf_op jit(solution)/shard_map/ppermute | solution.py:137

commit v3 on v2

--- a/solution.py
+++ b/solution.py
@@ -8,6 +8,7 @@
 from jax.sharding import PartitionSpec as P
 
 SHIFTS = (3, 7)
+KINDS = (1, 0)
 LONG = 400
 F32, BF16 = jnp.float32, jnp.bfloat16
 NT = (((1,), (1,)), ((), ()))
@@ -67,13 +68,15 @@
     return slot // 2, slot % 2, code > 0
 
 
-def exchange(count, slabs, odd):
+def descent(count, slabs, kind):
     pairs = []
     for e in range(count):
+        if e ^ 1 >= count and e % 2 != kind:
+            continue
         for s in range(slabs):
-            other = s + 1 if s % 2 == odd else s - 1
-            if 0 <= other < slabs:
-                pairs.append((e * slabs + s, e * slabs + other))
+            to = s - 1 if e % 2 == kind else s + 1
+            if 0 <= to < slabs:
+                pairs.append((e * slabs + s, e * slabs + to))
             elif e ^ 1 < count:
                 pairs.append((e * slabs + s, (e ^ 1) * slabs + s))
     return pairs
@@ -137,7 +140,7 @@
         return lax.ppermute(x, "energy", [(s, t) for t, (s, _, _) in step.items()])
 
     def from_next(x):
-        return [lax.ppermute(x, ("energy", "slab"), exchange(count, slabs, odd)) for odd in range(2)]
+        return [lax.ppermute(x, ("energy", "slab"), descent(count, slabs, kind)) for kind in KINDS]
 
     def sent_mode(r):
         return lookup(route[r][1], lax.axis_index("energy"))
@@ -180,21 +183,23 @@
 
     (begun,) = call(term_first, [VM, VM, VM], [wide], 2, size, factors, coupling_n, near[0])
 
-    def even_only(even_ref, after_ref, out_ref):
-        @pl.when(lax.axis_index("slab") % 2 == 0)
+    def is_kind(k):
+        return lax.axis_index("energy") % 2 == KINDS[k]
+
+    def hold(one_ref, after_ref, out_ref):
+        @pl.when(is_kind(0))
         def _():
-            out_ref[...] = even_ref[...]
-
-    (held,) = call(even_only, [VM, ANY], [block], 2, size, behind[0], begun)
+            out_ref[...] = one_ref[...]
+
+    (held,) = call(hold, [VM, ANY], [block], 2, size, behind[0], begun)
 
     def whole(rs, after):
-        def kernel(held_ref, odd_ref, cn_ref, after_ref, *refs):
+        def kernel(held_ref, two_ref, cn_ref, after_ref, *refs):
             parts, outs, next_ref = refs[: len(rs)], refs[len(rs) : -1], refs[-1]
-            slab = lax.axis_index("slab")
-            here = slab < slabs - 1
-            for odd, ref in enumerate((held_ref, odd_ref)):
-
-                @pl.when(here & (slab % 2 == odd))
+            here = lax.axis_index("slab") < slabs - 1
+            for k, ref in enumerate((held_ref, two_ref)):
+
+                @pl.when(here & is_kind(k))
                 def _():
                     next_ref[...] = ref[...]
 
@@ -274,27 +279,25 @@
 
     (real_sum,) = call(real_first, [VM, VM], [wide], LONG, size, factors, arrived[0])
 
-    def imag_part(odd, source):
+    def imag_part(k, source):
         def kernel(own_ref, term_ref, source_ref, out_ref):
-            slab = lax.axis_index("slab")
-            mine = slab % 2 == odd
-            last = slab == slabs - 1
-
-            @pl.when(mine & jnp.logical_not(last))
+            last = lax.axis_index("slab") == slabs - 1
+
+            @pl.when(is_kind(k) & jnp.logical_not(last))
             def _():
                 out_ref[...] = (own_ref[...] + term_ref[...].astype(F32)).astype(BF16)
 
-            if odd:
-
-                @pl.when(last)
-                def _():
-                    out_ref[...] = own_ref[...].astype(BF16)
-
-                @pl.when(jnp.logical_not(mine | last))
+            @pl.when(is_kind(k) & last)
+            def _():
+                out_ref[...] = own_ref[...].astype(BF16)
+
+            if k:
+
+                @pl.when(is_kind(0))
                 def _():
                     out_ref[...] = source_ref[...]
 
-        return call(kernel, [VM, VM, VM if odd else ANY], [block], LONG, size, own, term_next[odd], source)[0]
+        return call(kernel, [VM, VM, VM if k else ANY], [block], LONG, size, own, term_next[k], source)[0]
 
     imag_sum = imag_part(1, imag_part(0, real_sum))
 

time: 27.8 us -> 26.7 us (0.960)
  starting transfers between devices: 14.4 us -> 13.5 us
    ppermute x4, starting transfers between devices: 5.28 us -> 4.36 us  [from_next(): lax.ppermute(x, ('energy', 'slab'), descent(count, slabs, kind))]
    ppermute x4, waiting for transfers between devices: 2.12 us -> 1.38 us  [along(): return lax.ppermute(x, 'energy', [(s, t) for t, (s, _, _) in step.items()])]
    ppermute x4, waiting for transfers between devices: 4.53 us -> 5.18 us  [from_next(): lax.ppermute(x, ('energy', 'slab'), descent(count, slabs, kind))]
  transfers between devices with their start and end apart: 8 -> 8, of which waited for: 3 -> 6; matrix products, arithmetic and copies ran while one was open for 0% -> 0% of each run, Pallas kernels for 16% -> 16%
where the time goes in v3:
time: 26.7 us; the launch traced here: 26.5 us
  starting transfers between devices  13.5 us (51%)
  waiting for transfers between devices  6.57 us (25%)
  Pallas kernels  6.31 us (24%)
    ppermute x4, starting transfers between devices, along(): return lax.ppermute(x, 'energy', [(s, t) for t, (s, _, _) in step.items()])  9.15 us
    ppermute x4, waiting for transfers between devices, from_next(): lax.ppermute(x, ('energy', 'slab'), descent(count, slabs, kind))  5.18 us
    ppermute x4, starting transfers between devices, from_next(): lax.ppermute(x, ('energy', 'slab'), descent(count, slabs, kind))  4.36 us
    pallas_call x10, Pallas kernels, call(): pl.pallas_call(kernel, out_shape=outs, in_specs=ins, out_specs=[VM] * len...  4.35 us
    ppermute x4, waiting for transfers between devices, along(): return lax.ppermute(x, 'energy', [(s, t) for t, (s, _, _) in step.items()])  1.38 us
    pallas_call x1, Pallas kernels, body(): pl.pallas_call(split, out_shape=[block, block], in_specs=[ANY], out_specs...  1.13 us
    pallas_call x1, Pallas kernels, body(): pl.pallas_call(finish, out_shape=jax.ShapeDtypeStruct(green.shape, BF16),...  0.83 us
  transfers between devices with their start and end apart: 8, of which 6 were waited for; matrix products, arithmetic and copies ran while one was open for 0% of the time, Pallas kernels for 16%

profile of v3, /device:TPU:0, one launch (start us, length us, event | category | flops | bytes accessed | tf_op | source)
XLA Modules:
  0.0 26.5 jit_solution(7490054251857959428)
XLA Ops:
  0.0 0.0 copy-start.1
  0.0 1.1 %shard_map.46 = (bf16[384,384]{1,0:T(8,128)(2,1)S(1)}, bf16[384,384]{1,0:T(8,128)(2,1)S(1)}) custom-call(bf16[1,1,2,384,384]{4,3,2,1,0:T(8,128)(2,1)} %green_ref.1), custom_call_target="tpu_custom_call" | custom-call | tf_op jit(solution)/shard_map/pallas_call | solution.py:131
  1.1 0.0 copy-start.2
  1.2 3.4 %collective-permute-start.1 = (bf16[384,384]{1,0:T(8,128)(2,1)S(1)}, bf16[384,384]{1,0:T(8,128)(2,1)S(1)}, u32[]{:S(2)}, u32[]{:S(2)}) collective-permute-start(bf16[384,384]{1,0:T(8,128)(2,1)S(1)} %get-tuple-element.12), channel_id=1, source_target_pairs={{28,0},{16,4},{20,8},{24,12},{4,16},{8,20},{12,24},{0,28},{29,1},{... | collective-permute-start | bytes 884744 | tf_op jit(solution)/shard_map/ppermute | solution.py:140
  4.6 0.0 copy-start
  4.6 1.6 %collective-permute-start = (bf16[384,384]{1,0:T(8,128)(2,1)S(1)}, bf16[384,384]{1,0:T(8,128)(2,1)S(1)}, u32[]{:S(2)}, u32[]{:S(2)}) collective-permute-start(bf16[384,384]{1,0:T(8,128)(2,1)S(1)} %get-tuple-element.10.real_ref), channel_id=1, source_target_pairs={{0,1},{1,2},{2,3},{3,7},{4,0},{5,4},{6,5},{7,6},{8,9},{9,10},{10,1... | collective-permute-start | bytes 884744 | tf_op jit(solution)/shard_map/ppermute | solution.py:143
  6.1 0.0 collective-permute-start.2
  6.1 2.6 %collective-permute-start.3 = (bf16[384,384]{1,0:T(8,128)(2,1)S(1)}, bf16[384,384]{1,0:T(8,128)(2,1)S(1)}, u32[]{:S(2)}, u32[]{:S(2)}) collective-permute-start(bf16[384,384]{1,0:T(8,128)(2,1)S(1)} %get-tuple-element.12), channel_id=1, source_target_pairs={{12,0},{0,12},{28,16},{16,28},{13,1},{1,13},{29,17},{17,29},{14,2}... | collective-permute-start | bytes 884744 | tf_op jit(solution)/shard_map/ppermute | solution.py:140
  8.8 0.0 copy-done.1
  8.8 0.0 copy-done.2
  8.8 1.6 %shard_map.47 = (f32[2,8,384]{2,1,0:T(8,128)S(1)}, f32[384,384]{1,0:T(8,128)S(1)}, f32[384,384]{1,0:T(8,128)S(1)}) custom-call(s32[1,2,2]{2,1,0:T(2,128)S(1)} %copy-done.2, bf16[384,384]{1,0:T(8,128)(2,1)S(1)} %get-tuple-element.10.real_ref, bf16[2,384,384]{2,1,0:T(8,128)(2,1)S(1)} %copy-done.1), custom_call_target="tpu_custom_call" | custom-call | flops 452984832 | bytes 1048576 | tf_op jit(solution)/shard_map/pallas_call | solution.py:103
  10.3 0.0 collective-permute-done.1.got_ref.refs_0_
  10.4 0.0 copy-done
  10.4 0.1 shard_map.48.after_ref.begun_ref
  10.4 2.0 %collective-permute-done.one_ref = bf16[384,384]{1,0:T(8,128)(2,1)S(1)} collective-permute-done((bf16[384,384]{1,0:T(8,128)(2,1)S(1)}, bf16[384,384]{1,0:T(8,128)(2,1)S(1)}, u32[]{:S(2)}, u32[]{:S(2)}) %collective-permute-start) | collective-permute-done | bytes 294944 | tf_op jit(solution)/shard_map/ppermute | solution.py:143
  12.5 0.7 %collective-permute-done.2.two_ref = bf16[384,384]{1,0:T(8,128)(2,1)S(1)} collective-permute-done((bf16[384,384]{1,0:T(8,128)(2,1)S(1)}, bf16[384,384]{1,0:T(8,128)(2,1)S(1)}, u32[]{:S(2)}, u32[]{:S(2)}) %collective-permute-start.2) | collective-permute-done | bytes 294944 | tf_op jit(solution)/shard_map/ppermute | solution.py:143
  13.2 0.6 %shard_map.50.after_ref = bf16[384,384]{1,0:T(8,128)(2,1)S(1)} custom-call(bf16[384,384]{1,0:T(8,128)(2,1)S(1)} %shard_map.49.held_ref, bf16[384,384]{1,0:T(8,128)(2,1)S(1)} %collective-permute-done.2.two_ref, bf16[2,384,384]{2,1,0:T(8,128)(2,1)S(1)} %copy-done, f32[384,384]{1,0:T(8,128)S(1)} %shard_map.48.after_ref.begun_ref, ...), custom_call_target="tpu_custom_call" | custom-call | flops 226492416 | bytes 1048576 | tf_op jit(solution)/shard_map/pallas_call | solution.py:103
  13.9 0.1 collective-permute-start.6
  13.9 0.2 collective-permute-done.3.refs_0_.refs_1_
  14.2 0.1 shard_map.51.after_ref
  14.2 2.8 %collective-permute-start.5 = (bf16[384,384]{1,0:T(8,128)(2,1)S(1)}, bf16[384,384]{1,0:T(8,128)(2,1)S(1)}, u32[]{:S(2)}, u32[]{:S(2)}) collective-permute-start(bf16[384,384]{1,0:T(8,128)(2,1)S(1)} %shard_map.51.after_ref), channel_id=1, source_target_pairs={{0,1},{1,2},{2,3},{3,7},{4,0},{5,4},{6,5},{7,6},{8,9},{9,10},{10,1... | collective-permute-start | bytes 884744 | tf_op jit(solution)/shard_map/ppermute | solution.py:143
  17.0 0.0 collective-permute-start.4
  17.0 0.6 %shard_map.52.after_ref = bf16[384,384]{1,0:T(8,128)(2,1)S(1)} custom-call(bf16[384,384]{1,0:T(8,128)(2,1)S(1)} %shard_map.49.held_ref, bf16[384,384]{1,0:T(8,128)(2,1)S(1)} %collective-permute-done.2.two_ref, bf16[2,384,384]{2,1,0:T(8,128)(2,1)S(1)} %copy-done, bf16[384,384]{1,0:T(8,128)(2,1)S(1)} %shard_map.51.after_ref, ...), custom_call_target="tpu_custom_call" | custom-call | flops 226492416 | bytes 1048576 | tf_op jit(solution)/shard_map/pallas_call | solution.py:103
  17.7 3.1 %collective-permute-start.7 = (bf16[384,384]{1,0:T(8,128)(2,1)S(1)}, bf16[384,384]{1,0:T(8,128)(2,1)S(1)}, u32[]{:S(2)}, u32[]{:S(2)}) collective-permute-start(bf16[384,384]{1,0:T(8,128)(2,1)S(1)} %shard_map.52.after_ref), channel_id=1, source_target_pairs={{12,0},{0,12},{28,16},{16,28},{13,1},{1,13},{29,17},{17,29},{14,2}... | collective-permute-start | bytes 884744 | tf_op jit(solution)/shard_map/ppermute | solution.py:140
  20.7 1.3 %shard_map.53.own_ref = f32[384,384]{1,0:T(8,128)S(1)} custom-call(f32[2,8,384]{2,1,0:T(8,128)S(1)} %get-tuple-element.11.factor_ref, bf16[2,384,384]{2,1,0:T(8,128)(2,1)S(1)} %copy-done.1, bf16[384,384]{1,0:T(8,128)(2,1)S(1)} %shard_map.52.after_ref, bf16[384,384]{1,0:T(8,128)(2,1)S(1)} %collective-permute-done.1.got_ref.refs_0_, ...), custom_call_target="tpu_custom_call" | custom-call | flops 452984832 | bytes 1048576 | tf_op jit(solution)/shard_map/pallas_call | solution.py:103
  22.0 0.0 collective-permute-done.6.got_ref
  22.1 1.7 %collective-permute-done.5.term_ref = bf16[384,384]{1,0:T(8,128)(2,1)S(1)} collective-permute-done((bf16[384,384]{1,0:T(8,128)(2,1)S(1)}, bf16[384,384]{1,0:T(8,128)(2,1)S(1)}, u32[]{:S(2)}, u32[]{:S(2)}) %collective-permute-start.5) | collective-permute-done | bytes 294944 | tf_op jit(solution)/shard_map/ppermute | solution.py:143
  23.8 0.7 %collective-permute-done.4.term_ref = bf16[384,384]{1,0:T(8,128)(2,1)S(1)} collective-permute-done((bf16[384,384]{1,0:T(8,128)(2,1)S(1)}, bf16[384,384]{1,0:T(8,128)(2,1)S(1)}, u32[]{:S(2)}, u32[]{:S(2)}) %collective-permute-start.4) | collective-permute-done | bytes 294944 | tf_op jit(solution)/shard_map/ppermute | solution.py:143
  24.5 0.1 shard_map.56.imag_ref
  24.6 1.2 %collective-permute-done.7.refs_0_ = bf16[384,384]{1,0:T(8,128)(2,1)S(1)} collective-permute-done((bf16[384,384]{1,0:T(8,128)(2,1)S(1)}, bf16[384,384]{1,0:T(8,128)(2,1)S(1)}, u32[]{:S(2)}, u32[]{:S(2)}) %collective-permute-start.7) | collective-permute-done | bytes 294944 | tf_op jit(solution)/shard_map/ppermute | solution.py:140
  25.7 0.8 %shard_map.57 = bf16[1,1,2,384,384]{4,3,2,1,0:T(8,128)(2,1)} custom-call(f32[2,8,384]{2,1,0:T(8,128)S(1)} %get-tuple-element.11.factor_ref, bf16[384,384]{1,0:T(8,128)(2,1)S(1)} %shard_map.56.imag_ref, f32[384,384]{1,0:T(8,128)S(1)} %shard_map.54.source_ref.real_ref, bf16[384,384]{1,0:T(8,128)(2,1)S(1)} %collective-permute-done.7.refs_0_), custom_call_target="tpu_custom_call" | custom-call | tf_op jit(solution)/shard_map/pallas_call | solution.py:317
  (3 shorter events, 0.0 us)
Async XLA Ops:
  0.0 8.8 %copy-start.1 = (bf16[2,384,384]{2,1,0:T(8,128)(2,1)S(1)}, bf16[2,384,384]{2,1,0:T(8,128)(2,1)}, u32[]{:S(2)}) copy-start(bf16[2,384,384]{2,1,0:T(8,128)(2,1)} %cm_ref.3) | copy-start | bytes 1769476
  1.1 7.6 %copy-start.2 = (s32[1,2,2]{2,1,0:T(2,128)S(1)}, s32[1,2,2]{2,1,0:T(2,128)}, u32[]{:S(2)}) copy-start(s32[1,2,2]{2,1,0:T(2,128)} %weights_ref.1) | copy-start | bytes 52
  1.2 9.2 %collective-permute-start.1 = (bf16[384,384]{1,0:T(8,128)(2,1)S(1)}, bf16[384,384]{1,0:T(8,128)(2,1)S(1)}, u32[]{:S(2)}, u32[]{:S(2)}) collective-permute-start(bf16[384,384]{1,0:T(8,128)(2,1)S(1)} %get-tuple-element.12), channel_id=1, source_target_pairs={{28,0},{16,4},{20,8},{24,12},{4,16},{8,20},{12,24},{0,28},{29,1},{... | collective-permute-start | bytes 884744 | tf_op jit(solution)/shard_map/ppermute | solution.py:140
  4.6 5.8 %copy-start = (bf16[2,384,384]{2,1,0:T(8,128)(2,1)S(1)}, bf16[2,384,384]{2,1,0:T(8,128)(2,1)}, u32[]{:S(2)}) copy-start(bf16[2,384,384]{2,1,0:T(8,128)(2,1)} %cn_ref.7) | copy-start | bytes 1769476
  4.6 7.9 %collective-permute-start = (bf16[384,384]{1,0:T(8,128)(2,1)S(1)}, bf16[384,384]{1,0:T(8,128)(2,1)S(1)}, u32[]{:S(2)}, u32[]{:S(2)}) collective-permute-start(bf16[384,384]{1,0:T(8,128)(2,1)S(1)} %get-tuple-element.10.real_ref), channel_id=1, source_target_pairs={{0,1},{1,2},{2,3},{3,7},{4,0},{5,4},{6,5},{7,6},{8,9},{9,10},{10,1... | collective-permute-start | bytes 884744 | tf_op jit(solution)/shard_map/ppermute | solution.py:143
  6.1 7.1 %collective-permute-start.2 = (bf16[384,384]{1,0:T(8,128)(2,1)S(1)}, bf16[384,384]{1,0:T(8,128)(2,1)S(1)}, u32[]{:S(2)}, u32[]{:S(2)}) collective-permute-start(bf16[384,384]{1,0:T(8,128)(2,1)S(1)} %get-tuple-element.10.real_ref), channel_id=1, source_target_pairs={{0,4},{1,0},{2,1},{3,2},{4,5},{5,6},{6,7},{7,3},{8,12},{9,8},{10,9... | collective-permute-start | bytes 884744 | tf_op jit(solution)/shard_map/ppermute | solution.py:143
  6.1 8.0 %collective-permute-start.3 = (bf16[384,384]{1,0:T(8,128)(2,1)S(1)}, bf16[384,384]{1,0:T(8,128)(2,1)S(1)}, u32[]{:S(2)}, u32[]{:S(2)}) collective-permute-start(bf16[384,384]{1,0:T(8,128)(2,1)S(1)} %get-tuple-element.12), channel_id=1, source_target_pairs={{12,0},{0,12},{28,16},{16,28},{13,1},{1,13},{29,17},{17,29},{14,2}... | collective-permute-start | bytes 884744 | tf_op jit(solution)/shard_map/ppermute | solution.py:140
  13.9 8.2 %collective-permute-start.6 = (bf16[384,384]{1,0:T(8,128)(2,1)S(1)}, bf16[384,384]{1,0:T(8,128)(2,1)S(1)}, u32[]{:S(2)}, u32[]{:S(2)}) collective-permute-start(bf16[384,384]{1,0:T(8,128)(2,1)S(1)} %shard_map.50.after_ref), channel_id=1, source_target_pairs={{28,0},{16,4},{20,8},{24,12},{4,16},{8,20},{12,24},{0,28},{29,1},{... | collective-permute-start | bytes 884744 | tf_op jit(solution)/shard_map/ppermute | solution.py:140
  14.2 9.5 %collective-permute-start.5 = (bf16[384,384]{1,0:T(8,128)(2,1)S(1)}, bf16[384,384]{1,0:T(8,128)(2,1)S(1)}, u32[]{:S(2)}, u32[]{:S(2)}) collective-permute-start(bf16[384,384]{1,0:T(8,128)(2,1)S(1)} %shard_map.51.after_ref), channel_id=1, source_target_pairs={{0,1},{1,2},{2,3},{3,7},{4,0},{5,4},{6,5},{7,6},{8,9},{9,10},{10,1... | collective-permute-start | bytes 884744 | tf_op jit(solution)/shard_map/ppermute | solution.py:143
  17.0 7.5 %collective-permute-start.4 = (bf16[384,384]{1,0:T(8,128)(2,1)S(1)}, bf16[384,384]{1,0:T(8,128)(2,1)S(1)}, u32[]{:S(2)}, u32[]{:S(2)}) collective-permute-start(bf16[384,384]{1,0:T(8,128)(2,1)S(1)} %shard_map.51.after_ref), channel_id=1, source_target_pairs={{0,4},{1,0},{2,1},{3,2},{4,5},{5,6},{6,7},{7,3},{8,12},{9,8},{10,9... | collective-permute-start | bytes 884744 | tf_op jit(solution)/shard_map/ppermute | solution.py:143
  17.7 8.0 %collective-permute-start.7 = (bf16[384,384]{1,0:T(8,128)(2,1)S(1)}, bf16[384,384]{1,0:T(8,128)(2,1)S(1)}, u32[]{:S(2)}, u32[]{:S(2)}) collective-permute-start(bf16[384,384]{1,0:T(8,128)(2,1)S(1)} %shard_map.52.after_ref), channel_id=1, source_target_pairs={{12,0},{0,12},{28,16},{16,28},{13,1},{1,13},{29,17},{17,29},{14,2}... | collective-permute-start | bytes 884744 | tf_op jit(solution)/shard_map/ppermute | solution.py:140

commit v4 on v3

--- a/solution.py
+++ b/solution.py
@@ -10,6 +10,7 @@
 SHIFTS = (3, 7)
 KINDS = (1, 0)
 LONG = 400
+SHORT = 2
 F32, BF16 = jnp.float32, jnp.bfloat16
 NT = (((1,), (1,)), ((), ()))
 
@@ -82,6 +83,11 @@
     return pairs
 
 
+def closed(step, count):
+    sources = {source for source, _, _ in step.values()}
+    return count % 2 == 0 and sources == set(step) and all((e in step) != (e + 1 in step) for e in range(0, count, 2))
+
+
 def dot(a, b):
     return jnp.dot(a, b, preferred_element_type=F32)
 
@@ -139,6 +145,13 @@
     def along(x, step):
         return lax.ppermute(x, "energy", [(s, t) for t, (s, _, _) in step.items()])
 
+    def along_closed(x, step):
+        if not closed(step, count):
+            return along(x, step)
+        swapped = lax.ppermute(x, "energy", [(e, e ^ 1) for e in range(count)])
+        pairs = [(s ^ 1, t) for t, (s, _, _) in step.items()] + [(t, t ^ 1) for t in step]
+        return lax.ppermute(swapped, "energy", pairs)
+
     def from_next(x):
         return [lax.ppermute(x, ("energy", "slab"), descent(count, slabs, kind)) for kind in KINDS]
 
@@ -169,20 +182,6 @@
     def scaled(ref, factor_ref, r):
         return factor_ref[r, 0:1, :] * ref[...].astype(F32)
 
-    def term_first(factor_ref, cn_ref, got_ref, out_ref):
-        mode, _, present = arriving(route[0])
-        ahead = lax.axis_index("slab") > 0
-
-        @pl.when(present & ahead)
-        def _():
-            out_ref[...] = couple(cn_ref[mode], scaled(got_ref, factor_ref, 0).astype(BF16))
-
-        @pl.when(jnp.logical_not(present & ahead))
-        def _():
-            out_ref[...] = jnp.zeros_like(out_ref)
-
-    (begun,) = call(term_first, [VM, VM, VM], [wide], 2, size, factors, coupling_n, near[0])
-
     def is_kind(k):
         return lax.axis_index("energy") % 2 == KINDS[k]
 
@@ -191,7 +190,7 @@
         def _():
             out_ref[...] = one_ref[...]
 
-    (held,) = call(hold, [VM, ANY], [block], 2, size, behind[0], begun)
+    (held,) = call(hold, [VM, ANY], [block], 2, size, behind[0], factors)
 
     def whole(rs, after):
         def kernel(held_ref, two_ref, cn_ref, after_ref, *refs):
@@ -227,8 +226,25 @@
             scratch=[block],
         )
 
-    results = whole([0], begun)
+    results = whole([0], factors)
     arrived = [along(results[0], plan[0])]
+    if rounds > 1:
+        results = results + whole(list(range(1, rounds)), results[0])
+        arrived += [along_closed(results[r], plan[r]) for r in range(1, rounds)]
+
+    def term_first(factor_ref, cn_ref, got_ref, after_ref, out_ref):
+        mode, _, present = arriving(route[0])
+        ahead = lax.axis_index("slab") > 0
+
+        @pl.when(present & ahead)
+        def _():
+            out_ref[...] = couple(cn_ref[mode], scaled(got_ref, factor_ref, 0).astype(BF16))
+
+        @pl.when(jnp.logical_not(present & ahead))
+        def _():
+            out_ref[...] = jnp.zeros_like(out_ref)
+
+    (begun,) = call(term_first, [VM, VM, VM, ANY], [wide], 2, size, factors, coupling_n, near[0], results[-1])
 
     def term_rest(factor_ref, cn_ref, after_ref, begun_ref, *refs):
         got, out_ref, total_ref = refs[:-2], refs[-2], refs[-1]
@@ -246,19 +262,16 @@
         term_rest,
         [VM, VM, ANY, VM] + [VM] * (rounds - 1),
         [block],
-        2 * rounds - 2,
+        LONG,
         size,
         factors,
         coupling_n,
-        results[0],
+        results[-1],
         begun,
         *near[1:],
         scratch=[wide],
     )
     term_next = from_next(term)
-    if rounds > 1:
-        results = results + whole(list(range(1, rounds)), term)
-        arrived += [along(results[r], plan[r]) for r in range(1, rounds)]
 
     def own_sum(factor_ref, cm_ref, after_ref, *refs):
         got, out_ref = refs[:-1], refs[-1]
@@ -271,13 +284,13 @@
                 out_ref[...] += couple(cm_ref[mode], scaled(ref, factor_ref, r).astype(BF16))
 
     (own,) = call(
-        own_sum, [VM, VM, ANY] + [VM] * rounds, [wide], 2 * rounds, size, factors, coupling_m, results[-1], *near
+        own_sum, [VM, VM, ANY] + [VM] * rounds, [wide], 2 * rounds, size, factors, coupling_m, term, *near
     )
 
     def real_first(factor_ref, got_ref, out_ref):
         out_ref[...] = scaled(got_ref, factor_ref, 0)
 
-    (real_sum,) = call(real_first, [VM, VM], [wide], LONG, size, factors, arrived[0])
+    (real_sum,) = call(real_first, [VM, VM], [wide], SHORT, size, factors, arrived[0])
 
     def imag_part(k, source):
         def kernel(own_ref, term_ref, source_ref, out_ref):
@@ -297,7 +310,7 @@
                 def _():
                     out_ref[...] = source_ref[...]
 
-        return call(kernel, [VM, VM, VM if k else ANY], [block], LONG, size, own, term_next[k], source)[0]
+        return call(kernel, [VM, VM, VM if k else ANY], [block], SHORT, size, own, term_next[k], source)[0]
 
     imag_sum = imag_part(1, imag_part(0, real_sum))
 

time: 26.7 us -> 25.4 us (0.951)
  starting transfers between devices: 13.5 us -> 12.3 us
  waiting for transfers between devices: 6.57 us -> 6.17 us
  local copies, waits for them, and re-layouts: 0.01 us -> 0.29 us
    ppermute x4 -> x3, starting transfers between devices: 9.15 us -> 5.05 us  [along(): return lax.ppermute(x, 'energy', [(s, t) for t, (s, _, _) in step.items()])]
    ppermute x4, starting transfers between devices: 4.36 us -> 5.99 us  [from_next(): lax.ppermute(x, ('energy', 'slab'), descent(count, slabs, kind))]
    ppermute x0 -> x2, starting transfers between devices: none -> 1.23 us  [the longest x1 1.23 us: along_closed(): swapped = lax.ppermute(x, 'energy', [(e, e ^ 1) for e in range(count)])]
    ppermute x4 -> x3, waiting for transfers between devices: 1.38 us -> 0.53 us  [along(): return lax.ppermute(x, 'energy', [(s, t) for t, (s, _, _) in step.items()])]
    ppermute x4, waiting for transfers between devices: 5.18 us -> 5.63 us  [from_next(): lax.ppermute(x, ('energy', 'slab'), descent(count, slabs, kind))]
    unnamed x6, local copies, waits for them, and re-layouts: 0.01 us -> 0.29 us
  transfers between devices with their start and end apart: 8 -> 9, of which waited for: 6 -> 5; matrix products, arithmetic and copies ran while one was open for 0% -> 0% of each run, Pallas kernels for 16% -> 17%
where the time goes in v4:
time: 25.4 us; the launch traced here: 25.2 us
  starting transfers between devices  12.3 us (48%)
  Pallas kernels  6.29 us (25%)
  waiting for transfers between devices  6.17 us (24%)
  local copies, waits for them, and re-layouts  0.29 us (1%)
    ppermute x4, starting transfers between devices, from_next(): lax.ppermute(x, ('energy', 'slab'), descent(count, slabs, kind))  5.99 us
    ppermute x4, waiting for transfers between devices, from_next(): lax.ppermute(x, ('energy', 'slab'), descent(count, slabs, kind))  5.63 us
    ppermute x3, starting transfers between devices, along(): return lax.ppermute(x, 'energy', [(s, t) for t, (s, _, _) in step.items()])  5.05 us
    pallas_call x10, Pallas kernels, call(): pl.pallas_call(kernel, out_shape=outs, in_specs=ins, out_specs=[VM] * len...  4.33 us
    ppermute x1, starting transfers between devices, along_closed(): swapped = lax.ppermute(x, 'energy', [(e, e ^ 1) for e in range(count)])  1.23 us
    pallas_call x1, Pallas kernels, body(): pl.pallas_call(split, out_shape=[block, block], in_specs=[ANY], out_specs...  1.13 us
    pallas_call x1, Pallas kernels, body(): pl.pallas_call(finish, out_shape=jax.ShapeDtypeStruct(green.shape, BF16),...  0.83 us
    ppermute x3, waiting for transfers between devices, along(): return lax.ppermute(x, 'energy', [(s, t) for t, (s, _, _) in step.items()])  0.53 us
  transfers between devices with their start and end apart: 9, of which 5 were waited for; matrix products, arithmetic and copies ran while one was open for 0% of the time, Pallas kernels for 17%

profile of v4, /device:TPU:0, one launch (start us, length us, event | category | flops | bytes accessed | tf_op | source)
XLA Modules:
  0.0 25.2 jit_solution(885680391909486308)
XLA Ops:
  0.0 0.0 copy-start.1
  0.0 1.1 %shard_map.46 = (bf16[384,384]{1,0:T(8,128)(2,1)S(1)}, bf16[384,384]{1,0:T(8,128)(2,1)S(1)}) custom-call(bf16[1,1,2,384,384]{4,3,2,1,0:T(8,128)(2,1)} %green_ref.1), custom_call_target="tpu_custom_call" | custom-call | tf_op jit(solution)/shard_map/pallas_call | solution.py:137
  1.1 0.0 copy-start.2
  1.2 3.0 %collective-permute-start = (bf16[384,384]{1,0:T(8,128)(2,1)S(1)}, bf16[384,384]{1,0:T(8,128)(2,1)S(1)}, u32[]{:S(2)}, u32[]{:S(2)}) collective-permute-start(bf16[384,384]{1,0:T(8,128)(2,1)S(1)} %get-tuple-element.10.real_ref), channel_id=1, source_target_pairs={{0,1},{1,2},{2,3},{3,7},{4,0},{5,4},{6,5},{7,6},{8,9},{9,10},{10,1... | collective-permute-start | bytes 884744 | tf_op jit(solution)/shard_map/ppermute | solution.py:156
  4.2 0.0 collective-permute-start.1
  4.2 1.8 %collective-permute-start.2 = (bf16[384,384]{1,0:T(8,128)(2,1)S(1)}, bf16[384,384]{1,0:T(8,128)(2,1)S(1)}, u32[]{:S(2)}, u32[]{:S(2)}) collective-permute-start(bf16[384,384]{1,0:T(8,128)(2,1)S(1)} %get-tuple-element.14), channel_id=1, source_target_pairs={{28,0},{16,4},{20,8},{24,12},{4,16},{8,20},{12,24},{0,28},{29,1},{... | collective-permute-start | bytes 884744 | tf_op jit(solution)/shard_map/ppermute | solution.py:146
  6.0 2.9 %collective-permute-start.3 = (bf16[384,384]{1,0:T(8,128)(2,1)S(1)}, bf16[384,384]{1,0:T(8,128)(2,1)S(1)}, u32[]{:S(2)}, u32[]{:S(2)}) collective-permute-start(bf16[384,384]{1,0:T(8,128)(2,1)S(1)} %get-tuple-element.14), channel_id=1, source_target_pairs={{12,0},{0,12},{28,16},{16,28},{13,1},{1,13},{29,17},{17,29},{14,2}... | collective-permute-start | bytes 884744 | tf_op jit(solution)/shard_map/ppermute | solution.py:146
  8.8 0.0 copy-done.1
  8.8 0.0 copy-done.2
  8.9 1.6 %shard_map.47 = (f32[2,8,384]{2,1,0:T(8,128)S(1)}, f32[384,384]{1,0:T(8,128)S(1)}, f32[384,384]{1,0:T(8,128)S(1)}) custom-call(s32[1,2,2]{2,1,0:T(2,128)S(1)} %copy-done.2, bf16[384,384]{1,0:T(8,128)(2,1)S(1)} %get-tuple-element.10.real_ref, bf16[2,384,384]{2,1,0:T(8,128)(2,1)S(1)} %copy-done.1), custom_call_target="tpu_custom_call" | custom-call | flops 452984832 | bytes 1048576 | tf_op jit(solution)/shard_map/pallas_call | solution.py:109
  10.4 0.0 copy-start
  10.4 0.1 collective-permute-done.one_ref
  10.5 0.7 %collective-permute-done.1.two_ref = bf16[384,384]{1,0:T(8,128)(2,1)S(1)} collective-permute-done((bf16[384,384]{1,0:T(8,128)(2,1)S(1)}, bf16[384,384]{1,0:T(8,128)(2,1)S(1)}, u32[]{:S(2)}, u32[]{:S(2)}) %collective-permute-start.1) | collective-permute-done | bytes 294944 | tf_op jit(solution)/shard_map/ppermute | solution.py:156
  11.2 0.3 %copy-done = bf16[2,384,384]{2,1,0:T(8,128)(2,1)S(1)} copy-done((bf16[2,384,384]{2,1,0:T(8,128)(2,1)S(1)}, bf16[2,384,384]{2,1,0:T(8,128)(2,1)}, u32[]{:S(2)}) %copy-start) | copy-done | bytes 589848
  11.5 0.6 %shard_map.49.after_ref = bf16[384,384]{1,0:T(8,128)(2,1)S(1)} custom-call(bf16[384,384]{1,0:T(8,128)(2,1)S(1)} %shard_map.48.held_ref, bf16[384,384]{1,0:T(8,128)(2,1)S(1)} %collective-permute-done.1.two_ref, bf16[2,384,384]{2,1,0:T(8,128)(2,1)S(1)} %copy-done, f32[2,8,384]{2,1,0:T(8,128)S(1)} %get-tuple-element.11.after_ref.factor_ref, ...), custom_call_target="tpu_custom_call" | custom-call | flops 226492416 | bytes 1048576 | tf_op jit(solution)/shard_map/pallas_call | solution.py:109
  12.1 0.4 %collective-permute-start.6 = (bf16[384,384]{1,0:T(8,128)(2,1)S(1)}, bf16[384,384]{1,0:T(8,128)(2,1)S(1)}, u32[]{:S(2)}, u32[]{:S(2)}) collective-permute-start(bf16[384,384]{1,0:T(8,128)(2,1)S(1)} %shard_map.49.after_ref), channel_id=1, source_target_pairs={{28,0},{16,4},{20,8},{24,12},{4,16},{8,20},{12,24},{0,28},{29,1},{... | collective-permute-start | bytes 884744 | tf_op jit(solution)/shard_map/ppermute | solution.py:146
  12.6 0.6 %shard_map.50.after_ref = bf16[384,384]{1,0:T(8,128)(2,1)S(1)} custom-call(bf16[384,384]{1,0:T(8,128)(2,1)S(1)} %shard_map.48.held_ref, bf16[384,384]{1,0:T(8,128)(2,1)S(1)} %collective-permute-done.1.two_ref, bf16[2,384,384]{2,1,0:T(8,128)(2,1)S(1)} %copy-done, bf16[384,384]{1,0:T(8,128)(2,1)S(1)} %shard_map.49.after_ref, ...), custom_call_target="tpu_custom_call" | custom-call | flops 226492416 | bytes 1048576 | tf_op jit(solution)/shard_map/pallas_call | solution.py:109
  13.2 1.2 %collective-permute-start.7 = (bf16[384,384]{1,0:T(8,128)(2,1)S(1)}, bf16[384,384]{1,0:T(8,128)(2,1)S(1)}, u32[]{:S(2)}, u32[]{:S(2)}) collective-permute-start(bf16[384,384]{1,0:T(8,128)(2,1)S(1)} %shard_map.50.after_ref), channel_id=1, source_target_pairs={{0,4},{4,0},{8,12},{12,8},{16,20},{20,16},{24,28},{28,24},{1,5},{5... | collective-permute-start | bytes 884744 | tf_op jit(solution)/shard_map/ppermute | solution.py:151
  14.4 0.0 collective-permute-done.2.got_ref.refs_0_
  14.5 0.0 collective-permute-done.3.refs_0_.refs_1_
  14.5 0.1 shard_map.52.after_ref
  14.6 2.9 %collective-permute-start.5 = (bf16[384,384]{1,0:T(8,128)(2,1)S(1)}, bf16[384,384]{1,0:T(8,128)(2,1)S(1)}, u32[]{:S(2)}, u32[]{:S(2)}) collective-permute-start(bf16[384,384]{1,0:T(8,128)(2,1)S(1)} %shard_map.52.after_ref), channel_id=1, source_target_pairs={{0,1},{1,2},{2,3},{3,7},{4,0},{5,4},{6,5},{7,6},{8,9},{9,10},{10,1... | collective-permute-start | bytes 884744 | tf_op jit(solution)/shard_map/ppermute | solution.py:156
  17.5 0.0 collective-permute-start.4
  17.5 0.0 collective-permute-done.7
  17.5 0.0 collective-permute-start.8
  17.5 1.3 %shard_map.53.own_ref = f32[384,384]{1,0:T(8,128)S(1)} custom-call(f32[2,8,384]{2,1,0:T(8,128)S(1)} %get-tuple-element.11.after_ref.factor_ref, bf16[2,384,384]{2,1,0:T(8,128)(2,1)S(1)} %copy-done.1, bf16[384,384]{1,0:T(8,128)(2,1)S(1)} %shard_map.52.after_ref, bf16[384,384]{1,0:T(8,128)(2,1)S(1)} %collective-permute-done.2.got_ref.refs_0_, ...), custom_call_target="tpu_custom_call" | custom-call | flops 452984832 | bytes 1048576 | tf_op jit(solution)/shard_map/pallas_call | solution.py:109
  18.8 0.5 %collective-permute-done.6.got_ref = bf16[384,384]{1,0:T(8,128)(2,1)S(1)} collective-permute-done((bf16[384,384]{1,0:T(8,128)(2,1)S(1)}, bf16[384,384]{1,0:T(8,128)(2,1)S(1)}, u32[]{:S(2)}, u32[]{:S(2)}) %collective-permute-start.6) | collective-permute-done | bytes 294944 | tf_op jit(solution)/shard_map/ppermute | solution.py:146
  19.4 4.1 %collective-permute-done.5.term_ref = bf16[384,384]{1,0:T(8,128)(2,1)S(1)} collective-permute-done((bf16[384,384]{1,0:T(8,128)(2,1)S(1)}, bf16[384,384]{1,0:T(8,128)(2,1)S(1)}, u32[]{:S(2)}, u32[]{:S(2)}) %collective-permute-start.5) | collective-permute-done | bytes 294944 | tf_op jit(solution)/shard_map/ppermute | solution.py:156
  23.5 0.8 %collective-permute-done.4.term_ref = bf16[384,384]{1,0:T(8,128)(2,1)S(1)} collective-permute-done((bf16[384,384]{1,0:T(8,128)(2,1)S(1)}, bf16[384,384]{1,0:T(8,128)(2,1)S(1)}, u32[]{:S(2)}, u32[]{:S(2)}) %collective-permute-start.4) | collective-permute-done | bytes 294944 | tf_op jit(solution)/shard_map/ppermute | solution.py:156
  24.2 0.1 shard_map.56.imag_ref
  24.3 0.0 collective-permute-done.8.refs_0_
  24.3 0.8 %shard_map.57 = bf16[1,1,2,384,384]{4,3,2,1,0:T(8,128)(2,1)} custom-call(f32[2,8,384]{2,1,0:T(8,128)S(1)} %get-tuple-element.11.after_ref.factor_ref, bf16[384,384]{1,0:T(8,128)(2,1)S(1)} %shard_map.56.imag_ref, f32[384,384]{1,0:T(8,128)S(1)} %shard_map.54.source_ref.real_ref, bf16[384,384]{1,0:T(8,128)(2,1)S(1)} %collective-permute-done.8.refs_0_), custom_call_target="tpu_custom_call" | custom-call | tf_op jit(solution)/shard_map/pallas_call | solution.py:330
  (4 shorter events, 0.1 us)
Async XLA Ops:
  0.0 8.8 %copy-start.1 = (bf16[2,384,384]{2,1,0:T(8,128)(2,1)S(1)}, bf16[2,384,384]{2,1,0:T(8,128)(2,1)}, u32[]{:S(2)}) copy-start(bf16[2,384,384]{2,1,0:T(8,128)(2,1)} %cm_ref.3) | copy-start | bytes 1769476
  1.1 7.7 %copy-start.2 = (s32[1,2,2]{2,1,0:T(2,128)S(1)}, s32[1,2,2]{2,1,0:T(2,128)}, u32[]{:S(2)}) copy-start(s32[1,2,2]{2,1,0:T(2,128)} %weights_ref.1) | copy-start | bytes 52
  1.2 9.3 %collective-permute-start = (bf16[384,384]{1,0:T(8,128)(2,1)S(1)}, bf16[384,384]{1,0:T(8,128)(2,1)S(1)}, u32[]{:S(2)}, u32[]{:S(2)}) collective-permute-start(bf16[384,384]{1,0:T(8,128)(2,1)S(1)} %get-tuple-element.10.real_ref), channel_id=1, source_target_pairs={{0,1},{1,2},{2,3},{3,7},{4,0},{5,4},{6,5},{7,6},{8,9},{9,10},{10,1... | collective-permute-start | bytes 884744 | tf_op jit(solution)/shard_map/ppermute | solution.py:156
  4.2 7.0 %collective-permute-start.1 = (bf16[384,384]{1,0:T(8,128)(2,1)S(1)}, bf16[384,384]{1,0:T(8,128)(2,1)S(1)}, u32[]{:S(2)}, u32[]{:S(2)}) collective-permute-start(bf16[384,384]{1,0:T(8,128)(2,1)S(1)} %get-tuple-element.10.real_ref), channel_id=1, source_target_pairs={{0,4},{1,0},{2,1},{3,2},{4,5},{5,6},{6,7},{7,3},{8,12},{9,8},{10,9... | collective-permute-start | bytes 884744 | tf_op jit(solution)/shard_map/ppermute | solution.py:156
  4.2 10.2 %collective-permute-start.2 = (bf16[384,384]{1,0:T(8,128)(2,1)S(1)}, bf16[384,384]{1,0:T(8,128)(2,1)S(1)}, u32[]{:S(2)}, u32[]{:S(2)}) collective-permute-start(bf16[384,384]{1,0:T(8,128)(2,1)S(1)} %get-tuple-element.14), channel_id=1, source_target_pairs={{28,0},{16,4},{20,8},{24,12},{4,16},{8,20},{12,24},{0,28},{29,1},{... | collective-permute-start | bytes 884744 | tf_op jit(solution)/shard_map/ppermute | solution.py:146
  6.0 8.5 %collective-permute-start.3 = (bf16[384,384]{1,0:T(8,128)(2,1)S(1)}, bf16[384,384]{1,0:T(8,128)(2,1)S(1)}, u32[]{:S(2)}, u32[]{:S(2)}) collective-permute-start(bf16[384,384]{1,0:T(8,128)(2,1)S(1)} %get-tuple-element.14), channel_id=1, source_target_pairs={{12,0},{0,12},{28,16},{16,28},{13,1},{1,13},{29,17},{17,29},{14,2}... | collective-permute-start | bytes 884744 | tf_op jit(solution)/shard_map/ppermute | solution.py:146
  10.4 1.1 %copy-start = (bf16[2,384,384]{2,1,0:T(8,128)(2,1)S(1)}, bf16[2,384,384]{2,1,0:T(8,128)(2,1)}, u32[]{:S(2)}) copy-start(bf16[2,384,384]{2,1,0:T(8,128)(2,1)} %cn_ref.7) | copy-start | bytes 1769476
  12.1 7.2 %collective-permute-start.6 = (bf16[384,384]{1,0:T(8,128)(2,1)S(1)}, bf16[384,384]{1,0:T(8,128)(2,1)S(1)}, u32[]{:S(2)}, u32[]{:S(2)}) collective-permute-start(bf16[384,384]{1,0:T(8,128)(2,1)S(1)} %shard_map.49.after_ref), channel_id=1, source_target_pairs={{28,0},{16,4},{20,8},{24,12},{4,16},{8,20},{12,24},{0,28},{29,1},{... | collective-permute-start | bytes 884744 | tf_op jit(solution)/shard_map/ppermute | solution.py:146
  13.2 4.3 %collective-permute-start.7 = (bf16[384,384]{1,0:T(8,128)(2,1)S(1)}, bf16[384,384]{1,0:T(8,128)(2,1)S(1)}, u32[]{:S(2)}, u32[]{:S(2)}) collective-permute-start(bf16[384,384]{1,0:T(8,128)(2,1)S(1)} %shard_map.50.after_ref), channel_id=1, source_target_pairs={{0,4},{4,0},{8,12},{12,8},{16,20},{20,16},{24,28},{28,24},{1,5},{5... | collective-permute-start | bytes 884744 | tf_op jit(solution)/shard_map/ppermute | solution.py:151
  14.6 8.9 %collective-permute-start.5 = (bf16[384,384]{1,0:T(8,128)(2,1)S(1)}, bf16[384,384]{1,0:T(8,128)(2,1)S(1)}, u32[]{:S(2)}, u32[]{:S(2)}) collective-permute-start(bf16[384,384]{1,0:T(8,128)(2,1)S(1)} %shard_map.52.after_ref), channel_id=1, source_target_pairs={{0,1},{1,2},{2,3},{3,7},{4,0},{5,4},{6,5},{7,6},{8,9},{9,10},{10,1... | collective-permute-start | bytes 884744 | tf_op jit(solution)/shard_map/ppermute | solution.py:156
  17.5 6.7 %collective-permute-start.4 = (bf16[384,384]{1,0:T(8,128)(2,1)S(1)}, bf16[384,384]{1,0:T(8,128)(2,1)S(1)}, u32[]{:S(2)}, u32[]{:S(2)}) collective-permute-start(bf16[384,384]{1,0:T(8,128)(2,1)S(1)} %shard_map.52.after_ref), channel_id=1, source_target_pairs={{0,4},{1,0},{2,1},{3,2},{4,5},{5,6},{6,7},{7,3},{8,12},{9,8},{10,9... | collective-permute-start | bytes 884744 | tf_op jit(solution)/shard_map/ppermute | solution.py:156
  17.5 6.8 %collective-permute-start.8 = (bf16[384,384]{1,0:T(8,128)(2,1)S(1)}, bf16[384,384]{1,0:T(8,128)(2,1)S(1)}, u32[]{:S(2)}, u32[]{:S(2)}) collective-permute-start(bf16[384,384]{1,0:T(8,128)(2,1)S(1)} %collective-permute-done.7), channel_id=1, source_target_pairs={{8,0},{4,12},{24,16},{20,28},{0,4},{12,8},{16,20},{28,24},{9,1},{5... | collective-permute-start | bytes 884744 | tf_op jit(solution)/shard_map/ppermute | solution.py:153

commit v5 on v4

--- a/solution.py
+++ b/solution.py
@@ -161,22 +161,28 @@
     near = [along(imag, step) for step in plan]
     behind = from_next(real)
 
-    def first(weights_ref, real_ref, cm_ref, factor_ref, *outs):
+    def first(weights_ref, real_ref, cm_ref, cn_ref, factor_ref, near_ref, *rest):
+        outs, sem = rest[:-1], rest[-1]
+        copy = pltpu.make_async_copy(cn_ref, near_ref, sem)
+        copy.start()
         for r, out in enumerate(outs):
             mode, side, present = arriving(route[r])
             factor = jnp.where(present, weights_ref[0, mode, side], 0).astype(F32) / 32.0
             factor_ref[r] = jnp.full((8, size), factor, F32)
             out[...] = couple(cm_ref[sent_mode(r)], real_ref[...])
-
-    factors, *partial = call(
+        copy.wait()
+
+    factors, coupling_n, *partial = call(
         first,
-        [SM, VM, VM],
-        [pltpu.VMEM((rounds, 8, size), F32)] + [wide] * rounds,
+        [SM, VM, VM, ANY],
+        [pltpu.VMEM((rounds, 8, size), F32), pltpu.VMEM(coupling_n.shape, BF16)] + [wide] * rounds,
         2 * rounds,
         size,
         weights,
         real,
         coupling_m,
+        pltpu.with_memory_space_constraint(coupling_n, pltpu.HBM),
+        scratch=[pltpu.SemaphoreType.DMA],
     )
 
     def scaled(ref, factor_ref, r):
@@ -185,51 +191,82 @@
     def is_kind(k):
         return lax.axis_index("energy") % 2 == KINDS[k]
 
-    def hold(one_ref, after_ref, out_ref):
+    def own_result(r):
+        sources = {source: mode for source, mode, _ in plan[r].values()}
+        return lookup([int(e in sources and sources[e] != route[0][1][e]) for e in range(count)], lax.axis_index("energy"))
+
+    def result(r, partial_ref, behind_ref, cn_ref, out_ref):
+        here = lax.axis_index("slab") < slabs - 1
+
+        @pl.when(here)
+        def _():
+            out_ref[...] = (partial_ref[...] + couple(cn_ref[sent_mode(r)], behind_ref[...])).astype(BF16)
+
+        @pl.when(jnp.logical_not(here))
+        def _():
+            out_ref[...] = partial_ref[...].astype(BF16)
+
+    def later_result(r, partial_ref, behind_ref, cn_ref, first_ref, out_ref):
+        again = own_result(r) == 0
+
+        @pl.when(again)
+        def _():
+            out_ref[...] = first_ref[...]
+
+        @pl.when(jnp.logical_not(again))
+        def _():
+            result(r, partial_ref, behind_ref, cn_ref, out_ref)
+
+    def early(behind_ref, cn_ref, *refs):
+        parts, outs = refs[:rounds], refs[rounds:]
+
         @pl.when(is_kind(0))
         def _():
-            out_ref[...] = one_ref[...]
-
-    (held,) = call(hold, [VM, ANY], [block], 2, size, behind[0], factors)
-
-    def whole(rs, after):
-        def kernel(held_ref, two_ref, cn_ref, after_ref, *refs):
-            parts, outs, next_ref = refs[: len(rs)], refs[len(rs) : -1], refs[-1]
-            here = lax.axis_index("slab") < slabs - 1
-            for k, ref in enumerate((held_ref, two_ref)):
-
-                @pl.when(here & is_kind(k))
-                def _():
-                    next_ref[...] = ref[...]
-
-            for r, part, out in zip(rs, parts, outs):
-
-                @pl.when(here)
-                def _():
-                    out[...] = (part[...] + couple(cn_ref[sent_mode(r)], next_ref[...])).astype(BF16)
-
-                @pl.when(jnp.logical_not(here))
-                def _():
-                    out[...] = part[...].astype(BF16)
-
-        return call(
-            kernel,
-            [VM, VM, VM, ANY] + [VM] * len(rs),
-            [block] * len(rs),
-            2 * len(rs),
-            size,
-            held,
-            behind[1],
-            coupling_n,
-            after,
-            *[partial[r] for r in rs],
-            scratch=[block],
+            result(0, parts[0], behind_ref, cn_ref, outs[0])
+            for r in range(1, rounds):
+                later_result(r, parts[r], behind_ref, cn_ref, outs[0], outs[r])
+
+    ready = call(early, [VM] * (2 + rounds), [block] * rounds, 2, size, behind[0], coupling_n, *partial)
+
+    def late(behind_ref, cn_ref, partial_ref, ready_ref, out_ref):
+        @pl.when(is_kind(0))
+        def _():
+            out_ref[...] = ready_ref[...]
+
+        @pl.when(is_kind(1))
+        def _():
+            result(0, partial_ref, behind_ref, cn_ref, out_ref)
+
+    results = call(late, [VM] * 4, [block], 2, size, behind[1], coupling_n, partial[0], ready[0])
+    arrived = [along(results[0], plan[0])]
+
+    def late_rest(behind_ref, cn_ref, first_ref, *refs):
+        for r in range(1, rounds):
+            part, done, out = (refs[r - 1 + k * (rounds - 1)] for k in range(3))
+
+            @pl.when(is_kind(0))
+            def _():
+                out[...] = done[...]
+
+            @pl.when(is_kind(1))
+            def _():
+                later_result(r, part, behind_ref, cn_ref, first_ref, out)
+
+    if rounds > 1:
+        results = list(results) + list(
+            call(
+                late_rest,
+                [VM] * (3 + 2 * (rounds - 1)),
+                [block] * (rounds - 1),
+                2,
+                size,
+                behind[1],
+                coupling_n,
+                results[0],
+                *partial[1:],
+                *ready[1:],
+            )
         )
-
-    results = whole([0], factors)
-    arrived = [along(results[0], plan[0])]
-    if rounds > 1:
-        results = results + whole(list(range(1, rounds)), results[0])
         arrived += [along_closed(results[r], plan[r]) for r in range(1, rounds)]
 
     def term_first(factor_ref, cn_ref, got_ref, after_ref, out_ref):

time: 25.4 us -> 24.7 us (0.972)
  starting transfers between devices: 12.3 us -> 11.4 us
  waiting for transfers between devices: 6.17 us -> 6.62 us
  local copies, waits for them, and re-layouts: 0.29 us -> 0.01 us
    ppermute x3, waiting for transfers between devices: 0.53 us -> 1.43 us  [along(): return lax.ppermute(x, 'energy', [(s, t) for t, (s, _, _) in step.items()])]
    ppermute x4, starting transfers between devices: 5.99 us -> 5.46 us  [from_next(): lax.ppermute(x, ('energy', 'slab'), descent(count, slabs, kind))]
    ppermute x4, waiting for transfers between devices: 5.63 us -> 5.19 us  [from_next(): lax.ppermute(x, ('energy', 'slab'), descent(count, slabs, kind))]
    unnamed x6 -> x4, local copies, waits for them, and re-layouts: 0.29 us -> 0.01 us
  transfers between devices with their start and end apart: 9 -> 9, of which waited for: 5 -> 5; matrix products, arithmetic and copies ran while one was open for 0% -> 0% of each run, Pallas kernels for 17% -> 18%
where the time goes in v5:
time: 24.7 us; the launch traced here: 24.5 us
  starting transfers between devices  11.4 us (46%)
  waiting for transfers between devices  6.62 us (27%)
  Pallas kernels  6.35 us (26%)
    ppermute x4, starting transfers between devices, from_next(): lax.ppermute(x, ('energy', 'slab'), descent(count, slabs, kind))  5.46 us
    ppermute x4, waiting for transfers between devices, from_next(): lax.ppermute(x, ('energy', 'slab'), descent(count, slabs, kind))  5.19 us
    ppermute x3, starting transfers between devices, along(): return lax.ppermute(x, 'energy', [(s, t) for t, (s, _, _) in step.items()])  4.92 us
    pallas_call x10, Pallas kernels, call(): pl.pallas_call(kernel, out_shape=outs, in_specs=ins, out_specs=[VM] * len...  4.39 us
    ppermute x3, waiting for transfers between devices, along(): return lax.ppermute(x, 'energy', [(s, t) for t, (s, _, _) in step.items()])  1.43 us
    pallas_call x1, Pallas kernels, body(): pl.pallas_call(split, out_shape=[block, block], in_specs=[ANY], out_specs...  1.13 us
    ppermute x1, starting transfers between devices, along_closed(): swapped = lax.ppermute(x, 'energy', [(e, e ^ 1) for e in range(count)])  1.04 us
    pallas_call x1, Pallas kernels, body(): pl.pallas_call(finish, out_shape=jax.ShapeDtypeStruct(green.shape, BF16),...  0.83 us
  transfers between devices with their start and end apart: 9, of which 5 were waited for; matrix products, arithmetic and copies ran while one was open for 0% of the time, Pallas kernels for 18%

profile of v5, /device:TPU:0, one launch (start us, length us, event | category | flops | bytes accessed | tf_op | source)
XLA Modules:
  0.0 24.5 jit_solution(9155889486231244303)
XLA Ops:
  0.0 0.0 copy-start
  0.0 1.1 %shard_map.46 = (bf16[384,384]{1,0:T(8,128)(2,1)S(1)}, bf16[384,384]{1,0:T(8,128)(2,1)S(1)}) custom-call(bf16[1,1,2,384,384]{4,3,2,1,0:T(8,128)(2,1)} %green_ref.1), custom_call_target="tpu_custom_call" | custom-call | tf_op jit(solution)/shard_map/pallas_call | solution.py:137
  1.1 0.0 copy-start.1
  1.2 3.0 %collective-permute-start.1 = (bf16[384,384]{1,0:T(8,128)(2,1)S(1)}, bf16[384,384]{1,0:T(8,128)(2,1)S(1)}, u32[]{:S(2)}, u32[]{:S(2)}) collective-permute-start(bf16[384,384]{1,0:T(8,128)(2,1)S(1)} %get-tuple-element.13.real_ref), channel_id=1, source_target_pairs={{0,1},{1,2},{2,3},{3,7},{4,0},{5,4},{6,5},{7,6},{8,9},{9,10},{10,1... | collective-permute-start | bytes 884744 | tf_op jit(solution)/shard_map/ppermute | solution.py:156
  4.2 0.0 collective-permute-start
  4.2 1.8 %collective-permute-start.2 = (bf16[384,384]{1,0:T(8,128)(2,1)S(1)}, bf16[384,384]{1,0:T(8,128)(2,1)S(1)}, u32[]{:S(2)}, u32[]{:S(2)}) collective-permute-start(bf16[384,384]{1,0:T(8,128)(2,1)S(1)} %get-tuple-element.20), channel_id=1, source_target_pairs={{28,0},{16,4},{20,8},{24,12},{4,16},{8,20},{12,24},{0,28},{29,1},{... | collective-permute-start | bytes 884744 | tf_op jit(solution)/shard_map/ppermute | solution.py:146
  6.0 2.9 %collective-permute-start.3 = (bf16[384,384]{1,0:T(8,128)(2,1)S(1)}, bf16[384,384]{1,0:T(8,128)(2,1)S(1)}, u32[]{:S(2)}, u32[]{:S(2)}) collective-permute-start(bf16[384,384]{1,0:T(8,128)(2,1)S(1)} %get-tuple-element.20), channel_id=1, source_target_pairs={{12,0},{0,12},{28,16},{16,28},{13,1},{1,13},{29,17},{17,29},{14,2}... | collective-permute-start | bytes 884744 | tf_op jit(solution)/shard_map/ppermute | solution.py:146
  8.8 0.0 copy-done
  8.8 0.0 copy-done.1
  8.9 1.7 %shard_map.47 = (f32[2,8,384]{2,1,0:T(8,128)S(1)}, bf16[2,384,384]{2,1,0:T(8,128)(2,1)S(1)}, f32[384,384]{1,0:T(8,128)S(1)}, f32[384,384]{1,0:T(8,128)S(1)}) custom-call(s32[1,2,2]{2,1,0:T(2,128)S(1)} %copy-done.1, bf16[384,384]{1,0:T(8,128)(2,1)S(1)} %get-tuple-element.13.real_ref, bf16[2,384,384]{2,1,0:T(8,128)(2,1)S(1)} %copy-done, ...), custom_call_target="tpu_custom_call" | custom-call | flops 452984832 | bytes 1048576 | tf_op jit(solution)/shard_map/pallas_call | solution.py:109
  10.5 0.0 collective-permute-done.1.behind_ref
  10.6 0.6 %collective-permute-done.behind_ref = bf16[384,384]{1,0:T(8,128)(2,1)S(1)} collective-permute-done((bf16[384,384]{1,0:T(8,128)(2,1)S(1)}, bf16[384,384]{1,0:T(8,128)(2,1)S(1)}, u32[]{:S(2)}, u32[]{:S(2)}) %collective-permute-start) | collective-permute-done | bytes 294944 | tf_op jit(solution)/shard_map/ppermute | solution.py:156
  11.2 0.6 %shard_map.49.first_ref = bf16[384,384]{1,0:T(8,128)(2,1)S(1)} custom-call(bf16[384,384]{1,0:T(8,128)(2,1)S(1)} %collective-permute-done.behind_ref, bf16[2,384,384]{2,1,0:T(8,128)(2,1)S(1)} %get-tuple-element.15.cn_ref, f32[384,384]{1,0:T(8,128)S(1)} %get-tuple-element.16.refs_0_.partial_ref, bf16[384,384]{1,0:T(8,128)(2,1)S(1)} %get-tuple-element.18.ready_ref), custom_call_target="tpu_custom_call" | custom-call | flops 226492416 | bytes 1048576 | tf_op jit(solution)/shard_map/pallas_call | solution.py:109
  11.8 0.3 %collective-permute-start.6 = (bf16[384,384]{1,0:T(8,128)(2,1)S(1)}, bf16[384,384]{1,0:T(8,128)(2,1)S(1)}, u32[]{:S(2)}, u32[]{:S(2)}) collective-permute-start(bf16[384,384]{1,0:T(8,128)(2,1)S(1)} %shard_map.49.first_ref), channel_id=1, source_target_pairs={{28,0},{16,4},{20,8},{24,12},{4,16},{8,20},{12,24},{0,28},{29,1},{... | collective-permute-start | bytes 884744 | tf_op jit(solution)/shard_map/ppermute | solution.py:146
  12.1 0.6 %shard_map.50.after_ref = bf16[384,384]{1,0:T(8,128)(2,1)S(1)} custom-call(bf16[384,384]{1,0:T(8,128)(2,1)S(1)} %collective-permute-done.behind_ref, bf16[2,384,384]{2,1,0:T(8,128)(2,1)S(1)} %get-tuple-element.15.cn_ref, bf16[384,384]{1,0:T(8,128)(2,1)S(1)} %shard_map.49.first_ref, f32[384,384]{1,0:T(8,128)S(1)} %get-tuple-element.17.refs_1_.refs_0_, ...), custom_call_target="tpu_custom_call" | custom-call | flops 226492416 | bytes 1048576 | tf_op jit(solution)/shard_map/pallas_call | solution.py:109
  12.7 1.0 %collective-permute-start.7 = (bf16[384,384]{1,0:T(8,128)(2,1)S(1)}, bf16[384,384]{1,0:T(8,128)(2,1)S(1)}, u32[]{:S(2)}, u32[]{:S(2)}) collective-permute-start(bf16[384,384]{1,0:T(8,128)(2,1)S(1)} %shard_map.50.after_ref), channel_id=1, source_target_pairs={{0,4},{4,0},{8,12},{12,8},{16,20},{20,16},{24,28},{28,24},{1,5},{5... | collective-permute-start | bytes 884744 | tf_op jit(solution)/shard_map/ppermute | solution.py:151
  13.8 0.0 collective-permute-done.2.got_ref.refs_0_
  13.8 0.6 %collective-permute-done.3.refs_0_.refs_1_ = bf16[384,384]{1,0:T(8,128)(2,1)S(1)} collective-permute-done((bf16[384,384]{1,0:T(8,128)(2,1)S(1)}, bf16[384,384]{1,0:T(8,128)(2,1)S(1)}, u32[]{:S(2)}, u32[]{:S(2)}) %collective-permute-start.3) | collective-permute-done | bytes 294944 | tf_op jit(solution)/shard_map/ppermute | solution.py:146
  14.4 0.1 shard_map.52.after_ref
  14.5 2.4 %collective-permute-start.5 = (bf16[384,384]{1,0:T(8,128)(2,1)S(1)}, bf16[384,384]{1,0:T(8,128)(2,1)S(1)}, u32[]{:S(2)}, u32[]{:S(2)}) collective-permute-start(bf16[384,384]{1,0:T(8,128)(2,1)S(1)} %shard_map.52.after_ref), channel_id=1, source_target_pairs={{0,1},{1,2},{2,3},{3,7},{4,0},{5,4},{6,5},{7,6},{8,9},{9,10},{10,1... | collective-permute-start | bytes 884744 | tf_op jit(solution)/shard_map/ppermute | solution.py:156
  16.9 0.0 collective-permute-start.4
  16.9 0.0 collective-permute-done.7
  16.9 0.0 collective-permute-start.8
  16.9 1.3 %shard_map.53.own_ref = f32[384,384]{1,0:T(8,128)S(1)} custom-call(f32[2,8,384]{2,1,0:T(8,128)S(1)} %get-tuple-element.14.factor_ref, bf16[2,384,384]{2,1,0:T(8,128)(2,1)S(1)} %copy-done, bf16[384,384]{1,0:T(8,128)(2,1)S(1)} %shard_map.52.after_ref, bf16[384,384]{1,0:T(8,128)(2,1)S(1)} %collective-permute-done.2.got_ref.refs_0_, ...), custom_call_target="tpu_custom_call" | custom-call | flops 452984832 | bytes 1048576 | tf_op jit(solution)/shard_map/pallas_call | solution.py:109
  18.2 0.9 %collective-permute-done.6.got_ref = bf16[384,384]{1,0:T(8,128)(2,1)S(1)} collective-permute-done((bf16[384,384]{1,0:T(8,128)(2,1)S(1)}, bf16[384,384]{1,0:T(8,128)(2,1)S(1)}, u32[]{:S(2)}, u32[]{:S(2)}) %collective-permute-start.6) | collective-permute-done | bytes 294944 | tf_op jit(solution)/shard_map/ppermute | solution.py:146
  19.1 3.8 %collective-permute-done.5.term_ref = bf16[384,384]{1,0:T(8,128)(2,1)S(1)} collective-permute-done((bf16[384,384]{1,0:T(8,128)(2,1)S(1)}, bf16[384,384]{1,0:T(8,128)(2,1)S(1)}, u32[]{:S(2)}, u32[]{:S(2)}) %collective-permute-start.5) | collective-permute-done | bytes 294944 | tf_op jit(solution)/shard_map/ppermute | solution.py:156
  22.9 0.7 %collective-permute-done.4.term_ref = bf16[384,384]{1,0:T(8,128)(2,1)S(1)} collective-permute-done((bf16[384,384]{1,0:T(8,128)(2,1)S(1)}, bf16[384,384]{1,0:T(8,128)(2,1)S(1)}, u32[]{:S(2)}, u32[]{:S(2)}) %collective-permute-start.4) | collective-permute-done | bytes 294944 | tf_op jit(solution)/shard_map/ppermute | solution.py:156
  23.6 0.1 shard_map.56.imag_ref
  23.7 0.0 collective-permute-done.8.refs_0_
  23.7 0.8 %shard_map.57 = bf16[1,1,2,384,384]{4,3,2,1,0:T(8,128)(2,1)} custom-call(f32[2,8,384]{2,1,0:T(8,128)S(1)} %get-tuple-element.14.factor_ref, bf16[384,384]{1,0:T(8,128)(2,1)S(1)} %shard_map.56.imag_ref, f32[384,384]{1,0:T(8,128)S(1)} %shard_map.54.source_ref.real_ref, bf16[384,384]{1,0:T(8,128)(2,1)S(1)} %collective-permute-done.8.refs_0_), custom_call_target="tpu_custom_call" | custom-call | tf_op jit(solution)/shard_map/pallas_call | solution.py:367
  (4 shorter events, 0.1 us)
Async XLA Ops:
  0.0 8.8 %copy-start = (bf16[2,384,384]{2,1,0:T(8,128)(2,1)S(1)}, bf16[2,384,384]{2,1,0:T(8,128)(2,1)}, u32[]{:S(2)}) copy-start(bf16[2,384,384]{2,1,0:T(8,128)(2,1)} %cm_ref.3) | copy-start | bytes 1769476
  1.1 7.7 %copy-start.1 = (s32[1,2,2]{2,1,0:T(2,128)S(1)}, s32[1,2,2]{2,1,0:T(2,128)}, u32[]{:S(2)}) copy-start(s32[1,2,2]{2,1,0:T(2,128)} %weights_ref.1) | copy-start | bytes 52
  1.2 9.4 %collective-permute-start.1 = (bf16[384,384]{1,0:T(8,128)(2,1)S(1)}, bf16[384,384]{1,0:T(8,128)(2,1)S(1)}, u32[]{:S(2)}, u32[]{:S(2)}) collective-permute-start(bf16[384,384]{1,0:T(8,128)(2,1)S(1)} %get-tuple-element.13.real_ref), channel_id=1, source_target_pairs={{0,1},{1,2},{2,3},{3,7},{4,0},{5,4},{6,5},{7,6},{8,9},{9,10},{10,1... | collective-permute-start | bytes 884744 | tf_op jit(solution)/shard_map/ppermute | solution.py:156
  4.2 7.0 %collective-permute-start = (bf16[384,384]{1,0:T(8,128)(2,1)S(1)}, bf16[384,384]{1,0:T(8,128)(2,1)S(1)}, u32[]{:S(2)}, u32[]{:S(2)}) collective-permute-start(bf16[384,384]{1,0:T(8,128)(2,1)S(1)} %get-tuple-element.13.real_ref), channel_id=1, source_target_pairs={{0,4},{1,0},{2,1},{3,2},{4,5},{5,6},{6,7},{7,3},{8,12},{9,8},{10,9... | collective-permute-start | bytes 884744 | tf_op jit(solution)/shard_map/ppermute | solution.py:156
  4.2 9.6 %collective-permute-start.2 = (bf16[384,384]{1,0:T(8,128)(2,1)S(1)}, bf16[384,384]{1,0:T(8,128)(2,1)S(1)}, u32[]{:S(2)}, u32[]{:S(2)}) collective-permute-start(bf16[384,384]{1,0:T(8,128)(2,1)S(1)} %get-tuple-element.20), channel_id=1, source_target_pairs={{28,0},{16,4},{20,8},{24,12},{4,16},{8,20},{12,24},{0,28},{29,1},{... | collective-permute-start | bytes 884744 | tf_op jit(solution)/shard_map/ppermute | solution.py:146
  6.0 8.4 %collective-permute-start.3 = (bf16[384,384]{1,0:T(8,128)(2,1)S(1)}, bf16[384,384]{1,0:T(8,128)(2,1)S(1)}, u32[]{:S(2)}, u32[]{:S(2)}) collective-permute-start(bf16[384,384]{1,0:T(8,128)(2,1)S(1)} %get-tuple-element.20), channel_id=1, source_target_pairs={{12,0},{0,12},{28,16},{16,28},{13,1},{1,13},{29,17},{17,29},{14,2}... | collective-permute-start | bytes 884744 | tf_op jit(solution)/shard_map/ppermute | solution.py:146
  11.8 7.2 %collective-permute-start.6 = (bf16[384,384]{1,0:T(8,128)(2,1)S(1)}, bf16[384,384]{1,0:T(8,128)(2,1)S(1)}, u32[]{:S(2)}, u32[]{:S(2)}) collective-permute-start(bf16[384,384]{1,0:T(8,128)(2,1)S(1)} %shard_map.49.first_ref), channel_id=1, source_target_pairs={{28,0},{16,4},{20,8},{24,12},{4,16},{8,20},{12,24},{0,28},{29,1},{... | collective-permute-start | bytes 884744 | tf_op jit(solution)/shard_map/ppermute | solution.py:146
  12.7 4.2 %collective-permute-start.7 = (bf16[384,384]{1,0:T(8,128)(2,1)S(1)}, bf16[384,384]{1,0:T(8,128)(2,1)S(1)}, u32[]{:S(2)}, u32[]{:S(2)}) collective-permute-start(bf16[384,384]{1,0:T(8,128)(2,1)S(1)} %shard_map.50.after_ref), channel_id=1, source_target_pairs={{0,4},{4,0},{8,12},{12,8},{16,20},{20,16},{24,28},{28,24},{1,5},{5... | collective-permute-start | bytes 884744 | tf_op jit(solution)/shard_map/ppermute | solution.py:151
  14.5 8.4 %collective-permute-start.5 = (bf16[384,384]{1,0:T(8,128)(2,1)S(1)}, bf16[384,384]{1,0:T(8,128)(2,1)S(1)}, u32[]{:S(2)}, u32[]{:S(2)}) collective-permute-start(bf16[384,384]{1,0:T(8,128)(2,1)S(1)} %shard_map.52.after_ref), channel_id=1, source_target_pairs={{0,1},{1,2},{2,3},{3,7},{4,0},{5,4},{6,5},{7,6},{8,9},{9,10},{10,1... | collective-permute-start | bytes 884744 | tf_op jit(solution)/shard_map/ppermute | solution.py:156
  16.9 6.7 %collective-permute-start.4 = (bf16[384,384]{1,0:T(8,128)(2,1)S(1)}, bf16[384,384]{1,0:T(8,128)(2,1)S(1)}, u32[]{:S(2)}, u32[]{:S(2)}) collective-permute-start(bf16[384,384]{1,0:T(8,128)(2,1)S(1)} %shard_map.52.after_ref), channel_id=1, source_target_pairs={{0,4},{1,0},{2,1},{3,2},{4,5},{5,6},{6,7},{7,3},{8,12},{9,8},{10,9... | collective-permute-start | bytes 884744 | tf_op jit(solution)/shard_map/ppermute | solution.py:156
  16.9 6.8 %collective-permute-start.8 = (bf16[384,384]{1,0:T(8,128)(2,1)S(1)}, bf16[384,384]{1,0:T(8,128)(2,1)S(1)}, u32[]{:S(2)}, u32[]{:S(2)}) collective-permute-start(bf16[384,384]{1,0:T(8,128)(2,1)S(1)} %collective-permute-done.7), channel_id=1, source_target_pairs={{8,0},{4,12},{24,16},{20,28},{0,4},{12,8},{16,20},{28,24},{9,1},{5... | collective-permute-start | bytes 884744 | tf_op jit(solution)/shard_map/ppermute | solution.py:153

commit v6 on v5

--- a/solution.py
+++ b/solution.py
@@ -269,44 +269,76 @@
         )
         arrived += [along_closed(results[r], plan[r]) for r in range(1, rounds)]
 
-    def term_first(factor_ref, cn_ref, got_ref, after_ref, out_ref):
-        mode, _, present = arriving(route[0])
+    def arrivals():
+        modes, present = zip(*[(mode, there) for mode, _, there in map(arriving, route)])
         ahead = lax.axis_index("slab") > 0
-
-        @pl.when(present & ahead)
-        def _():
-            out_ref[...] = couple(cn_ref[mode], scaled(got_ref, factor_ref, 0).astype(BF16))
-
-        @pl.when(jnp.logical_not(present & ahead))
-        def _():
-            out_ref[...] = jnp.zeros_like(out_ref)
-
-    (begun,) = call(term_first, [VM, VM, VM, ANY], [wide], 2, size, factors, coupling_n, near[0], results[-1])
-
-    def term_rest(factor_ref, cn_ref, after_ref, begun_ref, *refs):
-        got, out_ref, total_ref = refs[:-2], refs[-2], refs[-1]
-        total_ref[...] = begun_ref[...]
-        for r, ref in enumerate(got, 1):
-            mode, _, present = arriving(route[r])
-
-            @pl.when(present & (lax.axis_index("slab") > 0))
-            def _():
-                total_ref[...] += couple(cn_ref[mode], scaled(ref, factor_ref, r).astype(BF16))
+        return modes, [ahead & there for there in present]
+
+    def term_first(factor_ref, cn_ref, after_ref, got_ref, left_ref, whole_ref):
+        modes, present = arrivals()
+        follows = present[1] if rounds > 1 else False
+        mat = cn_ref[modes[0]]
+
+        @pl.when(present[0])
+        def _():
+            left_ref[...] = dot(mat, scaled(got_ref, factor_ref, 0).astype(BF16)).astype(BF16)
+
+        @pl.when(present[0] & jnp.logical_not(follows))
+        def _():
+            whole_ref[...] = dot_t(left_ref[...], mat)
+
+    left, begun = call(
+        term_first, [VM, VM, ANY, VM], [block, wide], 2, size, factors, coupling_n, results[-1], near[0]
+    )
+
+    def term_sum(factor_ref, cn_ref, left_ref, begun_ref, *refs):
+        got, out_ref, total_ref, side_ref = refs[: rounds - 1], refs[-3], refs[-2], refs[-1]
+        modes, present = arrivals()
+        follows = present[1] if rounds > 1 else jnp.bool_(False)
+
+        def left_of(r):
+            return dot(cn_ref[modes[r]], scaled(got[r - 1], factor_ref, r).astype(BF16)).astype(BF16)
+
+        @pl.when(present[0] & jnp.logical_not(follows))
+        def _():
+            total_ref[...] = begun_ref[...]
+
+        @pl.when(jnp.logical_not(present[0] | follows))
+        def _():
+            total_ref[...] = jnp.zeros_like(total_ref)
+
+        if rounds > 1:
+            @pl.when(present[0] & follows)
+            def _():
+                side_ref[:, :size] = left_ref[...]
+                side_ref[:, size:] = left_of(1)
+                mats = jnp.concatenate([cn_ref[modes[0]], cn_ref[modes[1]]], 1)
+                total_ref[...] = dot_t(side_ref[...], mats)
+
+            @pl.when(jnp.logical_not(present[0]) & follows)
+            def _():
+                total_ref[...] = dot_t(left_of(1), cn_ref[modes[1]])
+
+        for r in range(2, rounds):
+
+            @pl.when(present[r])
+            def _():
+                total_ref[...] += dot_t(left_of(r), cn_ref[modes[r]])
 
         out_ref[...] = total_ref[...].astype(BF16)
 
     (term,) = call(
-        term_rest,
-        [VM, VM, ANY, VM] + [VM] * (rounds - 1),
+        term_sum,
+        [VM] * (4 + rounds - 1),
         [block],
         LONG,
         size,
         factors,
         coupling_n,
-        results[-1],
+        left,
         begun,
         *near[1:],
-        scratch=[wide],
+        scratch=[wide, pltpu.VMEM((size, 2 * size), BF16)],
     )
     term_next = from_next(term)
 
@@ -341,37 +373,50 @@
             def _():
                 out_ref[...] = own_ref[...].astype(BF16)
 
-            if k:
-
-                @pl.when(is_kind(0))
-                def _():
-                    out_ref[...] = source_ref[...]
-
-        return call(kernel, [VM, VM, VM if k else ANY], [block], SHORT, size, own, term_next[k], source)[0]
-
-    imag_sum = imag_part(1, imag_part(0, real_sum))
-
-    def finish(factor_ref, imag_ref, real_ref, *refs):
-        got, out_ref, held_ref, sems = refs[: rounds - 1], refs[-3], refs[-2], refs[-1]
-        imag_copy = pltpu.make_async_copy(imag_ref, out_ref.at[0, 0, 1], sems.at[1])
-        imag_copy.start()
+        return call(kernel, [VM, VM, ANY], [block], SHORT, size, own, term_next[k], source)[0]
+
+    imag_sum = imag_part(0, real_sum)
+
+    def finish(factor_ref, own_ref, term_ref, imag_ref, real_ref, *refs):
+        got, out_ref, held_ref, made_ref, sems = refs[: rounds - 1], refs[-4], refs[-3], refs[-2], refs[-1]
+        last = lax.axis_index("slab") == slabs - 1
+
+        def imag_copy(ref):
+            return pltpu.make_async_copy(ref, out_ref.at[0, 0, 1], sems.at[1])
+
+        @pl.when(is_kind(0))
+        def _():
+            imag_copy(imag_ref).start()
+
+        @pl.when(is_kind(1) & jnp.logical_not(last))
+        def _():
+            made_ref[...] = (own_ref[...] + term_ref[...].astype(F32)).astype(BF16)
+
+        @pl.when(is_kind(1) & last)
+        def _():
+            made_ref[...] = own_ref[...].astype(BF16)
+
+        @pl.when(is_kind(1))
+        def _():
+            imag_copy(made_ref).start()
+
         total = real_ref[...]
         for r, ref in enumerate(got, 1):
             total += scaled(ref, factor_ref, r)
         held_ref[...] = total.astype(BF16)
         real_copy = pltpu.make_async_copy(held_ref, out_ref.at[0, 0, 0], sems.at[0])
         real_copy.start()
-        imag_copy.wait()
+        imag_copy(made_ref).wait()
         real_copy.wait()
 
     return pl.pallas_call(
         finish,
         out_shape=jax.ShapeDtypeStruct(green.shape, BF16),
-        in_specs=[VM] * (2 + rounds),
+        in_specs=[VM] * (4 + rounds),
         out_specs=ANY,
-        scratch_shapes=[block, pltpu.SemaphoreType.DMA((2,))],
+        scratch_shapes=[block, block, pltpu.SemaphoreType.DMA((2,))],
         compiler_params=pltpu.CompilerParams(vmem_limit_bytes=24 << 20),
-    )(factors, imag_sum, real_sum, *arrived[1:])
+    )(factors, own, term_next[1], imag_sum, real_sum, *arrived[1:])
 
 
 def solution(mesh):

time: 24.7 us -> 24.9 us (level)
  waiting for transfers between devices: 6.62 us -> 6.94 us
    pallas_call x10 -> x9, Pallas kernels: 4.39 us -> 4.32 us  [call(): pl.pallas_call(kernel, out_shape=outs, in_specs=ins, out_specs=[VM] * len...]
where the time goes in v6:
time: 24.9 us; the launch traced here: 24.7 us
  starting transfers between devices  11.2 us (45%)
  waiting for transfers between devices  6.94 us (28%)
  Pallas kernels  6.35 us (26%)
    ppermute x4, waiting for transfers between devices, from_next(): lax.ppermute(x, ('energy', 'slab'), descent(count, slabs, kind))  5.32 us
    ppermute x4, starting transfers between devices, from_next(): lax.ppermute(x, ('energy', 'slab'), descent(count, slabs, kind))  5.27 us
    ppermute x3, starting transfers between devices, along(): return lax.ppermute(x, 'energy', [(s, t) for t, (s, _, _) in step.items()])  4.94 us
    pallas_call x9, Pallas kernels, call(): pl.pallas_call(kernel, out_shape=outs, in_specs=ins, out_specs=[VM] * len...  4.32 us
    ppermute x3, waiting for transfers between devices, along(): return lax.ppermute(x, 'energy', [(s, t) for t, (s, _, _) in step.items()])  1.61 us
    pallas_call x1, Pallas kernels, body(): pl.pallas_call(split, out_shape=[block, block], in_specs=[ANY], out_specs...  1.13 us
    ppermute x1, starting transfers between devices, along_closed(): swapped = lax.ppermute(x, 'energy', [(e, e ^ 1) for e in range(count)])  1.03 us
    pallas_call x1, Pallas kernels, body(): pl.pallas_call(finish, out_shape=jax.ShapeDtypeStruct(green.shape, BF16),...  0.89 us
  transfers between devices with their start and end apart: 9, of which 5 were waited for; matrix products, arithmetic and copies ran while one was open for 0% of the time, Pallas kernels for 18%

profile of v6, /device:TPU:0, one launch (start us, length us, event | category | flops | bytes accessed | tf_op | source)
XLA Modules:
  0.0 24.7 jit_solution(9629083999099110787)
XLA Ops:
  0.0 0.0 copy-start
  0.0 1.1 %shard_map.46 = (bf16[384,384]{1,0:T(8,128)(2,1)S(1)}, bf16[384,384]{1,0:T(8,128)(2,1)S(1)}) custom-call(bf16[1,1,2,384,384]{4,3,2,1,0:T(8,128)(2,1)} %green_ref.1), custom_call_target="tpu_custom_call" | custom-call | tf_op jit(solution)/shard_map/pallas_call | solution.py:137
  1.1 0.0 copy-start.1
  1.2 3.0 %collective-permute-start.1 = (bf16[384,384]{1,0:T(8,128)(2,1)S(1)}, bf16[384,384]{1,0:T(8,128)(2,1)S(1)}, u32[]{:S(2)}, u32[]{:S(2)}) collective-permute-start(bf16[384,384]{1,0:T(8,128)(2,1)S(1)} %get-tuple-element.15.real_ref), channel_id=1, source_target_pairs={{0,1},{1,2},{2,3},{3,7},{4,0},{5,4},{6,5},{7,6},{8,9},{9,10},{10,1... | collective-permute-start | bytes 884744 | tf_op jit(solution)/shard_map/ppermute | solution.py:156
  4.2 0.0 collective-permute-start
  4.2 1.8 %collective-permute-start.2 = (bf16[384,384]{1,0:T(8,128)(2,1)S(1)}, bf16[384,384]{1,0:T(8,128)(2,1)S(1)}, u32[]{:S(2)}, u32[]{:S(2)}) collective-permute-start(bf16[384,384]{1,0:T(8,128)(2,1)S(1)} %get-tuple-element.22), channel_id=1, source_target_pairs={{28,0},{16,4},{20,8},{24,12},{4,16},{8,20},{12,24},{0,28},{29,1},{... | collective-permute-start | bytes 884744 | tf_op jit(solution)/shard_map/ppermute | solution.py:146
  6.0 2.9 %collective-permute-start.3 = (bf16[384,384]{1,0:T(8,128)(2,1)S(1)}, bf16[384,384]{1,0:T(8,128)(2,1)S(1)}, u32[]{:S(2)}, u32[]{:S(2)}) collective-permute-start(bf16[384,384]{1,0:T(8,128)(2,1)S(1)} %get-tuple-element.22), channel_id=1, source_target_pairs={{12,0},{0,12},{28,16},{16,28},{13,1},{1,13},{29,17},{17,29},{14,2}... | collective-permute-start | bytes 884744 | tf_op jit(solution)/shard_map/ppermute | solution.py:146
  8.8 0.0 copy-done
  8.8 0.0 copy-done.1
  8.9 1.7 %shard_map.47 = (f32[2,8,384]{2,1,0:T(8,128)S(1)}, bf16[2,384,384]{2,1,0:T(8,128)(2,1)S(1)}, f32[384,384]{1,0:T(8,128)S(1)}, f32[384,384]{1,0:T(8,128)S(1)}) custom-call(s32[1,2,2]{2,1,0:T(2,128)S(1)} %copy-done.1, bf16[384,384]{1,0:T(8,128)(2,1)S(1)} %get-tuple-element.15.real_ref, bf16[2,384,384]{2,1,0:T(8,128)(2,1)S(1)} %copy-done, ...), custom_call_target="tpu_custom_call" | custom-call | flops 452984832 | bytes 1048576 | tf_op jit(solution)/shard_map/pallas_call | solution.py:109
  10.5 0.0 collective-permute-done.1.behind_ref
  10.6 0.6 %collective-permute-done.behind_ref = bf16[384,384]{1,0:T(8,128)(2,1)S(1)} collective-permute-done((bf16[384,384]{1,0:T(8,128)(2,1)S(1)}, bf16[384,384]{1,0:T(8,128)(2,1)S(1)}, u32[]{:S(2)}, u32[]{:S(2)}) %collective-permute-start) | collective-permute-done | bytes 294944 | tf_op jit(solution)/shard_map/ppermute | solution.py:156
  11.2 0.6 %shard_map.49.first_ref = bf16[384,384]{1,0:T(8,128)(2,1)S(1)} custom-call(bf16[384,384]{1,0:T(8,128)(2,1)S(1)} %collective-permute-done.behind_ref, bf16[2,384,384]{2,1,0:T(8,128)(2,1)S(1)} %get-tuple-element.17.cn_ref, f32[384,384]{1,0:T(8,128)S(1)} %get-tuple-element.18.refs_0_.partial_ref, bf16[384,384]{1,0:T(8,128)(2,1)S(1)} %get-tuple-element.20.ready_ref), custom_call_target="tpu_custom_call" | custom-call | flops 226492416 | bytes 1048576 | tf_op jit(solution)/shard_map/pallas_call | solution.py:109
  11.8 0.3 %collective-permute-start.6 = (bf16[384,384]{1,0:T(8,128)(2,1)S(1)}, bf16[384,384]{1,0:T(8,128)(2,1)S(1)}, u32[]{:S(2)}, u32[]{:S(2)}) collective-permute-start(bf16[384,384]{1,0:T(8,128)(2,1)S(1)} %shard_map.49.first_ref), channel_id=1, source_target_pairs={{28,0},{16,4},{20,8},{24,12},{4,16},{8,20},{12,24},{0,28},{29,1},{... | collective-permute-start | bytes 884744 | tf_op jit(solution)/shard_map/ppermute | solution.py:146
  12.1 0.6 %shard_map.50.after_ref = bf16[384,384]{1,0:T(8,128)(2,1)S(1)} custom-call(bf16[384,384]{1,0:T(8,128)(2,1)S(1)} %collective-permute-done.behind_ref, bf16[2,384,384]{2,1,0:T(8,128)(2,1)S(1)} %get-tuple-element.17.cn_ref, bf16[384,384]{1,0:T(8,128)(2,1)S(1)} %shard_map.49.first_ref, f32[384,384]{1,0:T(8,128)S(1)} %get-tuple-element.19.refs_1_.refs_0_, ...), custom_call_target="tpu_custom_call" | custom-call | flops 226492416 | bytes 1048576 | tf_op jit(solution)/shard_map/pallas_call | solution.py:109
  12.8 1.0 %collective-permute-start.7 = (bf16[384,384]{1,0:T(8,128)(2,1)S(1)}, bf16[384,384]{1,0:T(8,128)(2,1)S(1)}, u32[]{:S(2)}, u32[]{:S(2)}) collective-permute-start(bf16[384,384]{1,0:T(8,128)(2,1)S(1)} %shard_map.50.after_ref), channel_id=1, source_target_pairs={{0,4},{4,0},{8,12},{12,8},{16,20},{20,16},{24,28},{28,24},{1,5},{5... | collective-permute-start | bytes 884744 | tf_op jit(solution)/shard_map/ppermute | solution.py:151
  13.8 0.0 collective-permute-done.2.got_ref.refs_0_
  13.8 0.6 %collective-permute-done.3.refs_0_.refs_1_ = bf16[384,384]{1,0:T(8,128)(2,1)S(1)} collective-permute-done((bf16[384,384]{1,0:T(8,128)(2,1)S(1)}, bf16[384,384]{1,0:T(8,128)(2,1)S(1)}, u32[]{:S(2)}, u32[]{:S(2)}) %collective-permute-start.3) | collective-permute-done | bytes 294944 | tf_op jit(solution)/shard_map/ppermute | solution.py:146
  14.4 0.1 shard_map.52.after_ref
  14.5 2.2 %collective-permute-start.5 = (bf16[384,384]{1,0:T(8,128)(2,1)S(1)}, bf16[384,384]{1,0:T(8,128)(2,1)S(1)}, u32[]{:S(2)}, u32[]{:S(2)}) collective-permute-start(bf16[384,384]{1,0:T(8,128)(2,1)S(1)} %shard_map.52.after_ref), channel_id=1, source_target_pairs={{0,1},{1,2},{2,3},{3,7},{4,0},{5,4},{6,5},{7,6},{8,9},{9,10},{10,1... | collective-permute-start | bytes 884744 | tf_op jit(solution)/shard_map/ppermute | solution.py:156
  16.7 0.0 collective-permute-start.4
  16.7 0.0 collective-permute-done.7
  16.7 0.0 collective-permute-start.8
  16.7 1.3 %shard_map.53.own_ref = f32[384,384]{1,0:T(8,128)S(1)} custom-call(f32[2,8,384]{2,1,0:T(8,128)S(1)} %get-tuple-element.16.factor_ref, bf16[2,384,384]{2,1,0:T(8,128)(2,1)S(1)} %copy-done, bf16[384,384]{1,0:T(8,128)(2,1)S(1)} %shard_map.52.after_ref, bf16[384,384]{1,0:T(8,128)(2,1)S(1)} %collective-permute-done.2.got_ref.refs_0_, ...), custom_call_target="tpu_custom_call" | custom-call | flops 452984832 | bytes 1048576 | tf_op jit(solution)/shard_map/pallas_call | solution.py:109
  18.0 1.0 %collective-permute-done.6.got_ref = bf16[384,384]{1,0:T(8,128)(2,1)S(1)} collective-permute-done((bf16[384,384]{1,0:T(8,128)(2,1)S(1)}, bf16[384,384]{1,0:T(8,128)(2,1)S(1)}, u32[]{:S(2)}, u32[]{:S(2)}) %collective-permute-start.6) | collective-permute-done | bytes 294944 | tf_op jit(solution)/shard_map/ppermute | solution.py:146
  19.1 4.0 %collective-permute-done.5.term_ref = bf16[384,384]{1,0:T(8,128)(2,1)S(1)} collective-permute-done((bf16[384,384]{1,0:T(8,128)(2,1)S(1)}, bf16[384,384]{1,0:T(8,128)(2,1)S(1)}, u32[]{:S(2)}, u32[]{:S(2)}) %collective-permute-start.5) | collective-permute-done | bytes 294944 | tf_op jit(solution)/shard_map/ppermute | solution.py:156
  23.0 0.7 %collective-permute-done.4.term_ref = bf16[384,384]{1,0:T(8,128)(2,1)S(1)} collective-permute-done((bf16[384,384]{1,0:T(8,128)(2,1)S(1)}, bf16[384,384]{1,0:T(8,128)(2,1)S(1)}, u32[]{:S(2)}, u32[]{:S(2)}) %collective-permute-start.4) | collective-permute-done | bytes 294944 | tf_op jit(solution)/shard_map/ppermute | solution.py:156
  23.8 0.0 collective-permute-done.8.refs_0_
  23.8 0.9 %shard_map.56 = bf16[1,1,2,384,384]{4,3,2,1,0:T(8,128)(2,1)} custom-call(f32[2,8,384]{2,1,0:T(8,128)S(1)} %get-tuple-element.16.factor_ref, f32[384,384]{1,0:T(8,128)S(1)} %shard_map.53.own_ref, bf16[384,384]{1,0:T(8,128)(2,1)S(1)} %collective-permute-done.4.term_ref, bf16[384,384]{1,0:T(8,128)(2,1)S(1)} %shard_map.55.imag_ref, ...), custom_call_target="tpu_custom_call" | custom-call | tf_op jit(solution)/shard_map/pallas_call | solution.py:412
  (4 shorter events, 0.1 us)
Async XLA Ops:
  0.0 8.8 %copy-start = (bf16[2,384,384]{2,1,0:T(8,128)(2,1)S(1)}, bf16[2,384,384]{2,1,0:T(8,128)(2,1)}, u32[]{:S(2)}) copy-start(bf16[2,384,384]{2,1,0:T(8,128)(2,1)} %cm_ref.3) | copy-start | bytes 1769476
  1.1 7.7 %copy-start.1 = (s32[1,2,2]{2,1,0:T(2,128)S(1)}, s32[1,2,2]{2,1,0:T(2,128)}, u32[]{:S(2)}) copy-start(s32[1,2,2]{2,1,0:T(2,128)} %weights_ref.1) | copy-start | bytes 52
  1.2 9.4 %collective-permute-start.1 = (bf16[384,384]{1,0:T(8,128)(2,1)S(1)}, bf16[384,384]{1,0:T(8,128)(2,1)S(1)}, u32[]{:S(2)}, u32[]{:S(2)}) collective-permute-start(bf16[384,384]{1,0:T(8,128)(2,1)S(1)} %get-tuple-element.15.real_ref), channel_id=1, source_target_pairs={{0,1},{1,2},{2,3},{3,7},{4,0},{5,4},{6,5},{7,6},{8,9},{9,10},{10,1... | collective-permute-start | bytes 884744 | tf_op jit(solution)/shard_map/ppermute | solution.py:156
  4.2 7.0 %collective-permute-start = (bf16[384,384]{1,0:T(8,128)(2,1)S(1)}, bf16[384,384]{1,0:T(8,128)(2,1)S(1)}, u32[]{:S(2)}, u32[]{:S(2)}) collective-permute-start(bf16[384,384]{1,0:T(8,128)(2,1)S(1)} %get-tuple-element.15.real_ref), channel_id=1, source_target_pairs={{0,4},{1,0},{2,1},{3,2},{4,5},{5,6},{6,7},{7,3},{8,12},{9,8},{10,9... | collective-permute-start | bytes 884744 | tf_op jit(solution)/shard_map/ppermute | solution.py:156
  4.2 9.6 %collective-permute-start.2 = (bf16[384,384]{1,0:T(8,128)(2,1)S(1)}, bf16[384,384]{1,0:T(8,128)(2,1)S(1)}, u32[]{:S(2)}, u32[]{:S(2)}) collective-permute-start(bf16[384,384]{1,0:T(8,128)(2,1)S(1)} %get-tuple-element.22), channel_id=1, source_target_pairs={{28,0},{16,4},{20,8},{24,12},{4,16},{8,20},{12,24},{0,28},{29,1},{... | collective-permute-start | bytes 884744 | tf_op jit(solution)/shard_map/ppermute | solution.py:146
  6.0 8.4 %collective-permute-start.3 = (bf16[384,384]{1,0:T(8,128)(2,1)S(1)}, bf16[384,384]{1,0:T(8,128)(2,1)S(1)}, u32[]{:S(2)}, u32[]{:S(2)}) collective-permute-start(bf16[384,384]{1,0:T(8,128)(2,1)S(1)} %get-tuple-element.22), channel_id=1, source_target_pairs={{12,0},{0,12},{28,16},{16,28},{13,1},{1,13},{29,17},{17,29},{14,2}... | collective-permute-start | bytes 884744 | tf_op jit(solution)/shard_map/ppermute | solution.py:146
  11.8 7.2 %collective-permute-start.6 = (bf16[384,384]{1,0:T(8,128)(2,1)S(1)}, bf16[384,384]{1,0:T(8,128)(2,1)S(1)}, u32[]{:S(2)}, u32[]{:S(2)}) collective-permute-start(bf16[384,384]{1,0:T(8,128)(2,1)S(1)} %shard_map.49.first_ref), channel_id=1, source_target_pairs={{28,0},{16,4},{20,8},{24,12},{4,16},{8,20},{12,24},{0,28},{29,1},{... | collective-permute-start | bytes 884744 | tf_op jit(solution)/shard_map/ppermute | solution.py:146
  12.8 4.0 %collective-permute-start.7 = (bf16[384,384]{1,0:T(8,128)(2,1)S(1)}, bf16[384,384]{1,0:T(8,128)(2,1)S(1)}, u32[]{:S(2)}, u32[]{:S(2)}) collective-permute-start(bf16[384,384]{1,0:T(8,128)(2,1)S(1)} %shard_map.50.after_ref), channel_id=1, source_target_pairs={{0,4},{4,0},{8,12},{12,8},{16,20},{20,16},{24,28},{28,24},{1,5},{5... | collective-permute-start | bytes 884744 | tf_op jit(solution)/shard_map/ppermute | solution.py:151
  14.5 8.6 %collective-permute-start.5 = (bf16[384,384]{1,0:T(8,128)(2,1)S(1)}, bf16[384,384]{1,0:T(8,128)(2,1)S(1)}, u32[]{:S(2)}, u32[]{:S(2)}) collective-permute-start(bf16[384,384]{1,0:T(8,128)(2,1)S(1)} %shard_map.52.after_ref), channel_id=1, source_target_pairs={{0,1},{1,2},{2,3},{3,7},{4,0},{5,4},{6,5},{7,6},{8,9},{9,10},{10,1... | collective-permute-start | bytes 884744 | tf_op jit(solution)/shard_map/ppermute | solution.py:156
  16.7 7.0 %collective-permute-start.4 = (bf16[384,384]{1,0:T(8,128)(2,1)S(1)}, bf16[384,384]{1,0:T(8,128)(2,1)S(1)}, u32[]{:S(2)}, u32[]{:S(2)}) collective-permute-start(bf16[384,384]{1,0:T(8,128)(2,1)S(1)} %shard_map.52.after_ref), channel_id=1, source_target_pairs={{0,4},{1,0},{2,1},{3,2},{4,5},{5,6},{6,7},{7,3},{8,12},{9,8},{10,9... | collective-permute-start | bytes 884744 | tf_op jit(solution)/shard_map/ppermute | solution.py:156
  16.7 7.0 %collective-permute-start.8 = (bf16[384,384]{1,0:T(8,128)(2,1)S(1)}, bf16[384,384]{1,0:T(8,128)(2,1)S(1)}, u32[]{:S(2)}, u32[]{:S(2)}) collective-permute-start(bf16[384,384]{1,0:T(8,128)(2,1)S(1)} %collective-permute-done.7), channel_id=1, source_target_pairs={{8,0},{4,12},{24,16},{20,28},{0,4},{12,8},{16,20},{28,24},{9,1},{5... | collective-permute-start | bytes 884744 | tf_op jit(solution)/shard_map/ppermute | solution.py:153

commit v7 on v5

--- a/solution.py
+++ b/solution.py
@@ -124,23 +124,17 @@
     rounds = len(plan)
     route = routes(plan, count)
 
-    def split(green_ref, real_ref, imag_ref, sems):
-        copies = [
-            pltpu.make_async_copy(green_ref.at[0, 0, part], out, sems.at[part])
-            for part, out in enumerate((real_ref, imag_ref))
-        ]
-        for copy in copies:
-            copy.start()
-        for copy in copies:
-            copy.wait()
-
-    real, imag = pl.pallas_call(
-        split,
-        out_shape=[block, block],
-        in_specs=[ANY],
-        out_specs=[VM, VM],
-        scratch_shapes=[pltpu.SemaphoreType.DMA((2,))],
-    )(green)
+    def split(green_ref, real_ref, sem):
+        copy = pltpu.make_async_copy(green_ref.at[0, 0, 0], real_ref, sem)
+        copy.start()
+        copy.wait()
+
+    (real,) = call(split, [ANY], [block], 1, size, pltpu.with_memory_space_constraint(green, pltpu.HBM), scratch=[pltpu.SemaphoreType.DMA])
+
+    def second_part(green_ref, after_ref, imag_ref):
+        imag_ref[...] = green_ref[0, 0, 1]
+
+    (imag,) = call(second_part, [VM, ANY], [block], 1, size, green, real)
 
     def along(x, step):
         return lax.ppermute(x, "energy", [(s, t) for t, (s, _, _) in step.items()])
@@ -341,37 +335,50 @@
             def _():
                 out_ref[...] = own_ref[...].astype(BF16)
 
-            if k:
-
-                @pl.when(is_kind(0))
-                def _():
-                    out_ref[...] = source_ref[...]
-
-        return call(kernel, [VM, VM, VM if k else ANY], [block], SHORT, size, own, term_next[k], source)[0]
-
-    imag_sum = imag_part(1, imag_part(0, real_sum))
-
-    def finish(factor_ref, imag_ref, real_ref, *refs):
-        got, out_ref, held_ref, sems = refs[: rounds - 1], refs[-3], refs[-2], refs[-1]
-        imag_copy = pltpu.make_async_copy(imag_ref, out_ref.at[0, 0, 1], sems.at[1])
-        imag_copy.start()
+        return call(kernel, [VM, VM, ANY], [block], SHORT, size, own, term_next[k], source)[0]
+
+    imag_sum = imag_part(0, real_sum)
+
+    def finish(factor_ref, own_ref, term_ref, imag_ref, real_ref, *refs):
+        got, out_ref, held_ref, made_ref, sems = refs[: rounds - 1], refs[-4], refs[-3], refs[-2], refs[-1]
+        last = lax.axis_index("slab") == slabs - 1
+
+        def imag_copy(ref):
+            return pltpu.make_async_copy(ref, out_ref.at[0, 0, 1], sems.at[1])
+
+        @pl.when(is_kind(0))
+        def _():
+            imag_copy(imag_ref).start()
+
+        @pl.when(is_kind(1) & jnp.logical_not(last))
+        def _():
+            made_ref[...] = (own_ref[...] + term_ref[...].astype(F32)).astype(BF16)
+
+        @pl.when(is_kind(1) & last)
+        def _():
+            made_ref[...] = own_ref[...].astype(BF16)
+
+        @pl.when(is_kind(1))
+        def _():
+            imag_copy(made_ref).start()
+
         total = real_ref[...]
         for r, ref in enumerate(got, 1):
             total += scaled(ref, factor_ref, r)
         held_ref[...] = total.astype(BF16)
         real_copy = pltpu.make_async_copy(held_ref, out_ref.at[0, 0, 0], sems.at[0])
         real_copy.start()
-        imag_copy.wait()
+        imag_copy(made_ref).wait()
         real_copy.wait()
 
     return pl.pallas_call(
         finish,
         out_shape=jax.ShapeDtypeStruct(green.shape, BF16),
-        in_specs=[VM] * (2 + rounds),
+        in_specs=[VM] * (4 + rounds),
         out_specs=ANY,
-        scratch_shapes=[block, pltpu.SemaphoreType.DMA((2,))],
+        scratch_shapes=[block, block, pltpu.SemaphoreType.DMA((2,))],
         compiler_params=pltpu.CompilerParams(vmem_limit_bytes=24 << 20),
-    )(factors, imag_sum, real_sum, *arrived[1:])
+    )(factors, own, term_next[1], imag_sum, real_sum, *arrived[1:])
 
 
 def solution(mesh):

time: 24.7 us -> 24.7 us (level)
    pallas_call x1 -> x0, Pallas kernels: 1.13 us -> none  [body(): pl.pallas_call(split, out_shape=[block, block], in_specs=[ANY], out_specs...]
    pallas_call x10 -> x11, Pallas kernels: 4.39 us -> 5.39 us  [call(): pl.pallas_call(kernel, out_shape=outs, in_specs=ins, out_specs=[VM] * len...]
where the time goes in v7:
time: 24.7 us; the launch traced here: 24.5 us
  starting transfers between devices  11.4 us (46%)
  waiting for transfers between devices  6.72 us (27%)
  Pallas kernels  6.28 us (25%)
    pallas_call x11, Pallas kernels, call(): pl.pallas_call(kernel, out_shape=outs, in_specs=ins, out_specs=[VM] * len...  5.39 us
    ppermute x4, starting transfers between devices, from_next(): lax.ppermute(x, ('energy', 'slab'), descent(count, slabs, kind))  5.36 us
    ppermute x4, waiting for transfers between devices, from_next(): lax.ppermute(x, ('energy', 'slab'), descent(count, slabs, kind))  5.18 us
    ppermute x3, starting transfers between devices, along(): return lax.ppermute(x, 'energy', [(s, t) for t, (s, _, _) in step.items()])  5 us
    ppermute x3, waiting for transfers between devices, along(): return lax.ppermute(x, 'energy', [(s, t) for t, (s, _, _) in step.items()])  1.53 us
    ppermute x1, starting transfers between devices, along_closed(): swapped = lax.ppermute(x, 'energy', [(e, e ^ 1) for e in range(count)])  1.02 us
    pallas_call x1, Pallas kernels, body(): pl.pallas_call(finish, out_shape=jax.ShapeDtypeStruct(green.shape, BF16),...  0.88 us
  transfers between devices with their start and end apart: 9, of which 5 were waited for; matrix products, arithmetic and copies ran while one was open for 0% of the time, Pallas kernels for 18%

profile of v7, /device:TPU:0, one launch (start us, length us, event | category | flops | bytes accessed | tf_op | source)
XLA Modules:
  0.0 24.5 jit_solution(15318262544362008455)
XLA Ops:
  0.0 0.0 copy-start
  0.0 1.0 %shard_map.46.real_ref.after_ref = bf16[384,384]{1,0:T(8,128)(2,1)S(1)} custom-call(bf16[1,1,2,384,384]{4,3,2,1,0:T(8,128)(2,1)} %green_ref.3), custom_call_target="tpu_custom_call" | custom-call | flops 113246208 | bytes 1048576 | tf_op jit(solution)/shard_map/pallas_call | solution.py:109
  1.1 0.0 copy-start.1
  1.1 0.0 copy-start.2
  1.1 3.0 %collective-permute-start.1 = (bf16[384,384]{1,0:T(8,128)(2,1)S(1)}, bf16[384,384]{1,0:T(8,128)(2,1)S(1)}, u32[]{:S(2)}, u32[]{:S(2)}) collective-permute-start(bf16[384,384]{1,0:T(8,128)(2,1)S(1)} %shard_map.46.real_ref.after_ref), channel_id=1, source_target_pairs={{0,1},{1,2},{2,3},{3,7},{4,0},{5,4},{6,5},{7,6},{8,9},{9,10},{10,1... | collective-permute-start | bytes 884744 | tf_op jit(solution)/shard_map/ppermute | solution.py:150
  4.1 0.0 collective-permute-start
  4.1 0.0 copy-done
  4.2 1.8 %collective-permute-start.2 = (bf16[384,384]{1,0:T(8,128)(2,1)S(1)}, bf16[384,384]{1,0:T(8,128)(2,1)S(1)}, u32[]{:S(2)}, u32[]{:S(2)}) collective-permute-start(bf16[384,384]{1,0:T(8,128)(2,1)S(1)} %shard_map.51), channel_id=1, source_target_pairs={{28,0},{16,4},{20,8},{24,12},{4,16},{8,20},{12,24},{0,28},{29,1},{... | collective-permute-start | bytes 884744 | tf_op jit(solution)/shard_map/ppermute | solution.py:140
  6.0 2.9 %collective-permute-start.3 = (bf16[384,384]{1,0:T(8,128)(2,1)S(1)}, bf16[384,384]{1,0:T(8,128)(2,1)S(1)}, u32[]{:S(2)}, u32[]{:S(2)}) collective-permute-start(bf16[384,384]{1,0:T(8,128)(2,1)S(1)} %shard_map.51), channel_id=1, source_target_pairs={{12,0},{0,12},{28,16},{16,28},{13,1},{1,13},{29,17},{17,29},{14,2}... | collective-permute-start | bytes 884744 | tf_op jit(solution)/shard_map/ppermute | solution.py:140
  8.9 0.0 copy-done.1
  8.9 0.0 copy-done.2
  8.9 1.7 %shard_map.47 = (f32[2,8,384]{2,1,0:T(8,128)S(1)}, bf16[2,384,384]{2,1,0:T(8,128)(2,1)S(1)}, f32[384,384]{1,0:T(8,128)S(1)}, f32[384,384]{1,0:T(8,128)S(1)}) custom-call(s32[1,2,2]{2,1,0:T(2,128)S(1)} %copy-done.2, bf16[384,384]{1,0:T(8,128)(2,1)S(1)} %shard_map.46.real_ref.after_ref, bf16[2,384,384]{2,1,0:T(8,128)(2,1)S(1)} %copy-done.1, ...), custom_call_target="tpu_custom_call" | custom-call | flops 452984832 | bytes 1048576 | tf_op jit(solution)/shard_map/pallas_call | solution.py:109
  10.5 0.0 collective-permute-done.1.behind_ref
  10.6 0.6 %collective-permute-done.behind_ref = bf16[384,384]{1,0:T(8,128)(2,1)S(1)} collective-permute-done((bf16[384,384]{1,0:T(8,128)(2,1)S(1)}, bf16[384,384]{1,0:T(8,128)(2,1)S(1)}, u32[]{:S(2)}, u32[]{:S(2)}) %collective-permute-start) | collective-permute-done | bytes 294944 | tf_op jit(solution)/shard_map/ppermute | solution.py:150
  11.1 0.6 %shard_map.49.first_ref = bf16[384,384]{1,0:T(8,128)(2,1)S(1)} custom-call(bf16[384,384]{1,0:T(8,128)(2,1)S(1)} %collective-permute-done.behind_ref, bf16[2,384,384]{2,1,0:T(8,128)(2,1)S(1)} %get-tuple-element.12.cn_ref, f32[384,384]{1,0:T(8,128)S(1)} %get-tuple-element.13.refs_0_.partial_ref, bf16[384,384]{1,0:T(8,128)(2,1)S(1)} %get-tuple-element.15.ready_ref), custom_call_target="tpu_custom_call" | custom-call | flops 226492416 | bytes 1048576 | tf_op jit(solution)/shard_map/pallas_call | solution.py:109
  11.7 0.3 %collective-permute-start.6 = (bf16[384,384]{1,0:T(8,128)(2,1)S(1)}, bf16[384,384]{1,0:T(8,128)(2,1)S(1)}, u32[]{:S(2)}, u32[]{:S(2)}) collective-permute-start(bf16[384,384]{1,0:T(8,128)(2,1)S(1)} %shard_map.49.first_ref), channel_id=1, source_target_pairs={{28,0},{16,4},{20,8},{24,12},{4,16},{8,20},{12,24},{0,28},{29,1},{... | collective-permute-start | bytes 884744 | tf_op jit(solution)/shard_map/ppermute | solution.py:140
  12.1 0.6 %shard_map.50.after_ref = bf16[384,384]{1,0:T(8,128)(2,1)S(1)} custom-call(bf16[384,384]{1,0:T(8,128)(2,1)S(1)} %collective-permute-done.behind_ref, bf16[2,384,384]{2,1,0:T(8,128)(2,1)S(1)} %get-tuple-element.12.cn_ref, bf16[384,384]{1,0:T(8,128)(2,1)S(1)} %shard_map.49.first_ref, f32[384,384]{1,0:T(8,128)S(1)} %get-tuple-element.14.refs_1_.refs_0_, ...), custom_call_target="tpu_custom_call" | custom-call | flops 226492416 | bytes 1048576 | tf_op jit(solution)/shard_map/pallas_call | solution.py:109
  12.7 1.0 %collective-permute-start.7 = (bf16[384,384]{1,0:T(8,128)(2,1)S(1)}, bf16[384,384]{1,0:T(8,128)(2,1)S(1)}, u32[]{:S(2)}, u32[]{:S(2)}) collective-permute-start(bf16[384,384]{1,0:T(8,128)(2,1)S(1)} %shard_map.50.after_ref), channel_id=1, source_target_pairs={{0,4},{4,0},{8,12},{12,8},{16,20},{20,16},{24,28},{28,24},{1,5},{5... | collective-permute-start | bytes 884744 | tf_op jit(solution)/shard_map/ppermute | solution.py:145
  13.7 0.0 collective-permute-done.2.got_ref.refs_0_
  13.8 0.7 %collective-permute-done.3.refs_0_.refs_1_ = bf16[384,384]{1,0:T(8,128)(2,1)S(1)} collective-permute-done((bf16[384,384]{1,0:T(8,128)(2,1)S(1)}, bf16[384,384]{1,0:T(8,128)(2,1)S(1)}, u32[]{:S(2)}, u32[]{:S(2)}) %collective-permute-start.3) | collective-permute-done | bytes 294944 | tf_op jit(solution)/shard_map/ppermute | solution.py:140
  14.4 0.1 shard_map.53.after_ref
  14.5 2.3 %collective-permute-start.5 = (bf16[384,384]{1,0:T(8,128)(2,1)S(1)}, bf16[384,384]{1,0:T(8,128)(2,1)S(1)}, u32[]{:S(2)}, u32[]{:S(2)}) collective-permute-start(bf16[384,384]{1,0:T(8,128)(2,1)S(1)} %shard_map.53.after_ref), channel_id=1, source_target_pairs={{0,1},{1,2},{2,3},{3,7},{4,0},{5,4},{6,5},{7,6},{8,9},{9,10},{10,1... | collective-permute-start | bytes 884744 | tf_op jit(solution)/shard_map/ppermute | solution.py:150
  16.8 0.0 collective-permute-start.4
  16.8 0.0 collective-permute-done.7
  16.8 0.0 collective-permute-start.8
  16.8 1.3 %shard_map.54.own_ref = f32[384,384]{1,0:T(8,128)S(1)} custom-call(f32[2,8,384]{2,1,0:T(8,128)S(1)} %get-tuple-element.11.factor_ref, bf16[2,384,384]{2,1,0:T(8,128)(2,1)S(1)} %copy-done.1, bf16[384,384]{1,0:T(8,128)(2,1)S(1)} %shard_map.53.after_ref, bf16[384,384]{1,0:T(8,128)(2,1)S(1)} %collective-permute-done.2.got_ref.refs_0_, ...), custom_call_target="tpu_custom_call" | custom-call | flops 452984832 | bytes 1048576 | tf_op jit(solution)/shard_map/pallas_call | solution.py:109
  18.1 0.9 %collective-permute-done.6.got_ref = bf16[384,384]{1,0:T(8,128)(2,1)S(1)} collective-permute-done((bf16[384,384]{1,0:T(8,128)(2,1)S(1)}, bf16[384,384]{1,0:T(8,128)(2,1)S(1)}, u32[]{:S(2)}, u32[]{:S(2)}) %collective-permute-start.6) | collective-permute-done | bytes 294944 | tf_op jit(solution)/shard_map/ppermute | solution.py:140
  19.0 3.9 %collective-permute-done.5.term_ref = bf16[384,384]{1,0:T(8,128)(2,1)S(1)} collective-permute-done((bf16[384,384]{1,0:T(8,128)(2,1)S(1)}, bf16[384,384]{1,0:T(8,128)(2,1)S(1)}, u32[]{:S(2)}, u32[]{:S(2)}) %collective-permute-start.5) | collective-permute-done | bytes 294944 | tf_op jit(solution)/shard_map/ppermute | solution.py:150
  22.9 0.7 %collective-permute-done.4.term_ref = bf16[384,384]{1,0:T(8,128)(2,1)S(1)} collective-permute-done((bf16[384,384]{1,0:T(8,128)(2,1)S(1)}, bf16[384,384]{1,0:T(8,128)(2,1)S(1)}, u32[]{:S(2)}, u32[]{:S(2)}) %collective-permute-start.4) | collective-permute-done | bytes 294944 | tf_op jit(solution)/shard_map/ppermute | solution.py:150
  23.6 0.0 collective-permute-done.8.refs_0_
  23.6 0.9 %shard_map.57 = bf16[1,1,2,384,384]{4,3,2,1,0:T(8,128)(2,1)} custom-call(f32[2,8,384]{2,1,0:T(8,128)S(1)} %get-tuple-element.11.factor_ref, f32[384,384]{1,0:T(8,128)S(1)} %shard_map.54.own_ref, bf16[384,384]{1,0:T(8,128)(2,1)S(1)} %collective-permute-done.4.term_ref, bf16[384,384]{1,0:T(8,128)(2,1)S(1)} %shard_map.56.imag_ref, ...), custom_call_target="tpu_custom_call" | custom-call | tf_op jit(solution)/shard_map/pallas_call | solution.py:374
  (5 shorter events, 0.1 us)
Async XLA Ops:
  0.0 4.1 %copy-start = (bf16[1,1,2,384,384]{4,3,2,1,0:T(8,128)(2,1)S(1)}, bf16[1,1,2,384,384]{4,3,2,1,0:T(8,128)(2,1)}, u32[]{:S(2)}) copy-start(bf16[1,1,2,384,384]{4,3,2,1,0:T(8,128)(2,1)} %green_ref.3) | copy-start | bytes 1769476
  1.1 7.8 %copy-start.1 = (bf16[2,384,384]{2,1,0:T(8,128)(2,1)S(1)}, bf16[2,384,384]{2,1,0:T(8,128)(2,1)}, u32[]{:S(2)}) copy-start(bf16[2,384,384]{2,1,0:T(8,128)(2,1)} %cm_ref.3) | copy-start | bytes 1769476
  1.1 7.8 %copy-start.2 = (s32[1,2,2]{2,1,0:T(2,128)S(1)}, s32[1,2,2]{2,1,0:T(2,128)}, u32[]{:S(2)}) copy-start(s32[1,2,2]{2,1,0:T(2,128)} %weights_ref.1) | copy-start | bytes 52
  1.1 9.5 %collective-permute-start.1 = (bf16[384,384]{1,0:T(8,128)(2,1)S(1)}, bf16[384,384]{1,0:T(8,128)(2,1)S(1)}, u32[]{:S(2)}, u32[]{:S(2)}) collective-permute-start(bf16[384,384]{1,0:T(8,128)(2,1)S(1)} %shard_map.46.real_ref.after_ref), channel_id=1, source_target_pairs={{0,1},{1,2},{2,3},{3,7},{4,0},{5,4},{6,5},{7,6},{8,9},{9,10},{10,1... | collective-permute-start | bytes 884744 | tf_op jit(solution)/shard_map/ppermute | solution.py:150
  4.1 7.0 %collective-permute-start = (bf16[384,384]{1,0:T(8,128)(2,1)S(1)}, bf16[384,384]{1,0:T(8,128)(2,1)S(1)}, u32[]{:S(2)}, u32[]{:S(2)}) collective-permute-start(bf16[384,384]{1,0:T(8,128)(2,1)S(1)} %shard_map.46.real_ref.after_ref), channel_id=1, source_target_pairs={{0,4},{1,0},{2,1},{3,2},{4,5},{5,6},{6,7},{7,3},{8,12},{9,8},{10,9... | collective-permute-start | bytes 884744 | tf_op jit(solution)/shard_map/ppermute | solution.py:150
  4.2 9.6 %collective-permute-start.2 = (bf16[384,384]{1,0:T(8,128)(2,1)S(1)}, bf16[384,384]{1,0:T(8,128)(2,1)S(1)}, u32[]{:S(2)}, u32[]{:S(2)}) collective-permute-start(bf16[384,384]{1,0:T(8,128)(2,1)S(1)} %shard_map.51), channel_id=1, source_target_pairs={{28,0},{16,4},{20,8},{24,12},{4,16},{8,20},{12,24},{0,28},{29,1},{... | collective-permute-start | bytes 884744 | tf_op jit(solution)/shard_map/ppermute | solution.py:140
  6.0 8.4 %collective-permute-start.3 = (bf16[384,384]{1,0:T(8,128)(2,1)S(1)}, bf16[384,384]{1,0:T(8,128)(2,1)S(1)}, u32[]{:S(2)}, u32[]{:S(2)}) collective-permute-start(bf16[384,384]{1,0:T(8,128)(2,1)S(1)} %shard_map.51), channel_id=1, source_target_pairs={{12,0},{0,12},{28,16},{16,28},{13,1},{1,13},{29,17},{17,29},{14,2}... | collective-permute-start | bytes 884744 | tf_op jit(solution)/shard_map/ppermute | solution.py:140
  11.7 7.2 %collective-permute-start.6 = (bf16[384,384]{1,0:T(8,128)(2,1)S(1)}, bf16[384,384]{1,0:T(8,128)(2,1)S(1)}, u32[]{:S(2)}, u32[]{:S(2)}) collective-permute-start(bf16[384,384]{1,0:T(8,128)(2,1)S(1)} %shard_map.49.first_ref), channel_id=1, source_target_pairs={{28,0},{16,4},{20,8},{24,12},{4,16},{8,20},{12,24},{0,28},{29,1},{... | collective-permute-start | bytes 884744 | tf_op jit(solution)/shard_map/ppermute | solution.py:140
  12.7 4.1 %collective-permute-start.7 = (bf16[384,384]{1,0:T(8,128)(2,1)S(1)}, bf16[384,384]{1,0:T(8,128)(2,1)S(1)}, u32[]{:S(2)}, u32[]{:S(2)}) collective-permute-start(bf16[384,384]{1,0:T(8,128)(2,1)S(1)} %shard_map.50.after_ref), channel_id=1, source_target_pairs={{0,4},{4,0},{8,12},{12,8},{16,20},{20,16},{24,28},{28,24},{1,5},{5... | collective-permute-start | bytes 884744 | tf_op jit(solution)/shard_map/ppermute | solution.py:145
  14.5 8.4 %collective-permute-start.5 = (bf16[384,384]{1,0:T(8,128)(2,1)S(1)}, bf16[384,384]{1,0:T(8,128)(2,1)S(1)}, u32[]{:S(2)}, u32[]{:S(2)}) collective-permute-start(bf16[384,384]{1,0:T(8,128)(2,1)S(1)} %shard_map.53.after_ref), channel_id=1, source_target_pairs={{0,1},{1,2},{2,3},{3,7},{4,0},{5,4},{6,5},{7,6},{8,9},{9,10},{10,1... | collective-permute-start | bytes 884744 | tf_op jit(solution)/shard_map/ppermute | solution.py:150
  16.8 6.8 %collective-permute-start.4 = (bf16[384,384]{1,0:T(8,128)(2,1)S(1)}, bf16[384,384]{1,0:T(8,128)(2,1)S(1)}, u32[]{:S(2)}, u32[]{:S(2)}) collective-permute-start(bf16[384,384]{1,0:T(8,128)(2,1)S(1)} %shard_map.53.after_ref), channel_id=1, source_target_pairs={{0,4},{1,0},{2,1},{3,2},{4,5},{5,6},{6,7},{7,3},{8,12},{9,8},{10,9... | collective-permute-start | bytes 884744 | tf_op jit(solution)/shard_map/ppermute | solution.py:150
  16.8 6.8 %collective-permute-start.8 = (bf16[384,384]{1,0:T(8,128)(2,1)S(1)}, bf16[384,384]{1,0:T(8,128)(2,1)S(1)}, u32[]{:S(2)}, u32[]{:S(2)}) collective-permute-start(bf16[384,384]{1,0:T(8,128)(2,1)S(1)} %collective-permute-done.7), channel_id=1, source_target_pairs={{8,0},{4,12},{24,16},{20,28},{0,4},{12,8},{16,20},{28,24},{9,1},{5... | collective-permute-start | bytes 884744 | tf_op jit(solution)/shard_map/ppermute | solution.py:147

commit v8 on v5

--- a/solution.py
+++ b/solution.py
@@ -269,44 +269,47 @@
         )
         arrived += [along_closed(results[r], plan[r]) for r in range(1, rounds)]
 
-    def term_first(factor_ref, cn_ref, got_ref, after_ref, out_ref):
-        mode, _, present = arriving(route[0])
+    def term_sum(factor_ref, cn_ref, after_ref, *refs):
+        got, out_ref, total_ref, left_ref = refs[:rounds], refs[-3], refs[-2], refs[-1]
         ahead = lax.axis_index("slab") > 0
-
-        @pl.when(present & ahead)
-        def _():
-            out_ref[...] = couple(cn_ref[mode], scaled(got_ref, factor_ref, 0).astype(BF16))
-
-        @pl.when(jnp.logical_not(present & ahead))
-        def _():
-            out_ref[...] = jnp.zeros_like(out_ref)
-
-    (begun,) = call(term_first, [VM, VM, VM, ANY], [wide], 2, size, factors, coupling_n, near[0], results[-1])
-
-    def term_rest(factor_ref, cn_ref, after_ref, begun_ref, *refs):
-        got, out_ref, total_ref = refs[:-2], refs[-2], refs[-1]
-        total_ref[...] = begun_ref[...]
-        for r, ref in enumerate(got, 1):
-            mode, _, present = arriving(route[r])
-
-            @pl.when(present & (lax.axis_index("slab") > 0))
-            def _():
-                total_ref[...] += couple(cn_ref[mode], scaled(ref, factor_ref, r).astype(BF16))
+        modes, present = zip(*[(mode, there) for mode, _, there in map(arriving, route)])
+
+        def left(r):
+            return dot(cn_ref[modes[r]], scaled(got[r], factor_ref, r).astype(BF16)).astype(BF16)
+
+        both = ahead & present[0] & present[1] if rounds > 1 else False
+        if rounds > 1:
+            @pl.when(both)
+            def _():
+                for r in range(2):
+                    left_ref[:, r * size : (r + 1) * size] = left(r)
+                mats = jnp.concatenate([cn_ref[modes[0]], cn_ref[modes[1]]], 1)
+                total_ref[...] = dot_t(left_ref[...], mats)
+
+        @pl.when(jnp.logical_not(both))
+        def _():
+            total_ref[...] = jnp.zeros_like(total_ref)
+
+        for r in range(rounds):
+            alone = ahead & present[r]
+
+            @pl.when(alone & jnp.logical_not(both) if r < 2 else alone)
+            def _():
+                total_ref[...] += dot_t(left(r), cn_ref[modes[r]])
 
         out_ref[...] = total_ref[...].astype(BF16)
 
     (term,) = call(
-        term_rest,
-        [VM, VM, ANY, VM] + [VM] * (rounds - 1),
+        term_sum,
+        [VM, VM, ANY] + [VM] * rounds,
         [block],
         LONG,
         size,
         factors,
         coupling_n,
         results[-1],
-        begun,
-        *near[1:],
-        scratch=[wide],
+        *near,
+        scratch=[wide, pltpu.VMEM((size, 2 * size), BF16)],
     )
     term_next = from_next(term)
 

time: 24.7 us -> 24.7 us (level)
    pallas_call x10 -> x9, Pallas kernels: 4.39 us -> 4.36 us  [call(): pl.pallas_call(kernel, out_shape=outs, in_specs=ins, out_specs=[VM] * len...]
where the time goes in v8:
time: 24.7 us; the launch traced here: 24.5 us
  starting transfers between devices  11.4 us (46%)
  waiting for transfers between devices  6.66 us (27%)
  Pallas kernels  6.32 us (26%)
    ppermute x4, starting transfers between devices, from_next(): lax.ppermute(x, ('energy', 'slab'), descent(count, slabs, kind))  5.44 us
    ppermute x4, waiting for transfers between devices, from_next(): lax.ppermute(x, ('energy', 'slab'), descent(count, slabs, kind))  5.18 us
    ppermute x3, starting transfers between devices, along(): return lax.ppermute(x, 'energy', [(s, t) for t, (s, _, _) in step.items()])  4.92 us
    pallas_call x9, Pallas kernels, call(): pl.pallas_call(kernel, out_shape=outs, in_specs=ins, out_specs=[VM] * len...  4.36 us
    ppermute x3, waiting for transfers between devices, along(): return lax.ppermute(x, 'energy', [(s, t) for t, (s, _, _) in step.items()])  1.48 us
    pallas_call x1, Pallas kernels, body(): pl.pallas_call(split, out_shape=[block, block], in_specs=[ANY], out_specs...  1.13 us
    ppermute x1, starting transfers between devices, along_closed(): swapped = lax.ppermute(x, 'energy', [(e, e ^ 1) for e in range(count)])  1.04 us
    pallas_call x1, Pallas kernels, body(): pl.pallas_call(finish, out_shape=jax.ShapeDtypeStruct(green.shape, BF16),...  0.83 us
  transfers between devices with their start and end apart: 9, of which 5 were waited for; matrix products, arithmetic and copies ran while one was open for 0% of the time, Pallas kernels for 18%

profile of v8, /device:TPU:0, one launch (start us, length us, event | category | flops | bytes accessed | tf_op | source)
XLA Modules:
  0.0 24.5 jit_solution(13102913204422692845)
XLA Ops:
  0.0 0.0 copy-start
  0.0 1.1 %shard_map.46 = (bf16[384,384]{1,0:T(8,128)(2,1)S(1)}, bf16[384,384]{1,0:T(8,128)(2,1)S(1)}) custom-call(bf16[1,1,2,384,384]{4,3,2,1,0:T(8,128)(2,1)} %green_ref.1), custom_call_target="tpu_custom_call" | custom-call | tf_op jit(solution)/shard_map/pallas_call | solution.py:137
  1.1 0.0 copy-start.1
  1.2 3.0 %collective-permute-start.1 = (bf16[384,384]{1,0:T(8,128)(2,1)S(1)}, bf16[384,384]{1,0:T(8,128)(2,1)S(1)}, u32[]{:S(2)}, u32[]{:S(2)}) collective-permute-start(bf16[384,384]{1,0:T(8,128)(2,1)S(1)} %get-tuple-element.13.real_ref), channel_id=1, source_target_pairs={{0,1},{1,2},{2,3},{3,7},{4,0},{5,4},{6,5},{7,6},{8,9},{9,10},{10,1... | collective-permute-start | bytes 884744 | tf_op jit(solution)/shard_map/ppermute | solution.py:156
  4.2 0.0 collective-permute-start
  4.2 1.8 %collective-permute-start.2 = (bf16[384,384]{1,0:T(8,128)(2,1)S(1)}, bf16[384,384]{1,0:T(8,128)(2,1)S(1)}, u32[]{:S(2)}, u32[]{:S(2)}) collective-permute-start(bf16[384,384]{1,0:T(8,128)(2,1)S(1)} %get-tuple-element.20), channel_id=1, source_target_pairs={{28,0},{16,4},{20,8},{24,12},{4,16},{8,20},{12,24},{0,28},{29,1},{... | collective-permute-start | bytes 884744 | tf_op jit(solution)/shard_map/ppermute | solution.py:146
  6.0 2.9 %collective-permute-start.3 = (bf16[384,384]{1,0:T(8,128)(2,1)S(1)}, bf16[384,384]{1,0:T(8,128)(2,1)S(1)}, u32[]{:S(2)}, u32[]{:S(2)}) collective-permute-start(bf16[384,384]{1,0:T(8,128)(2,1)S(1)} %get-tuple-element.20), channel_id=1, source_target_pairs={{12,0},{0,12},{28,16},{16,28},{13,1},{1,13},{29,17},{17,29},{14,2}... | collective-permute-start | bytes 884744 | tf_op jit(solution)/shard_map/ppermute | solution.py:146
  8.8 0.0 copy-done
  8.8 0.0 copy-done.1
  8.9 1.7 %shard_map.47 = (f32[2,8,384]{2,1,0:T(8,128)S(1)}, bf16[2,384,384]{2,1,0:T(8,128)(2,1)S(1)}, f32[384,384]{1,0:T(8,128)S(1)}, f32[384,384]{1,0:T(8,128)S(1)}) custom-call(s32[1,2,2]{2,1,0:T(2,128)S(1)} %copy-done.1, bf16[384,384]{1,0:T(8,128)(2,1)S(1)} %get-tuple-element.13.real_ref, bf16[2,384,384]{2,1,0:T(8,128)(2,1)S(1)} %copy-done, ...), custom_call_target="tpu_custom_call" | custom-call | flops 452984832 | bytes 1048576 | tf_op jit(solution)/shard_map/pallas_call | solution.py:109
  10.5 0.0 collective-permute-done.1.behind_ref
  10.6 0.6 %collective-permute-done.behind_ref = bf16[384,384]{1,0:T(8,128)(2,1)S(1)} collective-permute-done((bf16[384,384]{1,0:T(8,128)(2,1)S(1)}, bf16[384,384]{1,0:T(8,128)(2,1)S(1)}, u32[]{:S(2)}, u32[]{:S(2)}) %collective-permute-start) | collective-permute-done | bytes 294944 | tf_op jit(solution)/shard_map/ppermute | solution.py:156
  11.2 0.6 %shard_map.49.first_ref = bf16[384,384]{1,0:T(8,128)(2,1)S(1)} custom-call(bf16[384,384]{1,0:T(8,128)(2,1)S(1)} %collective-permute-done.behind_ref, bf16[2,384,384]{2,1,0:T(8,128)(2,1)S(1)} %get-tuple-element.15.cn_ref, f32[384,384]{1,0:T(8,128)S(1)} %get-tuple-element.16.refs_0_.partial_ref, bf16[384,384]{1,0:T(8,128)(2,1)S(1)} %get-tuple-element.18.ready_ref), custom_call_target="tpu_custom_call" | custom-call | flops 226492416 | bytes 1048576 | tf_op jit(solution)/shard_map/pallas_call | solution.py:109
  11.8 0.3 %collective-permute-start.6 = (bf16[384,384]{1,0:T(8,128)(2,1)S(1)}, bf16[384,384]{1,0:T(8,128)(2,1)S(1)}, u32[]{:S(2)}, u32[]{:S(2)}) collective-permute-start(bf16[384,384]{1,0:T(8,128)(2,1)S(1)} %shard_map.49.first_ref), channel_id=1, source_target_pairs={{28,0},{16,4},{20,8},{24,12},{4,16},{8,20},{12,24},{0,28},{29,1},{... | collective-permute-start | bytes 884744 | tf_op jit(solution)/shard_map/ppermute | solution.py:146
  12.1 0.6 %shard_map.50.after_ref = bf16[384,384]{1,0:T(8,128)(2,1)S(1)} custom-call(bf16[384,384]{1,0:T(8,128)(2,1)S(1)} %collective-permute-done.behind_ref, bf16[2,384,384]{2,1,0:T(8,128)(2,1)S(1)} %get-tuple-element.15.cn_ref, bf16[384,384]{1,0:T(8,128)(2,1)S(1)} %shard_map.49.first_ref, f32[384,384]{1,0:T(8,128)S(1)} %get-tuple-element.17.refs_1_.refs_0_, ...), custom_call_target="tpu_custom_call" | custom-call | flops 226492416 | bytes 1048576 | tf_op jit(solution)/shard_map/pallas_call | solution.py:109
  12.7 1.0 %collective-permute-start.7 = (bf16[384,384]{1,0:T(8,128)(2,1)S(1)}, bf16[384,384]{1,0:T(8,128)(2,1)S(1)}, u32[]{:S(2)}, u32[]{:S(2)}) collective-permute-start(bf16[384,384]{1,0:T(8,128)(2,1)S(1)} %shard_map.50.after_ref), channel_id=1, source_target_pairs={{0,4},{4,0},{8,12},{12,8},{16,20},{20,16},{24,28},{28,24},{1,5},{5... | collective-permute-start | bytes 884744 | tf_op jit(solution)/shard_map/ppermute | solution.py:151
  13.8 0.0 collective-permute-done.2.refs_0_
  13.8 0.6 %collective-permute-done.3.refs_1_ = bf16[384,384]{1,0:T(8,128)(2,1)S(1)} collective-permute-done((bf16[384,384]{1,0:T(8,128)(2,1)S(1)}, bf16[384,384]{1,0:T(8,128)(2,1)S(1)}, u32[]{:S(2)}, u32[]{:S(2)}) %collective-permute-start.3) | collective-permute-done | bytes 294944 | tf_op jit(solution)/shard_map/ppermute | solution.py:146
  14.4 0.1 shard_map.51.after_ref
  14.5 2.4 %collective-permute-start.5 = (bf16[384,384]{1,0:T(8,128)(2,1)S(1)}, bf16[384,384]{1,0:T(8,128)(2,1)S(1)}, u32[]{:S(2)}, u32[]{:S(2)}) collective-permute-start(bf16[384,384]{1,0:T(8,128)(2,1)S(1)} %shard_map.51.after_ref), channel_id=1, source_target_pairs={{0,1},{1,2},{2,3},{3,7},{4,0},{5,4},{6,5},{7,6},{8,9},{9,10},{10,1... | collective-permute-start | bytes 884744 | tf_op jit(solution)/shard_map/ppermute | solution.py:156
  16.9 0.0 collective-permute-start.4
  16.9 0.0 collective-permute-done.7
  16.9 0.0 collective-permute-start.8
  16.9 1.3 %shard_map.52.own_ref = f32[384,384]{1,0:T(8,128)S(1)} custom-call(f32[2,8,384]{2,1,0:T(8,128)S(1)} %get-tuple-element.14.factor_ref, bf16[2,384,384]{2,1,0:T(8,128)(2,1)S(1)} %copy-done, bf16[384,384]{1,0:T(8,128)(2,1)S(1)} %shard_map.51.after_ref, bf16[384,384]{1,0:T(8,128)(2,1)S(1)} %collective-permute-done.2.refs_0_, ...), custom_call_target="tpu_custom_call" | custom-call | flops 452984832 | bytes 1048576 | tf_op jit(solution)/shard_map/pallas_call | solution.py:109
  18.2 0.9 %collective-permute-done.6.got_ref = bf16[384,384]{1,0:T(8,128)(2,1)S(1)} collective-permute-done((bf16[384,384]{1,0:T(8,128)(2,1)S(1)}, bf16[384,384]{1,0:T(8,128)(2,1)S(1)}, u32[]{:S(2)}, u32[]{:S(2)}) %collective-permute-start.6) | collective-permute-done | bytes 294944 | tf_op jit(solution)/shard_map/ppermute | solution.py:146
  19.1 3.8 %collective-permute-done.5.term_ref = bf16[384,384]{1,0:T(8,128)(2,1)S(1)} collective-permute-done((bf16[384,384]{1,0:T(8,128)(2,1)S(1)}, bf16[384,384]{1,0:T(8,128)(2,1)S(1)}, u32[]{:S(2)}, u32[]{:S(2)}) %collective-permute-start.5) | collective-permute-done | bytes 294944 | tf_op jit(solution)/shard_map/ppermute | solution.py:156
  22.9 0.7 %collective-permute-done.4.term_ref = bf16[384,384]{1,0:T(8,128)(2,1)S(1)} collective-permute-done((bf16[384,384]{1,0:T(8,128)(2,1)S(1)}, bf16[384,384]{1,0:T(8,128)(2,1)S(1)}, u32[]{:S(2)}, u32[]{:S(2)}) %collective-permute-start.4) | collective-permute-done | bytes 294944 | tf_op jit(solution)/shard_map/ppermute | solution.py:156
  23.6 0.1 shard_map.55.imag_ref
  23.7 0.0 collective-permute-done.8.refs_0_
  23.7 0.8 %shard_map.56 = bf16[1,1,2,384,384]{4,3,2,1,0:T(8,128)(2,1)} custom-call(f32[2,8,384]{2,1,0:T(8,128)S(1)} %get-tuple-element.14.factor_ref, bf16[384,384]{1,0:T(8,128)(2,1)S(1)} %shard_map.55.imag_ref, f32[384,384]{1,0:T(8,128)S(1)} %shard_map.53.source_ref.real_ref, bf16[384,384]{1,0:T(8,128)(2,1)S(1)} %collective-permute-done.8.refs_0_), custom_call_target="tpu_custom_call" | custom-call | tf_op jit(solution)/shard_map/pallas_call | solution.py:370
  (3 shorter events, 0.1 us)
Async XLA Ops:
  0.0 8.8 %copy-start = (bf16[2,384,384]{2,1,0:T(8,128)(2,1)S(1)}, bf16[2,384,384]{2,1,0:T(8,128)(2,1)}, u32[]{:S(2)}) copy-start(bf16[2,384,384]{2,1,0:T(8,128)(2,1)} %cm_ref.3) | copy-start | bytes 1769476
  1.1 7.7 %copy-start.1 = (s32[1,2,2]{2,1,0:T(2,128)S(1)}, s32[1,2,2]{2,1,0:T(2,128)}, u32[]{:S(2)}) copy-start(s32[1,2,2]{2,1,0:T(2,128)} %weights_ref.1) | copy-start | bytes 52
  1.2 9.4 %collective-permute-start.1 = (bf16[384,384]{1,0:T(8,128)(2,1)S(1)}, bf16[384,384]{1,0:T(8,128)(2,1)S(1)}, u32[]{:S(2)}, u32[]{:S(2)}) collective-permute-start(bf16[384,384]{1,0:T(8,128)(2,1)S(1)} %get-tuple-element.13.real_ref), channel_id=1, source_target_pairs={{0,1},{1,2},{2,3},{3,7},{4,0},{5,4},{6,5},{7,6},{8,9},{9,10},{10,1... | collective-permute-start | bytes 884744 | tf_op jit(solution)/shard_map/ppermute | solution.py:156
  4.2 7.0 %collective-permute-start = (bf16[384,384]{1,0:T(8,128)(2,1)S(1)}, bf16[384,384]{1,0:T(8,128)(2,1)S(1)}, u32[]{:S(2)}, u32[]{:S(2)}) collective-permute-start(bf16[384,384]{1,0:T(8,128)(2,1)S(1)} %get-tuple-element.13.real_ref), channel_id=1, source_target_pairs={{0,4},{1,0},{2,1},{3,2},{4,5},{5,6},{6,7},{7,3},{8,12},{9,8},{10,9... | collective-permute-start | bytes 884744 | tf_op jit(solution)/shard_map/ppermute | solution.py:156
  4.2 9.6 %collective-permute-start.2 = (bf16[384,384]{1,0:T(8,128)(2,1)S(1)}, bf16[384,384]{1,0:T(8,128)(2,1)S(1)}, u32[]{:S(2)}, u32[]{:S(2)}) collective-permute-start(bf16[384,384]{1,0:T(8,128)(2,1)S(1)} %get-tuple-element.20), channel_id=1, source_target_pairs={{28,0},{16,4},{20,8},{24,12},{4,16},{8,20},{12,24},{0,28},{29,1},{... | collective-permute-start | bytes 884744 | tf_op jit(solution)/shard_map/ppermute | solution.py:146
  6.0 8.4 %collective-permute-start.3 = (bf16[384,384]{1,0:T(8,128)(2,1)S(1)}, bf16[384,384]{1,0:T(8,128)(2,1)S(1)}, u32[]{:S(2)}, u32[]{:S(2)}) collective-permute-start(bf16[384,384]{1,0:T(8,128)(2,1)S(1)} %get-tuple-element.20), channel_id=1, source_target_pairs={{12,0},{0,12},{28,16},{16,28},{13,1},{1,13},{29,17},{17,29},{14,2}... | collective-permute-start | bytes 884744 | tf_op jit(solution)/shard_map/ppermute | solution.py:146
  11.8 7.2 %collective-permute-start.6 = (bf16[384,384]{1,0:T(8,128)(2,1)S(1)}, bf16[384,384]{1,0:T(8,128)(2,1)S(1)}, u32[]{:S(2)}, u32[]{:S(2)}) collective-permute-start(bf16[384,384]{1,0:T(8,128)(2,1)S(1)} %shard_map.49.first_ref), channel_id=1, source_target_pairs={{28,0},{16,4},{20,8},{24,12},{4,16},{8,20},{12,24},{0,28},{29,1},{... | collective-permute-start | bytes 884744 | tf_op jit(solution)/shard_map/ppermute | solution.py:146
  12.7 4.1 %collective-permute-start.7 = (bf16[384,384]{1,0:T(8,128)(2,1)S(1)}, bf16[384,384]{1,0:T(8,128)(2,1)S(1)}, u32[]{:S(2)}, u32[]{:S(2)}) collective-permute-start(bf16[384,384]{1,0:T(8,128)(2,1)S(1)} %shard_map.50.after_ref), channel_id=1, source_target_pairs={{0,4},{4,0},{8,12},{12,8},{16,20},{20,16},{24,28},{28,24},{1,5},{5... | collective-permute-start | bytes 884744 | tf_op jit(solution)/shard_map/ppermute | solution.py:151
  14.5 8.4 %collective-permute-start.5 = (bf16[384,384]{1,0:T(8,128)(2,1)S(1)}, bf16[384,384]{1,0:T(8,128)(2,1)S(1)}, u32[]{:S(2)}, u32[]{:S(2)}) collective-permute-start(bf16[384,384]{1,0:T(8,128)(2,1)S(1)} %shard_map.51.after_ref), channel_id=1, source_target_pairs={{0,1},{1,2},{2,3},{3,7},{4,0},{5,4},{6,5},{7,6},{8,9},{9,10},{10,1... | collective-permute-start | bytes 884744 | tf_op jit(solution)/shard_map/ppermute | solution.py:156
  16.9 6.7 %collective-permute-start.4 = (bf16[384,384]{1,0:T(8,128)(2,1)S(1)}, bf16[384,384]{1,0:T(8,128)(2,1)S(1)}, u32[]{:S(2)}, u32[]{:S(2)}) collective-permute-start(bf16[384,384]{1,0:T(8,128)(2,1)S(1)} %shard_map.51.after_ref), channel_id=1, source_target_pairs={{0,4},{1,0},{2,1},{3,2},{4,5},{5,6},{6,7},{7,3},{8,12},{9,8},{10,9... | collective-permute-start | bytes 884744 | tf_op jit(solution)/shard_map/ppermute | solution.py:156
  16.9 6.8 %collective-permute-start.8 = (bf16[384,384]{1,0:T(8,128)(2,1)S(1)}, bf16[384,384]{1,0:T(8,128)(2,1)S(1)}, u32[]{:S(2)}, u32[]{:S(2)}) collective-permute-start(bf16[384,384]{1,0:T(8,128)(2,1)S(1)} %collective-permute-done.7), channel_id=1, source_target_pairs={{8,0},{4,12},{24,16},{20,28},{0,4},{12,8},{16,20},{28,24},{9,1},{5... | collective-permute-start | bytes 884744 | tf_op jit(solution)/shard_map/ppermute | solution.py:153
